TPU v7x, 128 devices: a whole 4x4x4 slice. The times are simulated.
128 devices in a mesh: sec: 2 (over z_lo), dev: 64 (over z_hi, x, y, core).
Axes of the slice: x: 4, y: 4, z: 4 (z_hi: 2, z_lo: 2; z = z_hi * 2 + z_lo), core: 2. Of those that a mesh axis runs over, the one named last changes fastest.
Arguments:
- hidden: bfloat16 [1024, 7168], P(('sec', 'dev')), may hold values from -40 to 40
- norm_gain: float32 [7168], replicated, may hold values from 0.1 to 1.9
- routes: int32 [1024, 8], P(('sec', 'dev')), may hold values from 0 to 31, as said below
- gate_values: float32 [1024, 8], P(('sec', 'dev')), may hold values from 0.1 to 0.6
- w_gate: bfloat16 [7168, 65536], P(None, ('sec', 'dev')), may hold values from -0.0625 to 0.0625
- w_up: bfloat16 [7168, 65536], P(None, ('sec', 'dev')), may hold values from -0.0625 to 0.0625
- w_down: bfloat16 [65536, 7168], P(('sec', 'dev')), may hold values from -0.125 to 0.125
- queries: bfloat16 [128, 128, 576], P(('sec', 'dev')), may hold values from -80 to 80
- latent_cache: bfloat16 [128, 1536, 576], P(('sec', 'dev')), may hold values from -6 to 6
- lengths: int32 [128], P(('sec', 'dev')), may hold values from 2 to 1536, as said below
Outputs:
- moe_out: bfloat16 [1024, 7168], P(('sec', 'dev'))
- attn_out: bfloat16 [128, 128, 512], P(('sec', 'dev'))
Inputs may be any that keep to these rules, and one draw needn't show every extreme that they name: `routes`: each row names 8 different experts. Among the 8 rows of one device no expert is named more than 4 times, and one expert, the same for every device, is named exactly 4 times by the rows of each device. `lengths`: every row keeps its first two positions; some rows use all 1536.
All inputs are finite; a program needn't handle non-finite values.
Results may differ from a plain program's by a relative error of at most 0.013.
Values may be sent and summed in bfloat16 or wider, within the bound.
No kernel may reach another device: no remote copies, remote signals or barrier semaphores. Data moves between devices by JAX's collectives and lax.ppermute only.
A program may use at most 128 MiB of HBM per device.

v0:
```python
import jax
import jax.numpy as jnp
from jax import lax
from jax.sharding import PartitionSpec as P

LAT = 512
EXPERTS = 32
CAP = 4


norm_eps = 1e-06
score_scale = 0.07216878364870322


def expert_block(expert_input, w_gate, w_up, w_down):
    model_width = expert_input.shape[-1]
    flat_rows = expert_input.reshape(-1, model_width)
    gate_part = jnp.dot(flat_rows, w_gate, preferred_element_type=jnp.float32)
    up_part = jnp.dot(flat_rows, w_up, preferred_element_type=jnp.float32)
    hidden_act = (jax.nn.silu(gate_part) * up_part).astype(jnp.bfloat16)
    partial_out = jnp.dot(hidden_act, w_down, preferred_element_type=jnp.float32).astype(
        jnp.bfloat16
    )
    return partial_out.reshape(expert_input.shape)


def attend(queries, latent_cache, lengths):
    scores = (
        jnp.einsum("rhk,rck->rhc", queries, latent_cache, preferred_element_type=jnp.float32)
        * score_scale
    )
    in_range = jnp.arange(latent_cache.shape[1])[None, None, :] < lengths[:, None, None]
    scores = jnp.where(in_range, scores, -jnp.inf)
    row_max = jnp.max(scores, axis=-1, keepdims=True)
    raised = jnp.exp(scores - row_max)
    probs = (raised / jnp.sum(raised, axis=-1, keepdims=True)).astype(jnp.bfloat16)
    attended = jnp.einsum(
        "rhc,rcl->rhl", probs, latent_cache[:, :, :LAT], preferred_element_type=jnp.float32
    )
    return attended.astype(jnp.bfloat16)


def shards(
    hidden, norm_gain, routes, gate_values, w_gate, w_up, w_down, queries, latent_cache, lengths
):
    group_size = lax.axis_size("sec") * lax.axis_size("dev") // EXPERTS
    tok_rows = hidden.shape[0]
    model_width = hidden.shape[1]
    features = hidden.astype(jnp.float32)
    squares = jnp.mean(features * features, axis=-1, keepdims=True)
    normed = (features * lax.rsqrt(squares + norm_eps) * norm_gain).astype(jnp.bfloat16)
    flat_ids = routes.reshape(-1)
    onehot = (flat_ids[:, None] == jnp.arange(EXPERTS, dtype=jnp.int32)[None, :]).astype(jnp.int32)
    earlier = jnp.cumsum(onehot, axis=0) - onehot
    rank_of = jnp.sum(earlier * onehot, axis=1)
    slot_ids = (flat_ids * CAP + rank_of).reshape(tok_rows, -1)
    matches = slot_ids[None, :, :] == jnp.arange(EXPERTS * CAP, dtype=jnp.int32)[:, None, None]
    picked = jnp.any(matches, axis=2).astype(jnp.bfloat16)
    weighed = jnp.sum(jnp.where(matches, gate_values[None, :, :], 0.0), axis=2)
    packed = jnp.dot(picked, normed, preferred_element_type=jnp.float32).astype(jnp.bfloat16)
    copies = jnp.broadcast_to(
        packed.reshape(EXPERTS, 1, CAP, model_width), (EXPERTS, group_size, CAP, model_width)
    )
    copies = copies.reshape(EXPERTS * group_size, CAP, model_width)
    partial_rows = expert_block(
        lax.all_to_all(copies, ("sec", "dev"), split_axis=0, concat_axis=0, tiled=True),
        w_gate,
        w_up,
        w_down,
    )
    attn_out = attend(queries, latent_cache, lengths)
    returned = lax.all_to_all(partial_rows, ("sec", "dev"), split_axis=0, concat_axis=0, tiled=True)
    summed = jnp.sum(
        returned.reshape(EXPERTS, group_size, CAP, model_width), axis=1, dtype=jnp.float32
    )
    summed = summed.reshape(EXPERTS * CAP, model_width)
    moe_rows = jnp.einsum(
        "st,sd->td",
        weighed,
        summed,
        precision=lax.Precision.HIGHEST,
        preferred_element_type=jnp.float32,
    )
    return (moe_rows.astype(jnp.bfloat16), attn_out)


def solution(mesh):
    placed = (
        P(("sec", "dev"), None),
        P(),
        P(("sec", "dev"), None),
        P(("sec", "dev"), None),
        P(None, ("sec", "dev")),
        P(None, ("sec", "dev")),
        P(("sec", "dev"), None),
        P(("sec", "dev"), None, None),
        P(("sec", "dev"), None, None),
        P(("sec", "dev")),
    )
    return jax.shard_map(
        shards,
        mesh=mesh,
        in_specs=placed,
        out_specs=(P(("sec", "dev"), None), P(("sec", "dev"), None, None)),
        check_vma=False,
    )
```

profile of v0, /device:TPU:42, one launch (start us, length us, event | category | flops | bytes accessed | tf_op | source)
XLA Modules:
  0.0 293.8 jit_solution(15355648313586833141)
XLA Ops:
  0.6 0.0 copy-start
  0.6 0.8 eq.28
  1.4 0.1 fusion.29
  1.5 0.1 reduce_window_sum.11
  1.6 0.2 select_reduce_fusion.1
  1.8 0.1 reduce_sum.48
  1.9 0.7 multiply_add_fusion
  2.6 0.1 fusion.28
  2.7 1.1 fusion.21
  3.8 1.6 convolution_convert_fusion.1
  5.4 1.7 broadcast_in_dim.42
  7.1 6.7 %broadcast_in_dim.43 = bf16[32,4,4,7168]{3,2,1,0:T(4,128)(2,1)} broadcast(bf16[32,4,7168]{2,1,0:T(4,128)(2,1)} %broadcast_in_dim.42), dimensions={0,2,3} | broadcast | bytes 9175040 | tf_op jit(solution)/shard_map/broadcast_in_dim | solution.py:61
  13.8 98.3 %all_to_all.10 = bf16[128,4,7168]{2,1,0:T(4,128)(2,1)} all-to-all(bf16[128,4,7168]{2,1,0:T(4,128)(2,1)} %bitcast.33), channel_id=1, replica_groups=mesh['sec'=2,'dev'=64] {'sec','dev'}, dimensions={0} | all-to-all | bytes 14680064 | tf_op jit(solution)/shard_map/all_to_all | solution.py:66
  112.1 12.1 %reshape.80 = bf16[512,7168]{1,0:T(8,128)(2,1)} reshape(bf16[128,4,7168]{2,1,0:T(4,128)(2,1)} %all_to_all.10) | data formatting | bytes 14680064 | tf_op jit(solution)/shard_map/reshape | solution.py:17
  124.2 8.4 %fusion.32 = f32[512,512]{1,0:T(8,128)S(1)} fusion(bf16[512,7168]{1,0:T(8,128)(2,1)} %reshape.80, bf16[7168,512]{1,0:T(8,128)(2,1)} %param.14), kind=kOutput, calls=%fused_computation.44 | convolution fusion | flops 3758096384 | bytes 15728640 | tf_op jit(solution)/shard_map/dot_general | solution.py:18
  132.7 16.3 %convolution_convert_fusion = bf16[512,7168]{1,0:T(8,128)(2,1)} fusion(bf16[512,7168]{1,0:T(8,128)(2,1)} %param.16, bf16[512,7168]{1,0:T(8,128)(2,1)} %reshape.80, bf16[7168,512]{1,0:T(8,128)(2,1)} %param.15, f32[512,512]{1,0:T(8,128)S(1)} %fusion.32), kind=kOutput, calls=%fused_computation.1 | convolution fusion | flops 7521435648 | bytes 30408704 | tf_op jit(solution)/shard_map/dot_general | solution.py:21
  149.0 12.7 %reshape.81 = bf16[128,4,7168]{2,1,0:T(4,128)(2,1)} reshape(bf16[512,7168]{1,0:T(8,128)(2,1)} %convolution_convert_fusion) | data formatting | bytes 14680064 | tf_op jit(solution)/shard_map/reshape | solution.py:24
  161.7 0.0 copy-start.2
  161.7 0.0 copy-start.1
  161.7 12.1 %all-to-all-start.1 = ((bf16[128,4,7168]{2,1,0:T(4,128)(2,1)}), bf16[128,4,7168]{2,1,0:T(4,128)(2,1)}, u32[]{:S(2)}, u32[]{:S(2)}) async-start(bf16[128,4,7168]{2,1,0:T(4,128)(2,1)} %reshape.81), calls=%async_computation.1 | async-start | bytes 14680064 | tf_op jit(solution)/shard_map/all_to_all | solution.py:72
  174.4 0.0 copy-done.2
  174.5 0.1 select_reduce_fusion
  174.6 0.0 copy-done
  174.6 0.0 copy-done.1
  174.6 0.6 fusion.31
  175.2 0.3 fusion.17
  175.4 1.3 fusion.9
  176.8 97.7 %all-to-all-done.1 = bf16[128,4,7168]{2,1,0:T(4,128)(2,1)} async-done(((bf16[128,4,7168]{2,1,0:T(4,128)(2,1)}), bf16[128,4,7168]{2,1,0:T(4,128)(2,1)}, u32[]{:S(2)}, u32[]{:S(2)}) %all-to-all-start.1) | async-done | bytes 7340064 | tf_op jit(solution)/shard_map/all_to_all | solution.py:72
  274.4 9.6 %convert_reduce_fusion = f32[32,4,7168]{2,1,0:T(4,128)} fusion(bf16[128,4,7168]{2,1,0:T(4,128)(2,1)} %all-to-all-done.1), kind=kLoop, calls=%fused_computation | loop fusion | flops 6422528 | bytes 11010048 | tf_op jit(solution)/shard_map/reduce_sum | solution.py:73
  284.0 5.3 %reshape.82 = f32[128,7168]{1,0:T(8,128)} reshape(f32[32,4,7168]{2,1,0:T(4,128)} %convert_reduce_fusion) | data formatting | bytes 7340032 | tf_op jit(solution)/shard_map/reshape | solution.py:76
  289.3 4.5 %convolution_convert_fusion.2 = bf16[8,7168]{1,0:T(8,128)(2,1)} fusion(f32[128,8]{0,1:T(8,128)S(1)} %select_reduce_fusion, f32[128,7168]{1,0:T(8,128)} %reshape.82), kind=kOutput, calls=%fused_computation.3 | convolution fusion | flops 88137728 | bytes 3788800 | tf_op jit(solution)/shard_map/st,sd->td/dot_general | solution.py:77
  (2 shorter events, 0.0 us)
Async XLA Ops:
  0.6 173.9 %copy-start = (bf16[1,128,576]{1,2,0:T(8,128)(2,1)S(1)}, bf16[1,128,576]{1,2,0:T(8,128)(2,1)}, u32[]{:S(2)}) copy-start(bf16[1,128,576]{1,2,0:T(8,128)(2,1)} %param.17) | copy-start | bytes 442372
  161.7 12.8 %copy-start.2 = (f32[8,8]{1,0:T(8,128)S(1)}, f32[8,8]{1,0:T(8,128)}, u32[]{:S(2)}) copy-start(f32[8,8]{1,0:T(8,128)} %param.13) | copy-start | bytes 772
  161.7 12.9 %copy-start.1 = (bf16[1,1536,576]{1,2,0:T(8,128)(2,1)S(1)}, bf16[1,1536,576]{1,2,0:T(8,128)(2,1)}, u32[]{:S(2)}) copy-start(bf16[1,1536,576]{1,2,0:T(8,128)(2,1)} %param.18) | copy-start | bytes 5308420
  161.7 112.8 %all-to-all-start.1 = ((bf16[128,4,7168]{2,1,0:T(4,128)(2,1)}), bf16[128,4,7168]{2,1,0:T(4,128)(2,1)}, u32[]{:S(2)}, u32[]{:S(2)}) async-start(bf16[128,4,7168]{2,1,0:T(4,128)(2,1)} %reshape.81), calls=%async_computation.1 | async-start | bytes 14680064 | tf_op jit(solution)/shard_map/all_to_all | solution.py:72
where the time goes:
time: 295 us; the launch traced here: 294 us
  blocking collectives  98.3 us (33%)
  waiting for transfers between devices  97.7 us (33%)
  local copies, waits for them, and re-layouts  39.3 us (13%)
  matrix products  32.8 us (11%)
  other arithmetic  12.2 us (4%)
  starting transfers between devices  12.1 us (4%)
    all_to_all x1, blocking collectives, shards(): lax.all_to_all(copies, ('sec', 'dev'), split_axis=0, concat_axis=0, tiled...  98.3 us
    all_to_all x1, waiting for transfers between devices, shards(): lax.all_to_all(partial_rows, ('sec', 'dev'), split_axis=0, concat_axis=0,...  97.7 us
    dot_general x1, matrix products, expert_block(): jnp.dot(hidden_act, w_down, preferred_element_type=jnp.float32)  16.3 us
    reshape x1, local copies, waits for them, and re-layouts, expert_block(): return partial_out.reshape(expert_input.shape)  12.7 us
    all_to_all x1, starting transfers between devices, shards(): lax.all_to_all(partial_rows, ('sec', 'dev'), split_axis=0, concat_axis=0,...  12.1 us
    reshape x1, local copies, waits for them, and re-layouts, expert_block(): flat_rows = expert_input.reshape(-1, model_width)  12.1 us
    reduce_sum x1, other arithmetic, shards(): jnp.sum(returned.reshape(EXPERTS, group_size, CAP, model_width), axis=1,...  9.58 us
    dot_general x1, matrix products, expert_block(): gate_part = jnp.dot(flat_rows, w_gate, preferred_element_type=jnp.float32)  8.44 us
  transfers between devices with their start and end apart: 1, of which 1 were waited for; matrix products, arithmetic and copies ran while one was open for 1% of the time, Pallas kernels for 0%

commit v1 on v0

v1 whole, which is shorter than its diff:
```python
import jax
import jax.numpy as jnp
from jax import lax
from jax.experimental import pallas as pl
from jax.experimental.pallas import tpu as pltpu
from jax.sharding import Mesh, PartitionSpec as P

LAT = 512
EXPERTS = 32
CAP = 4

AXES = ("zl", "zh", "x", "y", "core")
SIZES = (2, 2, 4, 4, 2)
CHIPS = ("zl", "zh", "x", "y")
N_CHIPS = 64
QUARTERS = 4
BLOCK = CAP * QUARTERS
ROWS = N_CHIPS * BLOCK
STEP = 256

norm_eps = 1e-06
score_scale = 0.07216878364870322


def slot_matches(routes, lanes):
    rows = routes.shape[0]
    packed_row = lax.broadcasted_iota(jnp.int32, (rows, lanes), 1)
    expert = packed_row // (2 * BLOCK)
    slot = packed_row % CAP
    piece = (packed_row // CAP) % QUARTERS
    named = jnp.zeros((rows, lanes), jnp.bool_)
    for k in range(routes.shape[1]):
        named = named | (routes[:, k : k + 1] == expert)
    before = (
        lax.broadcasted_iota(jnp.int32, (rows, rows), 0)
        > lax.broadcasted_iota(jnp.int32, (rows, rows), 1)
    ).astype(jnp.float32)
    rank = jnp.dot(before, named.astype(jnp.float32), preferred_element_type=jnp.float32)
    return expert, piece, named & (rank == slot.astype(jnp.float32))


def pack_kernel(hidden_ref, gain_ref, routes_ref, send_ref):
    features = hidden_ref[...].astype(jnp.float32)
    squares = jnp.mean(features * features, axis=-1, keepdims=True)
    normed = features * lax.rsqrt(squares + norm_eps) * gain_ref[...]
    width = send_ref.shape[1]
    stacked = jnp.concatenate(
        [normed[:, q * width : (q + 1) * width] for q in range(QUARTERS)], axis=0
    ).astype(jnp.bfloat16)
    _, piece, match = slot_matches(routes_ref[...], send_ref.shape[0])
    picked = jnp.concatenate(
        [(match & (piece == q)).astype(jnp.float32) for q in range(QUARTERS)], axis=0
    ).astype(jnp.bfloat16)
    for start in range(0, send_ref.shape[0], STEP):
        send_ref[start : start + STEP, :] = lax.dot_general(
            picked[:, start : start + STEP],
            stacked,
            (((0,), (0,)), ((), ())),
            preferred_element_type=jnp.float32,
        ).astype(jnp.bfloat16)


def pack(hidden, norm_gain, routes):
    width = hidden.shape[1] // QUARTERS
    return pl.pallas_call(
        pack_kernel,
        out_shape=jax.ShapeDtypeStruct((ROWS, width), jnp.bfloat16),
        compiler_params=pltpu.CompilerParams(vmem_limit_bytes=24 * 2**20),
        name="pack_rows",
    )(hidden, norm_gain.reshape(1, -1), routes)


def ungroup_matrix():
    to = lax.broadcasted_iota(jnp.int32, (STEP, STEP), 0)
    frm = lax.broadcasted_iota(jnp.int32, (STEP, STEP), 1)
    per_piece = STEP // QUARTERS
    want = ((to % per_piece) // CAP) * BLOCK + (to // per_piece) * CAP + to % CAP
    return (frm == want).astype(jnp.float32).astype(jnp.bfloat16)


def gate_up_kernel(rows_ref, gate_ref, up_ref, act_ref, gate_acc, up_acc, order):
    step = pl.program_id(0)

    @pl.when(step == 0)
    def _():
        gate_acc[...] = jnp.zeros_like(gate_acc)
        up_acc[...] = jnp.zeros_like(up_acc)
        order[...] = ungroup_matrix()

    per_piece = STEP // QUARTERS
    parts = []
    for start in range(0, ROWS, STEP):
        moved = jnp.dot(
            order[...], rows_ref[start : start + STEP, :], preferred_element_type=jnp.float32
        ).astype(jnp.bfloat16)
        parts.append(
            jnp.concatenate(
                [moved[q * per_piece : (q + 1) * per_piece] for q in range(QUARTERS)], axis=1
            )
        )
    rows = jnp.concatenate(parts, axis=0)
    depth = rows.shape[1]
    units = gate_acc.shape[1]
    gate_acc[...] += jnp.dot(
        rows, gate_ref[...].reshape(depth, units), preferred_element_type=jnp.float32
    )
    up_acc[...] += jnp.dot(
        rows, up_ref[...].reshape(depth, units), preferred_element_type=jnp.float32
    )

    @pl.when(step == pl.num_programs(0) - 1)
    def _():
        gate = gate_acc[...]
        act_ref[...] = (gate / (1.0 + jnp.exp(-gate)) * up_acc[...]).astype(jnp.bfloat16)


def gate_up(packed, w_gate, w_up):
    width = packed.shape[1]
    units = w_gate.shape[1]
    weight_spec = pl.BlockSpec((QUARTERS, STEP, units), lambda j: (0, j, 0))
    flops = 2 * 2 * (ROWS // QUARTERS) * w_gate.size
    return pl.pallas_call(
        gate_up_kernel,
        grid=(width // STEP,),
        in_specs=[pl.BlockSpec((ROWS, STEP), lambda j: (0, j)), weight_spec, weight_spec],
        out_specs=pl.BlockSpec((ROWS // QUARTERS, units), lambda j: (0, 0)),
        out_shape=jax.ShapeDtypeStruct((ROWS // QUARTERS, units), jnp.bfloat16),
        scratch_shapes=[
            pltpu.VMEM((ROWS // QUARTERS, units), jnp.float32),
            pltpu.VMEM((ROWS // QUARTERS, units), jnp.float32),
            pltpu.VMEM((STEP, STEP), jnp.bfloat16),
        ],
        compiler_params=pltpu.CompilerParams(vmem_limit_bytes=24 * 2**20),
        cost_estimate=pl.CostEstimate(
            flops=flops, bytes_accessed=2 * (2 * w_gate.size + packed.size), transcendentals=0
        ),
        name="gate_up",
    )(
        packed,
        w_gate.reshape(QUARTERS, width, units),
        w_up.reshape(QUARTERS, width, units),
    )


def down_kernel(act_ref, *refs):
    weights = refs[:QUARTERS]
    other = refs[QUARTERS] if len(refs) == QUARTERS + 3 else None
    out_ref, order = refs[-2:]

    @pl.when(pl.program_id(0) == 0)
    def _():
        order[...] = ungroup_matrix()

    per_piece = STEP // QUARTERS
    parts = [
        jnp.dot(act_ref[...], w[...], preferred_element_type=jnp.float32).astype(jnp.bfloat16)
        for w in weights
    ]
    for index in range(ROWS // STEP):
        grouped = jnp.concatenate(
            [part[index * per_piece : (index + 1) * per_piece] for part in parts], axis=0
        )
        moved = lax.dot_general(
            order[...], grouped, (((0,), (0,)), ((), ())), preferred_element_type=jnp.float32
        )
        here = slice(index * STEP, (index + 1) * STEP)
        if other is not None:
            moved = moved + other[here, :].astype(jnp.float32)
        out_ref[here, :] = moved.astype(jnp.bfloat16)


def down(act, w_down, other=None):
    units, model_width = w_down.shape
    width = model_width // QUARTERS
    steps = width // STEP
    packed_spec = pl.BlockSpec((ROWS, STEP), lambda j: (0, j))
    weight_specs = [
        pl.BlockSpec((units, STEP), lambda j, q=q: (0, q * steps + j)) for q in range(QUARTERS)
    ]
    extra = [] if other is None else [other]
    return pl.pallas_call(
        down_kernel,
        grid=(steps,),
        in_specs=[pl.BlockSpec(act.shape, lambda j: (0, 0))]
        + weight_specs
        + [packed_spec] * len(extra),
        out_specs=packed_spec,
        out_shape=jax.ShapeDtypeStruct((ROWS, width), jnp.bfloat16),
        scratch_shapes=[pltpu.VMEM((STEP, STEP), jnp.bfloat16)],
        compiler_params=pltpu.CompilerParams(vmem_limit_bytes=24 * 2**20),
        cost_estimate=pl.CostEstimate(
            flops=2 * act.shape[0] * w_down.size,
            bytes_accessed=2 * (w_down.size + (1 + len(extra)) * ROWS * width),
            transcendentals=0,
        ),
        name="down",
    )(act, *([w_down] * QUARTERS), *extra)


def combine_kernel(rows_ref, routes_ref, gates_ref, out_ref, weigh):
    step = pl.program_id(0)
    tok_rows = routes_ref.shape[0]

    @pl.when(step == 0)
    def _():
        routes = routes_ref[...]
        gates = gates_ref[...]
        expert, piece, match = slot_matches(routes, rows_ref.shape[0])
        gate = jnp.zeros(expert.shape, jnp.float32)
        for k in range(routes.shape[1]):
            gate = gate + jnp.where(routes[:, k : k + 1] == expert, gates[:, k : k + 1], 0.0)
        spread = jnp.concatenate(
            [jnp.where(match & (piece == q), gate, 0.0) for q in range(QUARTERS)], axis=0
        )
        high = spread.astype(jnp.bfloat16)
        low = spread - high.astype(jnp.float32)
        weigh[...] = jnp.concatenate([high.astype(jnp.float32), low], axis=0).astype(jnp.bfloat16)

    half = QUARTERS * tok_rows
    width = out_ref.shape[1] // QUARTERS
    both = jnp.dot(weigh[...], rows_ref[...], preferred_element_type=jnp.float32)
    total = (both[:half] + both[half:]).astype(jnp.bfloat16)
    for q in range(QUARTERS):
        columns = pl.ds(pl.multiple_of(q * width + step * STEP, STEP), STEP)
        out_ref[:, columns] = total[q * tok_rows : (q + 1) * tok_rows]


def combine(returned, routes, gate_values):
    width = returned.shape[1]
    tok_rows = routes.shape[0]
    return pl.pallas_call(
        combine_kernel,
        grid=(width // STEP,),
        in_specs=[
            pl.BlockSpec((ROWS, STEP), lambda j: (0, j)),
            pl.BlockSpec(routes.shape, lambda j: (0, 0)),
            pl.BlockSpec(gate_values.shape, lambda j: (0, 0)),
        ],
        out_specs=pl.BlockSpec((tok_rows, width * QUARTERS), lambda j: (0, 0)),
        out_shape=jax.ShapeDtypeStruct((tok_rows, width * QUARTERS), jnp.bfloat16),
        scratch_shapes=[pltpu.VMEM((2 * QUARTERS * tok_rows, ROWS), jnp.bfloat16)],
        compiler_params=pltpu.CompilerParams(vmem_limit_bytes=24 * 2**20),
        name="combine",
    )(returned, routes, gate_values)


def attend(queries, latent_cache, lengths):
    scores = (
        jnp.einsum("rhk,rck->rhc", queries, latent_cache, preferred_element_type=jnp.float32)
        * score_scale
    )
    in_range = jnp.arange(latent_cache.shape[1])[None, None, :] < lengths[:, None, None]
    scores = jnp.where(in_range, scores, -jnp.inf)
    row_max = jnp.max(scores, axis=-1, keepdims=True)
    raised = jnp.exp(scores - row_max)
    probs = (raised / jnp.sum(raised, axis=-1, keepdims=True)).astype(jnp.bfloat16)
    attended = jnp.einsum(
        "rhc,rcl->rhl", probs, latent_cache[:, :, :LAT], preferred_element_type=jnp.float32
    )
    return attended.astype(jnp.bfloat16)


def to_other_core(rows):
    return lax.ppermute(rows, "core", [(0, 1), (1, 0)])


def between_chips(rows):
    return lax.all_to_all(rows, CHIPS, split_axis=0, concat_axis=0, tiled=True)


def shards(
    hidden, norm_gain, routes, gate_values, w_gate, w_up, w_down, queries, latent_cache, lengths
):
    sent = pack(hidden, norm_gain, routes)
    own_rows = between_chips(sent)
    other_rows = to_other_core(own_rows)
    own_act = gate_up(own_rows, w_gate, w_up)
    other_act = gate_up(other_rows, w_gate, w_up)
    for_other = down(other_act, w_down)
    from_other = to_other_core(for_other)
    summed = down(own_act, w_down, from_other)
    returned = between_chips(summed)
    attn_out = attend(queries, latent_cache, lengths)
    moe_out = combine(returned, routes, gate_values)
    return (moe_out, attn_out)


def solution(mesh):
    fine = Mesh(mesh.devices.reshape(SIZES), AXES)
    placed = (
        P(AXES, None),
        P(),
        P(AXES, None),
        P(AXES, None),
        P(None, AXES),
        P(None, AXES),
        P(AXES, None),
        P(AXES, None, None),
        P(AXES, None, None),
        P(AXES),
    )
    return jax.shard_map(
        shards,
        mesh=fine,
        in_specs=placed,
        out_specs=(P(AXES, None), P(AXES, None, None)),
        check_vma=False,
    )
```

time: 295 us -> 169 us (0.57)
  the two profiles are of different devices: /device:TPU:42 before, /device:TPU:4 now
where the time goes in v1:
time: 169 us
  blocking collectives  58 us (34%)
  waiting for transfers between devices  53.9 us (32%)
  Pallas kernels  35.6 us (21%)
  local copies, waits for them, and re-layouts  10.4 us (6%)
  starting transfers between devices  6.96 us (4%)
  matrix products  1.92 us (1%)
    all_to_all x1, blocking collectives, between_chips(): return lax.all_to_all(rows, CHIPS, split_axis=0, concat_axis=0, tiled=True)  58 us
    all_to_all x1, waiting for transfers between devices, between_chips(): return lax.all_to_all(rows, CHIPS, split_axis=0, concat_axis=0, tiled=True)  47.5 us
    pallas_call x2, Pallas kernels, gate_up(): pl.pallas_call(gate_up_kernel, grid=(width // STEP,), in_specs=[pl.BlockS...  15.5 us
    pallas_call x2, Pallas kernels, down(): pl.pallas_call(down_kernel, grid=(steps,), in_specs=[pl.BlockSpec(act.sha...  12.8 us
    unnamed x26, local copies, waits for them, and re-layouts  10.4 us
    all_to_all x1, starting transfers between devices, between_chips(): return lax.all_to_all(rows, CHIPS, split_axis=0, concat_axis=0, tiled=True)  6.74 us
    ppermute x2, waiting for transfers between devices, to_other_core(): return lax.ppermute(rows, 'core', [(0, 1), (1, 0)])  6.41 us
    pallas_call x1, Pallas kernels, combine(): pl.pallas_call(combine_kernel, grid=(width // STEP,), in_specs=[pl.BlockS...  5.92 us
  transfers between devices with their start and end apart: 3, of which 2 were waited for; matrix products, arithmetic and copies ran while one was open for 1% of the time, Pallas kernels for 5%

profile of v1, /device:TPU:4, one launch (start us, length us, event | category | flops | bytes accessed | tf_op | source)
XLA Modules:
  0.0 168.5 jit_solution(2325709137239076678)
XLA Ops:
  0.6 0.0 copy-start
  0.6 0.0 copy-start.5
  0.7 0.9 copy-done.5
  1.6 0.0 copy-start.6
  1.6 0.7 copy-done.6
  2.3 0.0 copy-start.7
  2.3 0.7 copy-done.7
  3.0 1.3 pack_rows.1
  4.4 0.0 copy-start.1
  4.4 0.0 slice-start
  4.4 58.0 %all_to_all.22 = bf16[64,16,1792]{2,1,0:T(8,128)(2,1)S(1)} all-to-all(bf16[64,16,1792]{2,1,0:T(8,128)(2,1)S(1)} %bitcast.35), channel_id=1, replica_groups=mesh['zl'=2,'zh'=2,'x'=4,'y'=4,'core'=2] {'zl','zh','x','y'}, dimensions={0} | all-to-all | bytes 7340032 | tf_op jit(solution)/shard_map/all_to_all | solution.py:268
  62.4 0.0 collective-permute-start
  62.4 6.4 %collective-permute-done.rows_ref = bf16[1024,1792]{1,0:T(8,128)(2,1)S(1)} collective-permute-done((bf16[1024,1792]{1,0:T(8,128)(2,1)S(1)}, bf16[1024,1792]{1,0:T(8,128)(2,1)S(1)}, u32[]{:S(2)}, u32[]{:S(2)}) %collective-permute-start) | collective-permute-done | bytes 3670048 | tf_op jit(solution)/shard_map/ppermute | solution.py:264
  68.8 0.0 copy-done.1
  68.8 0.0 copy-start.2
  68.8 3.1 %copy-done.2 = bf16[7168,512]{1,0:T(8,128)(2,1)S(1)} copy-done((bf16[7168,512]{1,0:T(8,128)(2,1)S(1)}, bf16[7168,512]{1,0:T(8,128)(2,1)}, u32[]{:S(2)}) %copy-start.2) | copy-done | bytes 7340056
  71.9 0.0 slice-start.1
  71.9 7.8 %gate_up.3.act_ref = bf16[256,512]{1,0:T(8,128)(2,1)S(1)} custom-call(bf16[1024,1792]{1,0:T(8,128)(2,1)S(1)} %collective-permute-done.rows_ref, bf16[4,1792,512]{2,1,0:T(8,128)(2,1)S(1)} %bitcast.30, bf16[4,1792,512]{2,1,0:T(8,128)(2,1)S(1)} %bitcast.32), custom_call_target="tpu_custom_call" | custom-call | flops 3758096384 | bytes 18350080 | tf_op jit(solution)/shard_map/gate_up/pallas_call | solution.py:122
  79.7 0.0 slice-done
  79.7 0.0 slice-done.1
  79.7 6.2 %down.2 = bf16[1024,1792]{1,0:T(8,128)(2,1)S(1)} custom-call(bf16[256,512]{1,0:T(8,128)(2,1)S(1)} %gate_up.3.act_ref, bf16[512,7168]{1,0:T(8,128)(2,1)S(1)} %bitcast.29, bf16[512,7168]{1,0:T(8,128)(2,1)S(1)} %bitcast.29, bf16[512,7168]{1,0:T(8,128)(2,1)S(1)} %bitcast.29, bf16[512,7168]{1,0:T(8,128)(2,1)S(1)} %bitcast.29), custom_call_target="tpu_custom_call" | custom-call | flops 1879048192 | bytes 11010048 | tf_op jit(solution)/shard_map/down/pallas_call | solution.py:181
  85.9 0.2 collective-permute-start.1
  86.2 0.0 copy-start.3
  86.2 3.1 %copy-done.3 = bf16[7168,512]{1,0:T(8,128)(2,1)S(1)} copy-done((bf16[7168,512]{1,0:T(8,128)(2,1)S(1)}, bf16[7168,512]{1,0:T(8,128)(2,1)}, u32[]{:S(2)}) %copy-start.3) | copy-done | bytes 7340056
  89.2 7.8 %gate_up.2.act_ref = bf16[256,512]{1,0:T(8,128)(2,1)S(1)} custom-call(bf16[1024,1792]{1,0:T(8,128)(2,1)S(1)} %bitcast.37, bf16[4,1792,512]{2,1,0:T(8,128)(2,1)S(1)} %bitcast.31, bf16[4,1792,512]{2,1,0:T(8,128)(2,1)S(1)} %bitcast.33), custom_call_target="tpu_custom_call" | custom-call | flops 3758096384 | bytes 18350080 | tf_op jit(solution)/shard_map/gate_up/pallas_call | solution.py:122
  97.0 0.0 collective-permute-done.1.refs_4_
  97.0 6.5 %down.3 = bf16[1024,1792]{1,0:T(8,128)(2,1)S(1)} custom-call(bf16[256,512]{1,0:T(8,128)(2,1)S(1)} %gate_up.2.act_ref, bf16[512,7168]{1,0:T(8,128)(2,1)S(1)} %bitcast.29, bf16[512,7168]{1,0:T(8,128)(2,1)S(1)} %bitcast.29, bf16[512,7168]{1,0:T(8,128)(2,1)S(1)} %bitcast.29, bf16[512,7168]{1,0:T(8,128)(2,1)S(1)} %bitcast.29, ...), custom_call_target="tpu_custom_call" | custom-call | flops 1879048192 | bytes 14680064 | tf_op jit(solution)/shard_map/down/pallas_call | solution.py:181
  103.6 0.0 copy-start.4
  103.6 1.8 %copy-done.4 = bf16[1024,1792]{1,0:T(8,128)(2,1)} copy-done((bf16[1024,1792]{1,0:T(8,128)(2,1)}, bf16[1024,1792]{1,0:T(8,128)(2,1)S(1)}, u32[]{:S(2)}) %copy-start.4) | copy-done | bytes 3670040
  105.4 0.0 copy-start.10
  105.4 6.7 %all-to-all-start.1 = ((bf16[64,16,1792]{2,1,0:T(8,128)(2,1)}), bf16[64,16,1792]{2,1,0:T(8,128)(2,1)}, u32[]{:S(2)}, u32[]{:S(2)}) async-start(bf16[64,16,1792]{2,1,0:T(8,128)(2,1)} %bitcast.34), calls=%async_computation.1 | async-start | bytes 7340032 | tf_op jit(solution)/shard_map/all_to_all | solution.py:268
  112.8 0.0 copy-done
  112.9 0.0 copy-done.10
  112.9 0.6 fusion.15
  113.5 0.0 copy-start.8
  113.5 0.0 copy-start.9
  113.5 0.3 fusion.11
  113.7 1.3 fusion.8
  115.1 47.5 %all-to-all-done.1 = bf16[64,16,1792]{2,1,0:T(8,128)(2,1)} async-done(((bf16[64,16,1792]{2,1,0:T(8,128)(2,1)}), bf16[64,16,1792]{2,1,0:T(8,128)(2,1)}, u32[]{:S(2)}, u32[]{:S(2)}) %all-to-all-start.1) | async-done | bytes 3670048 | tf_op jit(solution)/shard_map/all_to_all | solution.py:268
  162.6 0.0 copy-done.8
  162.6 0.0 copy-done.9
  162.6 5.9 %combine.1 = bf16[8,7168]{1,0:T(8,128)(2,1)} custom-call(bf16[1024,1792]{1,0:T(8,128)(2,1)} %bitcast.6.rows_ref, s32[8,8]{1,0:T(8,128)S(1)} %copy-done.8, f32[8,8]{1,0:T(8,128)S(1)} %copy-done.9), custom_call_target="tpu_custom_call" | custom-call | tf_op jit(solution)/shard_map/combine/pallas_call | solution.py:231
  (2 shorter events, 0.0 us)
Async XLA Ops:
  0.6 112.2 %copy-start = (bf16[1,128,576]{1,2,0:T(8,128)(2,1)S(1)}, bf16[1,128,576]{1,2,0:T(8,128)(2,1)}, u32[]{:S(2)}) copy-start(bf16[1,128,576]{1,2,0:T(8,128)(2,1)} %param.17) | copy-start | bytes 442372
  0.6 0.9 copy-start.5
  1.6 0.7 copy-start.6
  2.3 0.7 copy-start.7
  4.4 64.4 %copy-start.1 = (bf16[7168,512]{1,0:T(8,128)(2,1)S(1)}, bf16[7168,512]{1,0:T(8,128)(2,1)}, u32[]{:S(2)}) copy-start(bf16[7168,512]{1,0:T(8,128)(2,1)} %param.14) | copy-start | bytes 22020100
  4.4 75.3 %slice-start = ((s8[7340032]{0:T(1024)(128)(4,1)}), s8[4194304]{0:T(1024)(128)(4,1)S(1)}, s32[]{:S(2)}) async-start(s8[7340032]{0:T(1024)(128)(4,1)} %bitcast.28), calls=%async_computation.2 | async-start | bytes 8388608
  62.4 6.4 %collective-permute-start = (bf16[1024,1792]{1,0:T(8,128)(2,1)S(1)}, bf16[1024,1792]{1,0:T(8,128)(2,1)S(1)}, u32[]{:S(2)}, u32[]{:S(2)}) collective-permute-start(bf16[1024,1792]{1,0:T(8,128)(2,1)S(1)} %bitcast.36), channel_id=1, source_target_pairs={{0,1},{1,0},{2,3},{3,2},{4,5},{5,4},{6,7},{7,6},{8,9},{9,8},{10,11... | collective-permute-start | bytes 11010056 | tf_op jit(solution)/shard_map/ppermute | solution.py:264
  68.8 3.1 %copy-start.2 = (bf16[7168,512]{1,0:T(8,128)(2,1)S(1)}, bf16[7168,512]{1,0:T(8,128)(2,1)}, u32[]{:S(2)}) copy-start(bf16[7168,512]{1,0:T(8,128)(2,1)} %param.15) | copy-start | bytes 22020100
  71.9 7.8 %slice-start.1 = ((s8[7340032]{0:T(1024)(128)(4,1)}), s8[3145728]{0:T(1024)(128)(4,1)S(1)}, s32[]{:S(2)}) async-start(s8[7340032]{0:T(1024)(128)(4,1)} %bitcast.28), calls=%async_computation.3 | async-start | bytes 6291456
  85.9 11.1 %collective-permute-start.1 = (bf16[1024,1792]{1,0:T(8,128)(2,1)S(1)}, bf16[1024,1792]{1,0:T(8,128)(2,1)S(1)}, u32[]{:S(2)}, u32[]{:S(2)}) collective-permute-start(bf16[1024,1792]{1,0:T(8,128)(2,1)S(1)} %down.2), channel_id=1, source_target_pairs={{0,1},{1,0},{2,3},{3,2},{4,5},{5,4},{6,7},{7,6},{8,9},{9,8},{10,11... | collective-permute-start | bytes 11010056 | tf_op jit(solution)/shard_map/ppermute | solution.py:264
  86.2 3.1 %copy-start.3 = (bf16[7168,512]{1,0:T(8,128)(2,1)S(1)}, bf16[7168,512]{1,0:T(8,128)(2,1)}, u32[]{:S(2)}) copy-start(bf16[7168,512]{1,0:T(8,128)(2,1)} %param.15) | copy-start | bytes 22020100
  103.6 1.9 %copy-start.4 = (bf16[1024,1792]{1,0:T(8,128)(2,1)}, bf16[1024,1792]{1,0:T(8,128)(2,1)S(1)}, u32[]{:S(2)}) copy-start(bf16[1024,1792]{1,0:T(8,128)(2,1)S(1)} %down.3) | copy-start | bytes 11010052
  105.4 7.4 %copy-start.10 = (bf16[1,1536,576]{1,2,0:T(8,128)(2,1)S(1)}, bf16[1,1536,576]{1,2,0:T(8,128)(2,1)}, u32[]{:S(2)}) copy-start(bf16[1,1536,576]{1,2,0:T(8,128)(2,1)} %param.18) | copy-start | bytes 5308420
  105.4 57.1 %all-to-all-start.1 = ((bf16[64,16,1792]{2,1,0:T(8,128)(2,1)}), bf16[64,16,1792]{2,1,0:T(8,128)(2,1)}, u32[]{:S(2)}, u32[]{:S(2)}) async-start(bf16[64,16,1792]{2,1,0:T(8,128)(2,1)} %bitcast.34), calls=%async_computation.1 | async-start | bytes 7340032 | tf_op jit(solution)/shard_map/all_to_all | solution.py:268
  113.5 49.1 %copy-start.8 = (s32[8,8]{1,0:T(8,128)S(1)}, s32[8,8]{1,0:T(8,128)}, u32[]{:S(2)}) copy-start(s32[8,8]{1,0:T(8,128)} %routes_ref.3) | copy-start | bytes 772
  113.5 49.1 %copy-start.9 = (f32[8,8]{1,0:T(8,128)S(1)}, f32[8,8]{1,0:T(8,128)}, u32[]{:S(2)}) copy-start(f32[8,8]{1,0:T(8,128)} %gates_ref.1) | copy-start | bytes 772

commit v2 on v0

v2 whole, which is shorter than its diff:
```python
import jax
import jax.numpy as jnp
from jax import lax
from jax.experimental import pallas as pl
from jax.experimental.pallas import tpu as pltpu
from jax.sharding import Mesh, PartitionSpec as P

LAT = 512
EXPERTS = 32
CAP = 4

AXES = ("zl", "zh", "x", "y", "core")
SIZES = (2, 2, 4, 4, 2)
CHIPS = ("zl", "zh", "x", "y")
N_CHIPS = 64
QUARTERS = 4
BLOCK = CAP * QUARTERS
ROWS = N_CHIPS * BLOCK
STEP = 256

norm_eps = 1e-06
score_scale = 0.07216878364870322


def slot_matches(routes, lanes):
    rows = routes.shape[0]
    packed_row = lax.broadcasted_iota(jnp.int32, (rows, lanes), 1)
    expert = packed_row // (2 * BLOCK)
    slot = packed_row % CAP
    piece = (packed_row // CAP) % QUARTERS
    named = jnp.zeros((rows, lanes), jnp.bool_)
    for k in range(routes.shape[1]):
        named = named | (routes[:, k : k + 1] == expert)
    before = (
        lax.broadcasted_iota(jnp.int32, (rows, rows), 0)
        > lax.broadcasted_iota(jnp.int32, (rows, rows), 1)
    ).astype(jnp.float32)
    rank = jnp.dot(before, named.astype(jnp.float32), preferred_element_type=jnp.float32)
    return expert, piece, named & (rank == slot.astype(jnp.float32))


def pack_kernel(hidden_ref, gain_ref, routes_ref, send_ref):
    features = hidden_ref[...].astype(jnp.float32)
    squares = jnp.mean(features * features, axis=-1, keepdims=True)
    normed = features * lax.rsqrt(squares + norm_eps) * gain_ref[...]
    width = send_ref.shape[1]
    stacked = jnp.concatenate(
        [normed[:, q * width : (q + 1) * width] for q in range(QUARTERS)], axis=0
    ).astype(jnp.bfloat16)
    _, piece, match = slot_matches(routes_ref[...], send_ref.shape[0])
    picked = jnp.concatenate(
        [(match & (piece == q)).astype(jnp.float32) for q in range(QUARTERS)], axis=0
    ).astype(jnp.bfloat16)
    for start in range(0, send_ref.shape[0], STEP):
        send_ref[start : start + STEP, :] = lax.dot_general(
            picked[:, start : start + STEP],
            stacked,
            (((0,), (0,)), ((), ())),
            preferred_element_type=jnp.float32,
        ).astype(jnp.bfloat16)


def pack(hidden, norm_gain, routes):
    width = hidden.shape[1] // QUARTERS
    return pl.pallas_call(
        pack_kernel,
        out_shape=jax.ShapeDtypeStruct((ROWS, width), jnp.bfloat16),
        compiler_params=pltpu.CompilerParams(vmem_limit_bytes=24 * 2**20),
        name="pack_rows",
    )(hidden, norm_gain.reshape(1, -1), routes)


def gate_up_kernel(rows_ref, gate_ref, up_ref, act_ref, rows):
    width = rows_ref.shape[1]
    slots = ROWS // QUARTERS
    for start in range(0, width, STEP):
        blocks = rows_ref[:, start : start + STEP].reshape(N_CHIPS, BLOCK, STEP)
        for q in range(QUARTERS):
            rows[:, q * width + start : q * width + start + STEP] = blocks[
                :, q * CAP : (q + 1) * CAP, :
            ].reshape(slots, STEP)
    gate = jnp.dot(rows[...], gate_ref[...], preferred_element_type=jnp.float32)
    up = jnp.dot(rows[...], up_ref[...], preferred_element_type=jnp.float32)
    act_ref[...] = (gate / (1.0 + jnp.exp(-gate)) * up).astype(jnp.bfloat16)


def gate_up(packed, w_gate, w_up):
    in_vmem = pl.BlockSpec(memory_space=pltpu.VMEM)
    slots = ROWS // QUARTERS
    depth, units = w_gate.shape
    return pl.pallas_call(
        gate_up_kernel,
        in_specs=[in_vmem] * 3,
        out_specs=in_vmem,
        out_shape=jax.ShapeDtypeStruct((slots, units), jnp.bfloat16),
        scratch_shapes=[pltpu.VMEM((slots, depth), jnp.bfloat16)],
        compiler_params=pltpu.CompilerParams(vmem_limit_bytes=12 * 2**20),
        cost_estimate=pl.CostEstimate(
            flops=2 * 2 * slots * w_gate.size,
            bytes_accessed=2 * (2 * w_gate.size + packed.size),
            transcendentals=0,
        ),
        name="gate_up",
    )(packed, w_gate, w_up)


def down_kernel(near_act_ref, far_act_ref, near_ref, far_ref, out_ref):
    width = out_ref.shape[1]
    for start in range(0, width, STEP):
        pieces = []
        for q in range(QUARTERS):
            columns = slice(q * width + start, q * width + start + STEP)
            piece = jnp.dot(
                near_act_ref[...], near_ref[:, columns], preferred_element_type=jnp.float32
            ) + jnp.dot(far_act_ref[...], far_ref[:, columns], preferred_element_type=jnp.float32)
            pieces.append(piece.reshape(N_CHIPS, CAP, STEP))
        out_ref[:, start : start + STEP] = (
            jnp.concatenate(pieces, axis=1).reshape(ROWS, STEP).astype(jnp.bfloat16)
        )


def down(near_act, far_act, near, far):
    in_vmem = pl.BlockSpec(memory_space=pltpu.VMEM)
    width = near.shape[1] // QUARTERS
    return pl.pallas_call(
        down_kernel,
        in_specs=[in_vmem] * 4,
        out_specs=in_vmem,
        out_shape=jax.ShapeDtypeStruct((ROWS, width), jnp.bfloat16),
        compiler_params=pltpu.CompilerParams(vmem_limit_bytes=12 * 2**20),
        cost_estimate=pl.CostEstimate(
            flops=2 * 2 * near_act.shape[0] * near.size,
            bytes_accessed=2 * (2 * near.size + ROWS * width),
            transcendentals=0,
        ),
        name="down",
    )(near_act, far_act, near, far)


def weigh_kernel(routes_ref, gates_ref, weigh_ref):
    routes = routes_ref[...]
    gates = gates_ref[...]
    expert, piece, match = slot_matches(routes, weigh_ref.shape[1])
    gate = jnp.zeros(expert.shape, jnp.float32)
    for k in range(routes.shape[1]):
        gate = gate + jnp.where(routes[:, k : k + 1] == expert, gates[:, k : k + 1], 0.0)
    spread = jnp.concatenate(
        [jnp.where(match & (piece == q), gate, 0.0) for q in range(QUARTERS)], axis=0
    )
    high = spread.astype(jnp.bfloat16)
    low = (spread - high.astype(jnp.float32)).astype(jnp.bfloat16)
    weigh_ref[...] = jnp.concatenate([high, low], axis=0)


def weigh(routes, gate_values):
    return pl.pallas_call(
        weigh_kernel,
        out_shape=jax.ShapeDtypeStruct((2 * QUARTERS * routes.shape[0], ROWS), jnp.bfloat16),
        name="slot_weights",
    )(routes, gate_values)


def combine_kernel(rows_ref, weigh_ref, out_ref, total):
    step = pl.program_id(0)
    part = jnp.dot(weigh_ref[...], rows_ref[...], preferred_element_type=jnp.float32)

    @pl.when(step == 0)
    def _():
        total[...] = part

    @pl.when(step > 0)
    def _():
        total[...] += part

    @pl.when(step == pl.num_programs(0) - 1)
    def _():
        tok_rows = out_ref.shape[0]
        half = QUARTERS * tok_rows
        width = total.shape[1]
        both = (total[:half] + total[half:]).astype(jnp.bfloat16)
        for q in range(QUARTERS):
            out_ref[:, q * width : (q + 1) * width] = both[q * tok_rows : (q + 1) * tok_rows]


def combine(returned, weights):
    width = returned.shape[1]
    tok_rows = weights.shape[0] // (2 * QUARTERS)
    return pl.pallas_call(
        combine_kernel,
        grid=(ROWS // STEP,),
        in_specs=[
            pl.BlockSpec((STEP, width), lambda j: (j, 0)),
            pl.BlockSpec((weights.shape[0], STEP), lambda j: (0, j)),
        ],
        out_specs=pl.BlockSpec((tok_rows, width * QUARTERS), lambda j: (0, 0)),
        out_shape=jax.ShapeDtypeStruct((tok_rows, width * QUARTERS), jnp.bfloat16),
        scratch_shapes=[pltpu.VMEM((weights.shape[0], width), jnp.float32)],
        compiler_params=pltpu.CompilerParams(vmem_limit_bytes=16 * 2**20),
        name="combine",
    )(returned, weights)


def attend(queries, latent_cache, lengths):
    scores = (
        jnp.einsum("rhk,rck->rhc", queries, latent_cache, preferred_element_type=jnp.float32)
        * score_scale
    )
    in_range = jnp.arange(latent_cache.shape[1])[None, None, :] < lengths[:, None, None]
    scores = jnp.where(in_range, scores, -jnp.inf)
    row_max = jnp.max(scores, axis=-1, keepdims=True)
    raised = jnp.exp(scores - row_max)
    probs = (raised / jnp.sum(raised, axis=-1, keepdims=True)).astype(jnp.bfloat16)
    attended = jnp.einsum(
        "rhc,rcl->rhl", probs, latent_cache[:, :, :LAT], preferred_element_type=jnp.float32
    )
    return attended.astype(jnp.bfloat16)


def to_other_core(rows):
    return lax.ppermute(rows, "core", [(0, 1), (1, 0)])


def between_chips(rows):
    return lax.all_to_all(rows, CHIPS, split_axis=0, concat_axis=0, tiled=True)


def shards(
    hidden, norm_gain, routes, gate_values, w_gate, w_up, w_down, queries, latent_cache, lengths
):
    far_gate, far_up, far_down = [to_other_core(w) for w in (w_gate, w_up, w_down)]
    sent = pack(hidden, norm_gain, routes)
    arrived = between_chips(sent)
    near_act = gate_up(arrived, w_gate, w_up)
    far_act = gate_up(arrived, far_gate, far_up)
    partial_rows = down(near_act, far_act, w_down, far_down)
    returned = between_chips(partial_rows)
    attn_out = attend(queries, latent_cache, lengths)
    moe_out = combine(returned, weigh(routes, gate_values))
    return (moe_out, attn_out)


def solution(mesh):
    fine = Mesh(mesh.devices.reshape(SIZES), AXES)
    placed = (
        P(AXES, None),
        P(),
        P(AXES, None),
        P(AXES, None),
        P(None, AXES),
        P(None, AXES),
        P(AXES, None),
        P(AXES, None, None),
        P(AXES, None, None),
        P(AXES),
    )
    return jax.shard_map(
        shards,
        mesh=fine,
        in_specs=placed,
        out_specs=(P(AXES, None), P(AXES, None, None)),
        check_vma=False,
    )
```

time: 295 us -> 142 us (0.48)
  the two profiles are of different devices: /device:TPU:42 before, /device:TPU:4 now
where the time goes in v2:
time: 142 us; the launch traced here: 141 us
  blocking collectives  59.8 us (42%)
  waiting for transfers between devices  44.3 us (31%)
  Pallas kernels  19 us (13%)
  starting transfers between devices  7.41 us (5%)
  local copies, waits for them, and re-layouts  7.28 us (5%)
  matrix products  1.92 us (1%)
  between operations  1.43 us (1%)
    all_to_all x1, blocking collectives, between_chips(): return lax.all_to_all(rows, CHIPS, split_axis=0, concat_axis=0, tiled=True)  59.8 us
    all_to_all x1, waiting for transfers between devices, between_chips(): return lax.all_to_all(rows, CHIPS, split_axis=0, concat_axis=0, tiled=True)  44.3 us
    pallas_call x2, Pallas kernels, gate_up(): pl.pallas_call(gate_up_kernel, in_specs=[in_vmem] * 3, out_specs=in_vmem,...  7.9 us
    unnamed x22, local copies, waits for them, and re-layouts  7.28 us
    all_to_all x1, starting transfers between devices, between_chips(): return lax.all_to_all(rows, CHIPS, split_axis=0, concat_axis=0, tiled=True)  6.73 us
    pallas_call x1, Pallas kernels, combine(): pl.pallas_call(combine_kernel, grid=(ROWS // STEP,), in_specs=[pl.BlockSp...  4.1 us
    pallas_call x1, Pallas kernels, down(): pl.pallas_call(down_kernel, in_specs=[in_vmem] * 4, out_specs=in_vmem, ou...  4.07 us
  transfers between devices with their start and end apart: 4, of which 1 were waited for; matrix products, arithmetic and copies ran while one was open for 2% of the time, Pallas kernels for 8%

profile of v2, /device:TPU:4, one launch (start us, length us, event | category | flops | bytes accessed | tf_op | source)
XLA Modules:
  0.0 141.4 jit_solution(16654955381863776977)
XLA Ops:
  0.6 0.0 copy-start
  0.6 0.1 collective-permute-start
  0.7 0.5 collective-permute-start.1
  1.2 0.1 collective-permute-start.2
  1.3 0.0 copy-start.5
  1.3 0.9 copy-done.5
  2.2 0.0 copy-start.6
  2.2 0.7 copy-done.6
  3.0 0.0 copy-start.7
  3.0 0.7 copy-done.7
  3.7 1.3 pack_rows.1
  5.0 0.0 copy-start.2
  5.0 59.8 %all_to_all.22 = bf16[64,16,1792]{2,1,0:T(8,128)(2,1)S(1)} all-to-all(bf16[64,16,1792]{2,1,0:T(8,128)(2,1)S(1)} %bitcast.29), channel_id=1, replica_groups=mesh['zl'=2,'zh'=2,'x'=4,'y'=4,'core'=2] {'zl','zh','x','y'}, dimensions={0} | all-to-all | bytes 7340032 | tf_op jit(solution)/shard_map/all_to_all | solution.py:224
  64.8 0.0 copy-done.2
  64.8 0.0 copy-start.3
  64.8 3.1 %copy-done.3 = bf16[7168,512]{1,0:T(8,128)(2,1)S(1)} copy-done((bf16[7168,512]{1,0:T(8,128)(2,1)S(1)}, bf16[7168,512]{1,0:T(8,128)(2,1)}, u32[]{:S(2)}) %copy-start.3) | copy-done | bytes 7340056
  67.9 0.0 slice-start
  67.9 3.9 %gate_up.2.near_act_ref = bf16[256,512]{1,0:T(8,128)(2,1)S(1)} custom-call(bf16[1024,1792]{1,0:T(8,128)(2,1)S(1)} %bitcast.26, bf16[7168,512]{1,0:T(8,128)(2,1)S(1)} %copy-done.2, bf16[7168,512]{1,0:T(8,128)(2,1)S(1)} %copy-done.3), custom_call_target="tpu_custom_call" | custom-call | flops 3758096384 | bytes 18350080 | tf_op jit(solution)/shard_map/gate_up/pallas_call | solution.py:91
  71.9 0.0 slice-start.1
  71.9 0.0 collective-permute-done.gate_ref
  71.9 0.0 collective-permute-done.1.up_ref
  71.9 4.0 %gate_up.3.far_act_ref = bf16[256,512]{1,0:T(8,128)(2,1)S(1)} custom-call(bf16[1024,1792]{1,0:T(8,128)(2,1)S(1)} %bitcast.27, bf16[7168,512]{1,0:T(8,128)(2,1)S(1)} %collective-permute-done.gate_ref, bf16[7168,512]{1,0:T(8,128)(2,1)S(1)} %collective-permute-done.1.up_ref), custom_call_target="tpu_custom_call" | custom-call | flops 3758096384 | bytes 18350080 | tf_op jit(solution)/shard_map/gate_up/pallas_call | solution.py:91
  75.9 0.0 collective-permute-done.2.far_ref
  75.9 0.0 slice-done
  75.9 0.0 slice-done.1
  75.9 4.1 %down.1 = bf16[1024,1792]{1,0:T(8,128)(2,1)S(1)} custom-call(bf16[256,512]{1,0:T(8,128)(2,1)S(1)} %gate_up.2.near_act_ref, bf16[256,512]{1,0:T(8,128)(2,1)S(1)} %gate_up.3.far_act_ref, bf16[512,7168]{1,0:T(8,128)(2,1)S(1)} %bitcast.31, bf16[512,7168]{1,0:T(8,128)(2,1)S(1)} %collective-permute-done.2.far_ref), custom_call_target="tpu_custom_call" | custom-call | flops 3758096384 | bytes 18350080 | tf_op jit(solution)/shard_map/down/pallas_call | solution.py:125
  80.0 0.0 copy-start.1
  80.0 1.8 %copy-done.1 = bf16[1024,1792]{1,0:T(8,128)(2,1)} copy-done((bf16[1024,1792]{1,0:T(8,128)(2,1)}, bf16[1024,1792]{1,0:T(8,128)(2,1)S(1)}, u32[]{:S(2)}) %copy-start.1) | copy-done | bytes 3670040
  81.8 0.0 copy-start.8
  81.8 6.7 %all-to-all-start.1 = ((bf16[64,16,1792]{2,1,0:T(8,128)(2,1)}), bf16[64,16,1792]{2,1,0:T(8,128)(2,1)}, u32[]{:S(2)}, u32[]{:S(2)}) async-start(bf16[64,16,1792]{2,1,0:T(8,128)(2,1)} %bitcast.28), calls=%async_computation.1 | async-start | bytes 7340032 | tf_op jit(solution)/shard_map/all_to_all | solution.py:224
  89.2 1.6 %slot_weights.1.weigh_ref = bf16[64,1024]{1,0:T(8,128)(2,1)} custom-call(s32[8,8]{1,0:T(8,128)} %routes_ref.3, f32[8,8]{1,0:T(8,128)} %gates_ref.1), custom_call_target="tpu_custom_call" | custom-call | tf_op jit(solution)/shard_map/slot_weights/pallas_call | solution.py:156
  90.8 0.0 copy-done
  90.8 0.0 copy-done.8
  90.8 0.6 fusion.15
  91.4 0.0 copy-start.4
  91.4 0.3 fusion.11
  91.7 1.3 fusion.8
  93.0 44.3 %all-to-all-done.1 = bf16[64,16,1792]{2,1,0:T(8,128)(2,1)} async-done(((bf16[64,16,1792]{2,1,0:T(8,128)(2,1)}), bf16[64,16,1792]{2,1,0:T(8,128)(2,1)}, u32[]{:S(2)}, u32[]{:S(2)}) %all-to-all-start.1) | async-done | bytes 3670048 | tf_op jit(solution)/shard_map/all_to_all | solution.py:224
  137.3 0.0 copy-done.4
  137.3 4.1 %combine.1 = bf16[8,7168]{1,0:T(8,128)(2,1)} custom-call(bf16[1024,1792]{1,0:T(8,128)(2,1)} %bitcast.4.rows_ref, bf16[64,1024]{1,0:T(8,128)(2,1)S(1)} %copy-done.4), custom_call_target="tpu_custom_call" | custom-call | tf_op jit(solution)/shard_map/combine/pallas_call | solution.py:188
  (2 shorter events, 0.0 us)
Async XLA Ops:
  0.6 90.2 %copy-start = (bf16[1,128,576]{1,2,0:T(8,128)(2,1)S(1)}, bf16[1,128,576]{1,2,0:T(8,128)(2,1)}, u32[]{:S(2)}) copy-start(bf16[1,128,576]{1,2,0:T(8,128)(2,1)} %param.17) | copy-start | bytes 442372
  0.6 71.2 %collective-permute-start = (bf16[7168,512]{1,0:T(8,128)(2,1)}, bf16[7168,512]{1,0:T(8,128)(2,1)S(1)}, u32[]{:S(2)}, u32[]{:S(2)}) collective-permute-start(bf16[7168,512]{1,0:T(8,128)(2,1)} %gate_ref.1), channel_id=1, source_target_pairs={{0,1},{1,0},{2,3},{3,2},{4,5},{5,4},{6,7},{7,6},{8,9},{9,8},{10,11... | collective-permute-start | bytes 22020104 | tf_op jit(solution)/shard_map/ppermute | solution.py:220
  0.7 71.2 %collective-permute-start.1 = (bf16[7168,512]{1,0:T(8,128)(2,1)}, bf16[7168,512]{1,0:T(8,128)(2,1)S(1)}, u32[]{:S(2)}, u32[]{:S(2)}) collective-permute-start(bf16[7168,512]{1,0:T(8,128)(2,1)} %up_ref.1), channel_id=1, source_target_pairs={{0,1},{1,0},{2,3},{3,2},{4,5},{5,4},{6,7},{7,6},{8,9},{9,8},{10,11... | collective-permute-start | bytes 22020104 | tf_op jit(solution)/shard_map/ppermute | solution.py:220
  1.2 74.6 %collective-permute-start.2 = (bf16[512,7168]{1,0:T(8,128)(2,1)}, bf16[512,7168]{1,0:T(8,128)(2,1)S(1)}, u32[]{:S(2)}, u32[]{:S(2)}) collective-permute-start(bf16[512,7168]{1,0:T(8,128)(2,1)} %near_ref.1), channel_id=1, source_target_pairs={{0,1},{1,0},{2,3},{3,2},{4,5},{5,4},{6,7},{7,6},{8,9},{9,8},{10,11... | collective-permute-start | bytes 22020104 | tf_op jit(solution)/shard_map/ppermute | solution.py:220
  1.3 0.9 copy-start.5
  2.2 0.7 copy-start.6
  3.0 0.7 copy-start.7
  5.0 59.8 %copy-start.2 = (bf16[7168,512]{1,0:T(8,128)(2,1)S(1)}, bf16[7168,512]{1,0:T(8,128)(2,1)}, u32[]{:S(2)}) copy-start(bf16[7168,512]{1,0:T(8,128)(2,1)} %gate_ref.1) | copy-start | bytes 22020100
  64.8 3.1 %copy-start.3 = (bf16[7168,512]{1,0:T(8,128)(2,1)S(1)}, bf16[7168,512]{1,0:T(8,128)(2,1)}, u32[]{:S(2)}) copy-start(bf16[7168,512]{1,0:T(8,128)(2,1)} %up_ref.1) | copy-start | bytes 22020100
  67.9 8.0 %slice-start = ((s8[7340032]{0:T(1024)(128)(4,1)}), s8[4194304]{0:T(1024)(128)(4,1)S(1)}, s32[]{:S(2)}) async-start(s8[7340032]{0:T(1024)(128)(4,1)} %bitcast.30), calls=%async_computation.2 | async-start | bytes 8388608
  71.9 4.0 %slice-start.1 = ((s8[7340032]{0:T(1024)(128)(4,1)}), s8[3145728]{0:T(1024)(128)(4,1)S(1)}, s32[]{:S(2)}) async-start(s8[7340032]{0:T(1024)(128)(4,1)} %bitcast.30), calls=%async_computation.3 | async-start | bytes 6291456
  80.0 1.8 %copy-start.1 = (bf16[1024,1792]{1,0:T(8,128)(2,1)}, bf16[1024,1792]{1,0:T(8,128)(2,1)S(1)}, u32[]{:S(2)}) copy-start(bf16[1024,1792]{1,0:T(8,128)(2,1)S(1)} %down.1) | copy-start | bytes 11010052
  81.8 9.0 %copy-start.8 = (bf16[1,1536,576]{1,2,0:T(8,128)(2,1)S(1)}, bf16[1,1536,576]{1,2,0:T(8,128)(2,1)}, u32[]{:S(2)}) copy-start(bf16[1,1536,576]{1,2,0:T(8,128)(2,1)} %param.18) | copy-start | bytes 5308420
  81.8 55.5 %all-to-all-start.1 = ((bf16[64,16,1792]{2,1,0:T(8,128)(2,1)}), bf16[64,16,1792]{2,1,0:T(8,128)(2,1)}, u32[]{:S(2)}, u32[]{:S(2)}) async-start(bf16[64,16,1792]{2,1,0:T(8,128)(2,1)} %bitcast.28), calls=%async_computation.1 | async-start | bytes 7340032 | tf_op jit(solution)/shard_map/all_to_all | solution.py:224
  91.4 45.9 %copy-start.4 = (bf16[64,1024]{1,0:T(8,128)(2,1)S(1)}, bf16[64,1024]{1,0:T(8,128)(2,1)}, u32[]{:S(2)}) copy-start(bf16[64,1024]{1,0:T(8,128)(2,1)} %slot_weights.1.weigh_ref) | copy-start | bytes 393220

commit v3 on v0

v3 whole, which is shorter than its diff:
```python
import itertools

import jax
import jax.numpy as jnp
from jax import lax
from jax.experimental import pallas as pl
from jax.experimental.pallas import tpu as pltpu
from jax.sharding import Mesh, PartitionSpec as P

LAT = 512
CAP = 4

AXES = ("zl", "zh", "x", "y", "core")
SIZES = (2, 2, 4, 4, 2)
LINE = 4
STEPS = (0, 1, -1, 2)
META = 128
CHUNK = 512
LIMIT = 5

norm_eps = 1e-06
score_scale = 0.07216878364870322


def moved_along(place, axis, step):
    place = dict(place)
    if axis == "z":
        z = (place["zh"] * 2 + place["zl"] + step) % LINE
        place["zh"], place["zl"] = z // 2, z % 2
    else:
        place[axis] = (place[axis] + step) % LINE
    return place


def index_of(place):
    index = 0
    for axis, size in zip(AXES, SIZES):
        index = index * size + place[axis]
    return index


def shift(rows, axes, step):
    pairs = []
    for values in itertools.product(*[range(size) for size in SIZES]):
        place = dict(zip(AXES, values))
        pairs.append((index_of(place), index_of(moved_along(place, axes[place["core"]], step))))
    return lax.ppermute(rows, AXES, pairs)


def to_other_core(rows):
    return lax.ppermute(rows, "core", [(0, 1), (1, 0)])


def in_vmem(count):
    return [pl.BlockSpec(memory_space=pltpu.VMEM)] * count


def normalize_kernel(hidden_ref, gain_ref, routes_ref, gates_ref, out_ref):
    features = hidden_ref[...].astype(jnp.float32)
    squares = jnp.mean(features * features, axis=-1, keepdims=True)
    normed = features * lax.rsqrt(squares + norm_eps) * gain_ref[...]
    gates = gates_ref[...]
    high = gates.astype(jnp.bfloat16).astype(jnp.float32)
    tok_rows, topk = gates.shape
    rest = jnp.zeros((tok_rows, META - 3 * topk), jnp.float32)
    meta = jnp.concatenate(
        [routes_ref[...].astype(jnp.float32), high, gates - high, rest], axis=1
    )
    width = hidden_ref.shape[1]
    out_ref[:, :width] = normed.astype(jnp.bfloat16)
    out_ref[:, width:] = meta.astype(jnp.bfloat16)


def normalize(hidden, norm_gain, routes, gate_values):
    tok_rows, width = hidden.shape
    return pl.pallas_call(
        normalize_kernel,
        in_specs=in_vmem(4),
        out_specs=in_vmem(1)[0],
        out_shape=jax.ShapeDtypeStruct((tok_rows, width + META), jnp.bfloat16),
        name="normalize",
    )(hidden, norm_gain.reshape(1, -1), routes, gate_values)


def slot_table(meta, experts_ref, tok_rows, topk):
    rows = meta.shape[0]
    slots = rows // tok_rows * CAP
    shape = (rows, LINE * slots)
    row = lax.broadcasted_iota(jnp.int32, shape, 0)
    slot = lax.broadcasted_iota(jnp.int32, shape, 1)
    which = lax.broadcasted_iota(jnp.int32, (1, LINE * slots), 1) // slots
    expert = jnp.zeros(which.shape, jnp.int32)
    for n in range(LINE):
        expert = jnp.where(which == n, experts_ref[n], expert)
    expert = expert.astype(jnp.float32)
    named = jnp.zeros(shape, jnp.float32)
    high = jnp.zeros(shape, jnp.float32)
    low = jnp.zeros(shape, jnp.float32)
    for k in range(topk):
        hit = meta[:, k : k + 1] == expert
        named = jnp.where(hit, 1.0, named)
        high = jnp.where(hit, meta[:, topk + k : topk + k + 1], high)
        low = jnp.where(hit, meta[:, 2 * topk + k : 2 * topk + k + 1], low)
    to = lax.broadcasted_iota(jnp.int32, (rows, rows), 0)
    frm = lax.broadcasted_iota(jnp.int32, (rows, rows), 1)
    before = ((to // tok_rows == frm // tok_rows) & (frm < to)).astype(jnp.float32)
    rank = jnp.dot(
        before.astype(jnp.bfloat16), named.astype(jnp.bfloat16), preferred_element_type=jnp.float32
    )
    place = slot % slots
    fills = (
        (named > 0.5)
        & (row // tok_rows == place // CAP)
        & (rank == (place % CAP).astype(jnp.float32))
    )
    return fills, jnp.where(fills, high, 0.0), jnp.where(fills, low, 0.0)


def select_kernel(tok_rows, topk, experts_ref, *refs):
    pieces, outs = refs[:LINE], refs[LINE:]
    width = outs[0].shape[1]
    slots = outs[0].shape[0]
    meta = jnp.concatenate([p[:, width:] for p in pieces], axis=0).astype(jnp.float32)
    fills, _, _ = slot_table(meta, experts_ref, tok_rows, topk)
    pick = fills.astype(jnp.float32).astype(jnp.bfloat16)
    for start in range(0, width, CHUNK):
        columns = slice(start, start + CHUNK)
        rows = jnp.concatenate([p[:, columns] for p in pieces], axis=0)
        picked = lax.dot_general(
            pick, rows, (((0,), (0,)), ((), ())), preferred_element_type=jnp.float32
        ).astype(jnp.bfloat16)
        for n in range(LINE):
            outs[n][:, columns] = picked[n * slots : (n + 1) * slots]


def select(pieces, experts, tok_rows, topk):
    piece_rows = pieces[0].shape[0]
    width = pieces[0].shape[1] - META
    slots = LINE * piece_rows // tok_rows * CAP
    return pl.pallas_call(
        lambda *refs: select_kernel(tok_rows, topk, *refs),
        in_specs=[pl.BlockSpec(memory_space=pltpu.SMEM)] + in_vmem(LINE),
        out_specs=in_vmem(LINE),
        out_shape=[jax.ShapeDtypeStruct((slots, width), jnp.bfloat16)] * LINE,
        compiler_params=pltpu.CompilerParams(vmem_limit_bytes=8 * 2**20),
        cost_estimate=pl.CostEstimate(
            flops=2 * LINE * slots * LINE * piece_rows * width,
            bytes_accessed=2 * LINE * width * (slots + piece_rows),
            transcendentals=0,
        ),
        name="select_slots",
    )(experts, *pieces)


def weigh_kernel(tok_rows, topk, experts_ref, *refs):
    metas, weigh_ref = refs[:LINE], refs[LINE]
    meta = jnp.concatenate([m[:, -META:] for m in metas], axis=0).astype(jnp.float32)
    _, high, low = slot_table(meta, experts_ref, tok_rows, topk)
    weigh_ref[...] = jnp.concatenate([high, low], axis=0).astype(jnp.bfloat16)


def weigh(pieces, experts, tok_rows, topk):
    piece_rows = pieces[0].shape[0]
    rows = LINE * piece_rows
    slots = rows // tok_rows * CAP
    return pl.pallas_call(
        lambda *refs: weigh_kernel(tok_rows, topk, *refs),
        in_specs=[pl.BlockSpec(memory_space=pltpu.SMEM)] + in_vmem(LINE),
        out_specs=in_vmem(1)[0],
        out_shape=jax.ShapeDtypeStruct((2 * rows, LINE * slots), jnp.bfloat16),
        name="slot_weights",
    )(experts, *pieces)


def load_kernel(count, *refs):
    stored, loaded, arrived = refs[:count], refs[count : 2 * count], refs[2 * count]
    fetches = [
        pltpu.make_async_copy(source, target, arrived.at[n])
        for n, (source, target) in enumerate(zip(stored, loaded))
    ]
    for fetch in fetches:
        fetch.start()
    for fetch in fetches:
        fetch.wait()


def load(weights):
    count = len(weights)
    return pl.pallas_call(
        lambda *refs: load_kernel(count, *refs),
        in_specs=[pl.BlockSpec(memory_space=pltpu.HBM)] * count,
        out_specs=in_vmem(count),
        out_shape=[jax.ShapeDtypeStruct(w.shape, jnp.bfloat16) for w in weights],
        scratch_shapes=[pltpu.SemaphoreType.DMA((count,))],
        compiler_params=pltpu.CompilerParams(vmem_limit_bytes=LIMIT * 2**20),
        cost_estimate=pl.CostEstimate(
            flops=0, bytes_accessed=2 * sum(w.size for w in weights), transcendentals=0
        ),
        name="load_weights",
    )(*weights)


def experts_kernel(count, *refs):
    pieces, refs = refs[:count], refs[count:]
    near, far, outs = refs[:3], refs[3:6], refs[6:]
    rows = jnp.concatenate([piece[...] for piece in pieces], axis=0)
    piece_rows, width = pieces[0].shape

    def activate(gates, ups):
        gate = jnp.dot(rows, gates[...], preferred_element_type=jnp.float32)
        up = jnp.dot(rows, ups[...], preferred_element_type=jnp.float32)
        return (gate / (1.0 + jnp.exp(-gate)) * up).astype(jnp.bfloat16)

    near_act = activate(near[0], near[1])
    far_act = activate(far[0], far[1])
    for start in range(0, width, CHUNK):
        columns = slice(start, start + CHUNK)
        total = (
            jnp.dot(near_act, near[2][:, columns], preferred_element_type=jnp.float32)
            + jnp.dot(far_act, far[2][:, columns], preferred_element_type=jnp.float32)
        ).astype(jnp.bfloat16)
        for n, out in enumerate(outs):
            out[:, columns] = total[n * piece_rows : (n + 1) * piece_rows]


def run_experts(pieces, near, far):
    count = len(pieces)
    piece_rows, width = pieces[0].shape
    size = sum(w.size for w in near) + sum(w.size for w in far)
    return pl.pallas_call(
        lambda *refs: experts_kernel(count, *refs),
        in_specs=in_vmem(count + 6),
        out_specs=in_vmem(count),
        out_shape=[jax.ShapeDtypeStruct((piece_rows, width), jnp.bfloat16)] * count,
        compiler_params=pltpu.CompilerParams(vmem_limit_bytes=LIMIT * 2**20),
        cost_estimate=pl.CostEstimate(
            flops=2 * count * piece_rows * size, bytes_accessed=2 * size, transcendentals=0
        ),
        name="experts",
    )(*pieces, *near, *far)


def spread_kernel(weigh_ref, *refs):
    pieces, outs = refs[:LINE], refs[LINE:]
    count, width = outs[0].shape
    half = weigh_ref.shape[0] // 2
    for start in range(0, width, CHUNK):
        columns = slice(start, start + CHUNK)
        rows = jnp.concatenate([p[:, columns] for p in pieces], axis=0)
        both = jnp.dot(weigh_ref[...], rows, preferred_element_type=jnp.float32)
        total = (both[:half] + both[half:]).astype(jnp.bfloat16)
        for n in range(LINE):
            outs[n][:, columns] = total[n * count : (n + 1) * count]


def spread(weights, pieces):
    slots, width = pieces[0].shape
    rows = weights.shape[0] // 2
    return pl.pallas_call(
        spread_kernel,
        in_specs=in_vmem(1 + LINE),
        out_specs=in_vmem(LINE),
        out_shape=[jax.ShapeDtypeStruct((rows // LINE, width), jnp.bfloat16)] * LINE,
        compiler_params=pltpu.CompilerParams(vmem_limit_bytes=8 * 2**20),
        cost_estimate=pl.CostEstimate(
            flops=2 * 2 * rows * LINE * slots * width,
            bytes_accessed=2 * width * (LINE * slots + rows),
            transcendentals=0,
        ),
        name="spread_slots",
    )(weights, *pieces)


def add_kernel(parts, *refs):
    pieces, outs = refs[:LINE], refs[LINE:]
    total = pieces[0][...].astype(jnp.float32)
    for piece in pieces[1:]:
        total = total + piece[...].astype(jnp.float32)
    count = outs[0].shape[0]
    for n in range(parts):
        outs[n][...] = total[n * count : (n + 1) * count].astype(jnp.bfloat16)


def add(pieces, parts):
    rows, width = pieces[0].shape
    return pl.pallas_call(
        lambda *refs: add_kernel(parts, *refs),
        in_specs=in_vmem(LINE),
        out_specs=in_vmem(parts),
        out_shape=[jax.ShapeDtypeStruct((rows // parts, width), jnp.bfloat16)] * parts,
        compiler_params=pltpu.CompilerParams(vmem_limit_bytes=8 * 2**20),
        cost_estimate=pl.CostEstimate(
            flops=LINE * rows * width,
            bytes_accessed=2 * (LINE + 1) * rows * width,
            transcendentals=0,
        ),
        name="add_pieces",
    )(*pieces)


def attend(queries, latent_cache, lengths):
    scores = (
        jnp.einsum("rhk,rck->rhc", queries, latent_cache, preferred_element_type=jnp.float32)
        * score_scale
    )
    in_range = jnp.arange(latent_cache.shape[1])[None, None, :] < lengths[:, None, None]
    scores = jnp.where(in_range, scores, -jnp.inf)
    row_max = jnp.max(scores, axis=-1, keepdims=True)
    raised = jnp.exp(scores - row_max)
    probs = (raised / jnp.sum(raised, axis=-1, keepdims=True)).astype(jnp.bfloat16)
    attended = jnp.einsum(
        "rhc,rcl->rhl", probs, latent_cache[:, :, :LAT], preferred_element_type=jnp.float32
    )
    return attended.astype(jnp.bfloat16)


FIRST = ("y", "y")
SECOND = ("x", "z")
THIRD = ("z", "x")


def target_experts():
    zl, zh, x, y, core = [lax.axis_index(axis) for axis in AXES]
    z = zh * 2 + zl
    found = []
    for step in STEPS:
        to_z = jnp.where(core == 0, (z + step) % LINE, z)
        to_x = jnp.where(core == 0, x, (x + step) % LINE)
        found.append((((to_z % 2) * 2 + to_z // 2) * 4 + to_x) * 2 + y // 2)
    return jnp.stack(found).astype(jnp.int32)


def gather_line(rows, axes):
    return [rows] + [shift(rows, axes, step) for step in STEPS[1:]]


def hand_out(pieces, axes):
    return [pieces[0]] + [shift(p, axes, step) for p, step in zip(pieces[1:], STEPS[1:])]


def hand_back(piece, axes, step):
    return shift(piece, axes, -step)


def shards(
    hidden, norm_gain, routes, gate_values, w_gate, w_up, w_down, queries, latent_cache, lengths
):
    tok_rows, topk = routes.shape
    experts = target_experts()
    far_gate = to_other_core(w_gate)
    own = normalize(hidden, norm_gain, routes, gate_values)
    line = jnp.concatenate(gather_line(own, FIRST), axis=0)
    line, w_up = lax.optimization_barrier((line, w_up))
    far_up = to_other_core(w_up)
    plane = gather_line(line, SECOND)
    plane, w_gate, w_up, w_down, far_gate = lax.optimization_barrier(
        (plane, w_gate, w_up, w_down, far_gate)
    )
    far_down = to_other_core(w_down)
    slots = hand_out(select(plane, experts, tok_rows, topk), THIRD)
    weights = weigh(plane, experts, tok_rows, topk)
    attn_out = attend(queries, latent_cache, lengths)

    loaded = load((w_gate, w_up, w_down, far_gate, far_up, far_down))
    results = []
    for group in (slots[:2], slots[2:]):
        group, loaded, results = lax.optimization_barrier((group, loaded, results))
        results = results + list(run_experts(group, loaded[:3], loaded[3:]))
    back = [results[0]] + [
        hand_back(piece, THIRD, step) for piece, step in zip(results[1:], STEPS[1:])
    ]
    dense = spread(weights, back)
    dense = [dense[0]] + [
        hand_back(piece, SECOND, step) for piece, step in zip(dense[1:], STEPS[1:])
    ]
    sums = add(dense, LINE)
    sums = [sums[0]] + [hand_back(piece, FIRST, step) for piece, step in zip(sums[1:], STEPS[1:])]
    (moe_out,) = add(sums, 1)
    return (moe_out, attn_out)


def solution(mesh):
    fine = Mesh(mesh.devices.reshape(SIZES), AXES)
    placed = (
        P(AXES, None),
        P(),
        P(AXES, None),
        P(AXES, None),
        P(None, AXES),
        P(None, AXES),
        P(AXES, None),
        P(AXES, None, None),
        P(AXES, None, None),
        P(AXES),
    )
    return jax.shard_map(
        shards,
        mesh=fine,
        in_specs=placed,
        out_specs=(P(AXES, None), P(AXES, None, None)),
        check_vma=False,
    )
```

time: 295 us -> 127 us (0.43)
  the two profiles are of different devices: /device:TPU:42 before, /device:TPU:4 now
where the time goes in v3:
time: 127 us; the launch traced here: 125 us
  waiting for transfers between devices  50.9 us (40%)
  Pallas kernels  37.5 us (30%)
  starting transfers between devices  29.8 us (23%)
  matrix products  3.38 us (3%)
  between operations  1.42 us (1%)
  other arithmetic  1.28 us (1%)
    ppermute x18, waiting for transfers between devices, shift(): return lax.ppermute(rows, AXES, pairs)  45.6 us
    ppermute x18, starting transfers between devices, shift(): return lax.ppermute(rows, AXES, pairs)  26.6 us
    pallas_call x2, Pallas kernels, run_experts(): pl.pallas_call(lambda *refs: experts_kernel(count, *refs), in_specs=in_vm...  14.2 us
    pallas_call x1, Pallas kernels, load(): pl.pallas_call(lambda *refs: load_kernel(count, *refs), in_specs=[pl.Bloc...  13.6 us
    ppermute x3, waiting for transfers between devices, to_other_core(): return lax.ppermute(rows, 'core', [(0, 1), (1, 0)])  5.29 us
    ppermute x3, starting transfers between devices, to_other_core(): return lax.ppermute(rows, 'core', [(0, 1), (1, 0)])  3.15 us
    pallas_call x1, Pallas kernels, weigh(): pl.pallas_call(lambda *refs: weigh_kernel(tok_rows, topk, *refs), in_spec...  2.63 us
  transfers between devices with their start and end apart: 21, of which 14 were waited for; matrix products, arithmetic and copies ran while one was open for 4% of the time, Pallas kernels for 22%

profile of v3, /device:TPU:4, one launch (start us, length us, event | category | flops | bytes accessed | tf_op | source)
XLA Modules:
  0.0 125.2 jit_solution(733958831621458509)
XLA Ops:
  0.7 1.7 %normalize.1 = bf16[8,7296]{1,0:T(8,128)(2,1)} custom-call(bf16[8,7168]{1,0:T(8,128)(2,1)} %hidden_ref.1, f32[1,7168]{1,0:T(1,128)} %bitcast.26, s32[8,8]{1,0:T(8,128)} %routes_ref.1, f32[8,8]{1,0:T(8,128)} %gates_ref.1), custom_call_target="tpu_custom_call" | custom-call | tf_op jit(solution)/shard_map/normalize/pallas_call | solution.py:76
  2.5 1.6 %collective-permute-start = (bf16[8,7296]{1,0:T(8,128)(2,1)}, bf16[8,7296]{1,0:T(8,128)(2,1)S(1)}, u32[]{:S(2)}, u32[]{:S(2)}) collective-permute-start(bf16[8,7296]{1,0:T(8,128)(2,1)} %normalize.1), channel_id=1, source_target_pairs={{0,2},{1,3},{2,4},{3,5},{4,6},{5,7},{6,0},{7,1},{8,10},{9,11},{10,... | collective-permute-start | bytes 350216 | tf_op jit(solution)/shard_map/ppermute | solution.py:47
  4.1 1.7 %collective-permute-start.1 = (bf16[8,7296]{1,0:T(8,128)(2,1)}, bf16[8,7296]{1,0:T(8,128)(2,1)S(1)}, u32[]{:S(2)}, u32[]{:S(2)}) collective-permute-start(bf16[8,7296]{1,0:T(8,128)(2,1)} %normalize.1), channel_id=1, source_target_pairs={{0,6},{1,7},{2,0},{3,1},{4,2},{5,3},{6,4},{7,5},{8,14},{9,15},{10,... | collective-permute-start | bytes 350216 | tf_op jit(solution)/shard_map/ppermute | solution.py:47
  5.7 2.0 %collective-permute-start.2 = (bf16[8,7296]{1,0:T(8,128)(2,1)}, bf16[8,7296]{1,0:T(8,128)(2,1)S(1)}, u32[]{:S(2)}, u32[]{:S(2)}) collective-permute-start(bf16[8,7296]{1,0:T(8,128)(2,1)} %normalize.1), channel_id=1, source_target_pairs={{0,4},{1,5},{2,6},{3,7},{4,0},{5,1},{6,2},{7,3},{8,12},{9,13},{10,... | collective-permute-start | bytes 350216 | tf_op jit(solution)/shard_map/ppermute | solution.py:47
  7.7 1.8 %collective-permute-done = bf16[8,7296]{1,0:T(8,128)(2,1)S(1)} collective-permute-done((bf16[8,7296]{1,0:T(8,128)(2,1)}, bf16[8,7296]{1,0:T(8,128)(2,1)S(1)}, u32[]{:S(2)}, u32[]{:S(2)}) %collective-permute-start) | collective-permute-done | bytes 116768 | tf_op jit(solution)/shard_map/ppermute | solution.py:47
  9.6 0.5 collective-permute-done.1
  10.0 3.2 %collective-permute-done.2 = bf16[8,7296]{1,0:T(8,128)(2,1)S(1)} collective-permute-done((bf16[8,7296]{1,0:T(8,128)(2,1)}, bf16[8,7296]{1,0:T(8,128)(2,1)S(1)}, u32[]{:S(2)}, u32[]{:S(2)}) %collective-permute-start.2) | collective-permute-done | bytes 116768 | tf_op jit(solution)/shard_map/ppermute | solution.py:47
  13.2 0.9 pad_maximum_fusion.refs_1_
  14.2 1.3 %collective-permute-start.3 = (bf16[32,7296]{1,0:T(8,128)(2,1)S(1)}, bf16[32,7296]{1,0:T(8,128)(2,1)S(1)}, u32[]{:S(2)}, u32[]{:S(2)}) collective-permute-start(bf16[32,7296]{1,0:T(8,128)(2,1)S(1)} %pad_maximum_fusion.refs_1_), channel_id=1, source_target_pairs={{0,8},{1,65},{2,10},{3,67},{4,12},{5,69},{6,14},{7,71},{8,16},{9,7... | collective-permute-start | bytes 1400840 | tf_op jit(solution)/shard_map/ppermute | solution.py:47
  15.4 0.8 collective-permute-start.4
  16.3 1.7 %collective-permute-start.5 = (bf16[32,7296]{1,0:T(8,128)(2,1)S(1)}, bf16[32,7296]{1,0:T(8,128)(2,1)S(1)}, u32[]{:S(2)}, u32[]{:S(2)}) collective-permute-start(bf16[32,7296]{1,0:T(8,128)(2,1)S(1)} %pad_maximum_fusion.refs_1_), channel_id=1, source_target_pairs={{0,16},{1,33},{2,18},{3,35},{4,20},{5,37},{6,22},{7,39},{8,24},{9,... | collective-permute-start | bytes 1400840 | tf_op jit(solution)/shard_map/ppermute | solution.py:47
  18.0 1.0 collective-permute-start.10
  19.0 3.8 %collective-permute-done.3.refs_2_ = bf16[32,7296]{1,0:T(8,128)(2,1)S(1)} collective-permute-done((bf16[32,7296]{1,0:T(8,128)(2,1)S(1)}, bf16[32,7296]{1,0:T(8,128)(2,1)S(1)}, u32[]{:S(2)}, u32[]{:S(2)}) %collective-permute-start.3) | collective-permute-done | bytes 466976 | tf_op jit(solution)/shard_map/ppermute | solution.py:47
  22.8 1.2 collective-permute-done.4.refs_3_
  24.0 3.8 %collective-permute-done.5.refs_4_ = bf16[32,7296]{1,0:T(8,128)(2,1)S(1)} collective-permute-done((bf16[32,7296]{1,0:T(8,128)(2,1)S(1)}, bf16[32,7296]{1,0:T(8,128)(2,1)S(1)}, u32[]{:S(2)}, u32[]{:S(2)}) %collective-permute-start.5) | collective-permute-done | bytes 466976 | tf_op jit(solution)/shard_map/ppermute | solution.py:47
  27.8 2.0 %collective-permute-start.11 = (bf16[512,7168]{1,0:T(8,128)(2,1)}, bf16[512,7168]{1,0:T(8,128)(2,1)}, u32[]{:S(2)}, u32[]{:S(2)}) collective-permute-start(bf16[512,7168]{1,0:T(8,128)(2,1)} %refs_2_), channel_id=1, source_target_pairs={{0,1},{1,0},{2,3},{3,2},{4,5},{5,4},{6,7},{7,6},{8,9},{9,8},{10,11... | collective-permute-start | bytes 22020104 | tf_op jit(solution)/shard_map/ppermute | solution.py:51
  29.9 2.0 %select_slots.1 = (bf16[64,7168]{1,0:T(8,128)(2,1)S(1)}, bf16[64,7168]{1,0:T(8,128)(2,1)S(1)}, bf16[64,7168]{1,0:T(8,128)(2,1)S(1)}, bf16[64,7168]{1,0:T(8,128)(2,1)S(1)}) custom-call(s32[4]{0:T(128)S(1)} %pad_add_fusion.refs_0_, bf16[32,7296]{1,0:T(8,128)(2,1)S(1)} %pad_maximum_fusion.refs_1_, bf16[32,7296]{1,0:T(8,128)(2,1)S(1)} %collective-permute-done.3.refs_2_, ...), custom_call_target="tpu_custom_call" | custom-call | flops 469762048 | bytes 5505024 | tf_op jit(solution)/shard_map/select_slots/pallas_call | solution.py:140
  32.0 1.2 collective-permute-start.9
  33.2 2.1 %collective-permute-start.7 = (bf16[64,7168]{1,0:T(8,128)(2,1)S(1)}, bf16[64,7168]{1,0:T(8,128)(2,1)S(1)}, u32[]{:S(2)}, u32[]{:S(2)}) collective-permute-start(bf16[64,7168]{1,0:T(8,128)(2,1)S(1)} %get-tuple-element.58), channel_id=1, source_target_pairs={{0,96},{1,25},{2,98},{3,27},{4,100},{5,29},{6,102},{7,31},{8,104},... | collective-permute-start | bytes 2752520 | tf_op jit(solution)/shard_map/ppermute | solution.py:47
  35.3 0.9 collective-permute-start.8
  36.2 5.3 %collective-permute-done.11.refs_5_ = bf16[512,7168]{1,0:T(8,128)(2,1)} collective-permute-done((bf16[512,7168]{1,0:T(8,128)(2,1)}, bf16[512,7168]{1,0:T(8,128)(2,1)}, u32[]{:S(2)}, u32[]{:S(2)}) %collective-permute-start.11) | collective-permute-done | bytes 7340064 | tf_op jit(solution)/shard_map/ppermute | solution.py:51
  41.5 13.6 %load_weights.1 = (bf16[7168,512]{1,0:T(8,128)(2,1)S(1)}, bf16[7168,512]{1,0:T(8,128)(2,1)S(1)}, bf16[512,7168]{1,0:T(8,128)(2,1)S(1)}, bf16[7168,512]{1,0:T(8,1...) custom-call(bf16[7168,512]{1,0:T(8,128)(2,1)} %refs_0_, bf16[7168,512]{1,0:T(8,128)(2,1)} %refs_1_, ...), custom_call_target="tpu_custom_call" | custom-call | bytes 44040192 | tf_op jit(solution)/shard_map/load_weights/pallas_call | solution.py:189
  55.1 7.0 %experts.2 = (bf16[64,7168]{1,0:T(8,128)(2,1)S(1)}, bf16[64,7168]{1,0:T(8,128)(2,1)}) custom-call(bf16[64,7168]{1,0:T(8,128)(2,1)S(1)} %get-tuple-element.78.refs_0_, bf16[64,7168]{1,0:T(8,128)(2,1)S(1)} %collective-permute-done.9.refs_1_, bf16[7168,512]{1,0:T(8,128)(2,1)S(1)} %get-tuple-element.86.refs_2_, bf16[7168,512]{1,0:T(8,128)(2,1)S(1)} %get-tuple-element.87.refs_3_, ...), custom_call_target="tpu_custom_call" | custom-call | flops 5637144576 | bytes 44040192 | tf_op jit(solution)/shard_map/experts/pallas_call | solution.py:230
  62.1 7.2 %experts.3 = (bf16[64,7168]{1,0:T(8,128)(2,1)}, bf16[64,7168]{1,0:T(8,128)(2,1)}) custom-call(bf16[64,7168]{1,0:T(8,128)(2,1)S(1)} %collective-permute-done.7.refs_0_, bf16[64,7168]{1,0:T(8,128)(2,1)S(1)} %collective-permute-done.8.refs_1_, bf16[7168,512]{1,0:T(8,128)(2,1)S(1)} %get-tuple-element.86.refs_2_, ...), custom_call_target="tpu_custom_call" | custom-call | flops 5637144576 | bytes 44040192 | tf_op jit(solution)/shard_map/experts/pallas_call | solution.py:230
  69.3 1.1 collective-permute-start.13
  70.5 3.4 %collective-permute-start.14 = (bf16[64,7168]{1,0:T(8,128)(2,1)}, bf16[64,7168]{1,0:T(8,128)(2,1)S(1)}, u32[]{:S(2)}, u32[]{:S(2)}) collective-permute-start(bf16[64,7168]{1,0:T(8,128)(2,1)} %get-tuple-element.93), channel_id=1, source_target_pairs={{0,32},{1,17},{2,34},{3,19},{4,36},{5,21},{6,38},{7,23},{8,40},{9,... | collective-permute-start | bytes 2752520 | tf_op jit(solution)/shard_map/ppermute | solution.py:47
  73.8 1.0 collective-permute-start.12
  75.5 2.6 %slot_weights.1.weigh_ref = bf16[256,256]{1,0:T(8,128)(2,1)} custom-call(s32[4]{0:T(128)} %copy-done.6, bf16[32,7296]{1,0:T(8,128)(2,1)} %copy-done.1, bf16[32,7296]{1,0:T(8,128)(2,1)} %copy-done.2, bf16[32,7296]{1,0:T(8,128)(2,1)} %copy-done.3, bf16[32,7296]{1,0:T(8,128)(2,1)} %copy-done.4), custom_call_target="tpu_custom_call" | custom-call | tf_op jit(solution)/shard_map/slot_weights/pallas_call | solution.py:166
  78.1 6.0 %collective-permute-done.13.refs_2_ = bf16[64,7168]{1,0:T(8,128)(2,1)S(1)} collective-permute-done((bf16[64,7168]{1,0:T(8,128)(2,1)}, bf16[64,7168]{1,0:T(8,128)(2,1)S(1)}, u32[]{:S(2)}, u32[]{:S(2)}) %collective-permute-start.13) | collective-permute-done | bytes 917536 | tf_op jit(solution)/shard_map/ppermute | solution.py:47
  84.1 11.1 %collective-permute-done.14.refs_3_ = bf16[64,7168]{1,0:T(8,128)(2,1)S(1)} collective-permute-done((bf16[64,7168]{1,0:T(8,128)(2,1)}, bf16[64,7168]{1,0:T(8,128)(2,1)S(1)}, u32[]{:S(2)}, u32[]{:S(2)}) %collective-permute-start.14) | collective-permute-done | bytes 917536 | tf_op jit(solution)/shard_map/ppermute | solution.py:47
  95.2 0.9 copy-done.5
  96.1 2.4 %spread_slots.1 = (bf16[32,7168]{1,0:T(8,128)(2,1)S(1)}, bf16[32,7168]{1,0:T(8,128)(2,1)S(1)}, bf16[32,7168]{1,0:T(8,128)(2,1)S(1)}, bf16[32,7168]{1,0:T(8,128)(2,1)S(1)}) custom-call(bf16[256,256]{1,0:T(8,128)(2,1)S(1)} %copy-done.5, bf16[64,7168]{1,0:T(8,128)(2,1)S(1)} %get-tuple-element.82.refs_0_, bf16[64,7168]{1,0:T(8,128)(2,1)} %collective-permute-done.12.refs_1_, ...), custom_call_target="tpu_custom_call" | custom-call | flops 939524096 | bytes 5505024 | tf_op jit(solution)/shard_map/spread_slots/pallas_call | solution.py:259
  98.6 2.1 %collective-permute-start.15 = (bf16[32,7168]{1,0:T(8,128)(2,1)S(1)}, bf16[32,7168]{1,0:T(8,128)(2,1)S(1)}, u32[]{:S(2)}, u32[]{:S(2)}) collective-permute-start(bf16[32,7168]{1,0:T(8,128)(2,1)S(1)} %get-tuple-element.95), channel_id=1, source_target_pairs={{0,24},{1,97},{2,26},{3,99},{4,28},{5,101},{6,30},{7,103},{8,0},{9... | collective-permute-start | bytes 1376264 | tf_op jit(solution)/shard_map/ppermute | solution.py:47
  100.6 0.4 collective-permute-start.16
  101.0 2.0 %collective-permute-start.17 = (bf16[32,7168]{1,0:T(8,128)(2,1)S(1)}, bf16[32,7168]{1,0:T(8,128)(2,1)S(1)}, u32[]{:S(2)}, u32[]{:S(2)}) collective-permute-start(bf16[32,7168]{1,0:T(8,128)(2,1)S(1)} %get-tuple-element.97), channel_id=1, source_target_pairs={{0,16},{1,33},{2,18},{3,35},{4,20},{5,37},{6,22},{7,39},{8,24},{9,... | collective-permute-start | bytes 1376264 | tf_op jit(solution)/shard_map/ppermute | solution.py:47
  103.0 2.1 %fusion.15 = (f32[128]{0:T(128)S(1)}, f32[128,1536]{1,0:T(8,128)S(1)}) fusion(bf16[1,1536,576]{1,2,0:T(8,128)(2,1)} %param.18, bf16[1,128,576]{1,2,0:T(8,128)(2,1)S(1)} %copy-done, pred[1536]{0:T(1024)(128)(4,1)S(1)} %iota_compare_fusion), kind=kOutput, calls=%fused_computation.17 | convolution fusion | flops 227082112 | bytes 2705408 | tf_op jit(solution)/shard_map/rhk,rck->rhc/dot_general | solution.py:303
  105.1 0.3 fusion.11
  105.4 2.0 %collective-permute-done.15.refs_1_ = bf16[32,7168]{1,0:T(8,128)(2,1)S(1)} collective-permute-done((bf16[32,7168]{1,0:T(8,128)(2,1)S(1)}, bf16[32,7168]{1,0:T(8,128)(2,1)S(1)}, u32[]{:S(2)}, u32[]{:S(2)}) %collective-permute-start.15) | collective-permute-done | bytes 458784 | tf_op jit(solution)/shard_map/ppermute | solution.py:47
  107.4 1.7 %collective-permute-done.16.refs_2_ = bf16[32,7168]{1,0:T(8,128)(2,1)S(1)} collective-permute-done((bf16[32,7168]{1,0:T(8,128)(2,1)S(1)}, bf16[32,7168]{1,0:T(8,128)(2,1)S(1)}, u32[]{:S(2)}, u32[]{:S(2)}) %collective-permute-start.16) | collective-permute-done | bytes 458784 | tf_op jit(solution)/shard_map/ppermute | solution.py:47
  109.1 5.3 %collective-permute-done.17.refs_3_ = bf16[32,7168]{1,0:T(8,128)(2,1)S(1)} collective-permute-done((bf16[32,7168]{1,0:T(8,128)(2,1)S(1)}, bf16[32,7168]{1,0:T(8,128)(2,1)S(1)}, u32[]{:S(2)}, u32[]{:S(2)}) %collective-permute-start.17) | collective-permute-done | bytes 458784 | tf_op jit(solution)/shard_map/ppermute | solution.py:47
  114.4 0.2 add_pieces.2
  114.6 1.8 %collective-permute-start.18 = (bf16[8,7168]{1,0:T(8,128)(2,1)S(1)}, bf16[8,7168]{1,0:T(8,128)(2,1)S(1)}, u32[]{:S(2)}, u32[]{:S(2)}) collective-permute-start(bf16[8,7168]{1,0:T(8,128)(2,1)S(1)} %get-tuple-element.99), channel_id=1, source_target_pairs={{0,6},{1,7},{2,0},{3,1},{4,2},{5,3},{6,4},{7,5},{8,14},{9,15},{10,... | collective-permute-start | bytes 344072 | tf_op jit(solution)/shard_map/ppermute | solution.py:47
  116.5 0.2 collective-permute-start.19
  116.7 1.3 %collective-permute-start.20 = (bf16[8,7168]{1,0:T(8,128)(2,1)S(1)}, bf16[8,7168]{1,0:T(8,128)(2,1)S(1)}, u32[]{:S(2)}, u32[]{:S(2)}) collective-permute-start(bf16[8,7168]{1,0:T(8,128)(2,1)S(1)} %get-tuple-element.101), channel_id=1, source_target_pairs={{0,4},{1,5},{2,6},{3,7},{4,0},{5,1},{6,2},{7,3},{8,12},{9,13},{10,... | collective-permute-start | bytes 344072 | tf_op jit(solution)/shard_map/ppermute | solution.py:47
  118.0 1.3 %fusion.8 = bf16[1,128,512]{2,1,0:T(8,128)(2,1)} fusion(bf16[1,1536,576]{1,2,0:T(8,128)(2,1)S(1)} %copy-done.7, f32[128,1536]{1,0:T(8,128)S(1)} %get-tuple-element.103, f32[128]{0:T(128)S(1)} %fusion.11, f32[128]{0:T(128)S(1)} %get-tuple-element.102), kind=kOutput, calls=%fused_computation.7 | convolution fusion | flops 201981952 | bytes 2491392 | tf_op jit(solution)/shard_map/rhc,rcl->rhl/dot_general | solution.py:311
  119.3 0.1 collective-permute-done.18.refs_1_
  119.5 5.0 %collective-permute-done.19.refs_2_ = bf16[8,7168]{1,0:T(8,128)(2,1)S(1)} collective-permute-done((bf16[8,7168]{1,0:T(8,128)(2,1)S(1)}, bf16[8,7168]{1,0:T(8,128)(2,1)S(1)}, u32[]{:S(2)}, u32[]{:S(2)}) %collective-permute-start.19) | collective-permute-done | bytes 114720 | tf_op jit(solution)/shard_map/ppermute | solution.py:47
  124.5 0.7 add_pieces.3
  (25 shorter events, 0.2 us)
Async XLA Ops:
  0.6 102.4 %copy-start = (bf16[1,128,576]{1,2,0:T(8,128)(2,1)S(1)}, bf16[1,128,576]{1,2,0:T(8,128)(2,1)}, u32[]{:S(2)}) copy-start(bf16[1,128,576]{1,2,0:T(8,128)(2,1)} %param.17) | copy-start | bytes 442372
  0.6 27.2 %collective-permute-start.6 = (bf16[7168,512]{1,0:T(8,128)(2,1)}, bf16[7168,512]{1,0:T(8,128)(2,1)}, u32[]{:S(2)}, u32[]{:S(2)}) collective-permute-start(bf16[7168,512]{1,0:T(8,128)(2,1)} %refs_0_), channel_id=1, source_target_pairs={{0,1},{1,0},{2,3},{3,2},{4,5},{5,4},{6,7},{7,6},{8,9},{9,8},{10,11... | collective-permute-start | bytes 22020104 | tf_op jit(solution)/shard_map/ppermute | solution.py:51
  2.5 7.1 %collective-permute-start = (bf16[8,7296]{1,0:T(8,128)(2,1)}, bf16[8,7296]{1,0:T(8,128)(2,1)S(1)}, u32[]{:S(2)}, u32[]{:S(2)}) collective-permute-start(bf16[8,7296]{1,0:T(8,128)(2,1)} %normalize.1), channel_id=1, source_target_pairs={{0,2},{1,3},{2,4},{3,5},{4,6},{5,7},{6,0},{7,1},{8,10},{9,11},{10,... | collective-permute-start | bytes 350216 | tf_op jit(solution)/shard_map/ppermute | solution.py:47
  4.1 6.0 %collective-permute-start.1 = (bf16[8,7296]{1,0:T(8,128)(2,1)}, bf16[8,7296]{1,0:T(8,128)(2,1)S(1)}, u32[]{:S(2)}, u32[]{:S(2)}) collective-permute-start(bf16[8,7296]{1,0:T(8,128)(2,1)} %normalize.1), channel_id=1, source_target_pairs={{0,6},{1,7},{2,0},{3,1},{4,2},{5,3},{6,4},{7,5},{8,14},{9,15},{10,... | collective-permute-start | bytes 350216 | tf_op jit(solution)/shard_map/ppermute | solution.py:47
  5.7 7.5 %collective-permute-start.2 = (bf16[8,7296]{1,0:T(8,128)(2,1)}, bf16[8,7296]{1,0:T(8,128)(2,1)S(1)}, u32[]{:S(2)}, u32[]{:S(2)}) collective-permute-start(bf16[8,7296]{1,0:T(8,128)(2,1)} %normalize.1), channel_id=1, source_target_pairs={{0,4},{1,5},{2,6},{3,7},{4,0},{5,1},{6,2},{7,3},{8,12},{9,13},{10,... | collective-permute-start | bytes 350216 | tf_op jit(solution)/shard_map/ppermute | solution.py:47
  14.2 40.9 %copy-start.1 = (bf16[32,7296]{1,0:T(8,128)(2,1)}, bf16[32,7296]{1,0:T(8,128)(2,1)S(1)}, u32[]{:S(2)}) copy-start(bf16[32,7296]{1,0:T(8,128)(2,1)S(1)} %pad_maximum_fusion.refs_1_) | copy-start | bytes 1400836
  14.2 8.6 %collective-permute-start.3 = (bf16[32,7296]{1,0:T(8,128)(2,1)S(1)}, bf16[32,7296]{1,0:T(8,128)(2,1)S(1)}, u32[]{:S(2)}, u32[]{:S(2)}) collective-permute-start(bf16[32,7296]{1,0:T(8,128)(2,1)S(1)} %pad_maximum_fusion.refs_1_), channel_id=1, source_target_pairs={{0,8},{1,65},{2,10},{3,67},{4,12},{5,69},{6,14},{7,71},{8,16},{9,7... | collective-permute-start | bytes 1400840 | tf_op jit(solution)/shard_map/ppermute | solution.py:47
  15.4 8.6 %collective-permute-start.4 = (bf16[32,7296]{1,0:T(8,128)(2,1)S(1)}, bf16[32,7296]{1,0:T(8,128)(2,1)S(1)}, u32[]{:S(2)}, u32[]{:S(2)}) collective-permute-start(bf16[32,7296]{1,0:T(8,128)(2,1)S(1)} %pad_maximum_fusion.refs_1_), channel_id=1, source_target_pairs={{0,24},{1,97},{2,26},{3,99},{4,28},{5,101},{6,30},{7,103},{8,0},{9... | collective-permute-start | bytes 1400840 | tf_op jit(solution)/shard_map/ppermute | solution.py:47
  16.3 11.5 %collective-permute-start.5 = (bf16[32,7296]{1,0:T(8,128)(2,1)S(1)}, bf16[32,7296]{1,0:T(8,128)(2,1)S(1)}, u32[]{:S(2)}, u32[]{:S(2)}) collective-permute-start(bf16[32,7296]{1,0:T(8,128)(2,1)S(1)} %pad_maximum_fusion.refs_1_), channel_id=1, source_target_pairs={{0,16},{1,33},{2,18},{3,35},{4,20},{5,37},{6,22},{7,39},{8,24},{9,... | collective-permute-start | bytes 1400840 | tf_op jit(solution)/shard_map/ppermute | solution.py:47
  18.0 18.2 %collective-permute-start.10 = (bf16[7168,512]{1,0:T(8,128)(2,1)}, bf16[7168,512]{1,0:T(8,128)(2,1)}, u32[]{:S(2)}, u32[]{:S(2)}) collective-permute-start(bf16[7168,512]{1,0:T(8,128)(2,1)} %refs_1_), channel_id=1, source_target_pairs={{0,1},{1,0},{2,3},{3,2},{4,5},{5,4},{6,7},{7,6},{8,9},{9,8},{10,11... | collective-permute-start | bytes 22020104 | tf_op jit(solution)/shard_map/ppermute | solution.py:51
  22.8 32.3 %copy-start.2 = (bf16[32,7296]{1,0:T(8,128)(2,1)}, bf16[32,7296]{1,0:T(8,128)(2,1)S(1)}, u32[]{:S(2)}) copy-start(bf16[32,7296]{1,0:T(8,128)(2,1)S(1)} %collective-permute-done.3.refs_2_) | copy-start | bytes 1400836
  24.0 31.1 %copy-start.3 = (bf16[32,7296]{1,0:T(8,128)(2,1)}, bf16[32,7296]{1,0:T(8,128)(2,1)S(1)}, u32[]{:S(2)}) copy-start(bf16[32,7296]{1,0:T(8,128)(2,1)S(1)} %collective-permute-done.4.refs_3_) | copy-start | bytes 1400836
  27.8 27.3 %copy-start.4 = (bf16[32,7296]{1,0:T(8,128)(2,1)}, bf16[32,7296]{1,0:T(8,128)(2,1)S(1)}, u32[]{:S(2)}) copy-start(bf16[32,7296]{1,0:T(8,128)(2,1)S(1)} %collective-permute-done.5.refs_4_) | copy-start | bytes 1400836
  27.8 13.7 %collective-permute-start.11 = (bf16[512,7168]{1,0:T(8,128)(2,1)}, bf16[512,7168]{1,0:T(8,128)(2,1)}, u32[]{:S(2)}, u32[]{:S(2)}) collective-permute-start(bf16[512,7168]{1,0:T(8,128)(2,1)} %refs_2_), channel_id=1, source_target_pairs={{0,1},{1,0},{2,3},{3,2},{4,5},{5,4},{6,7},{7,6},{8,9},{9,8},{10,11... | collective-permute-start | bytes 22020104 | tf_op jit(solution)/shard_map/ppermute | solution.py:51
  29.9 25.2 %copy-start.6 = (s32[4]{0:T(128)}, s32[4]{0:T(128)S(1)}, u32[]{:S(2)}) copy-start(s32[4]{0:T(128)S(1)} %pad_add_fusion.refs_0_) | copy-start | bytes 52
  32.0 23.2 %collective-permute-start.9 = (bf16[64,7168]{1,0:T(8,128)(2,1)S(1)}, bf16[64,7168]{1,0:T(8,128)(2,1)S(1)}, u32[]{:S(2)}, u32[]{:S(2)}) collective-permute-start(bf16[64,7168]{1,0:T(8,128)(2,1)S(1)} %get-tuple-element.61), channel_id=1, source_target_pairs={{0,64},{1,9},{2,66},{3,11},{4,68},{5,13},{6,70},{7,15},{8,72},{9,1... | collective-permute-start | bytes 2752520 | tf_op jit(solution)/shard_map/ppermute | solution.py:47
  33.2 28.9 %collective-permute-start.7 = (bf16[64,7168]{1,0:T(8,128)(2,1)S(1)}, bf16[64,7168]{1,0:T(8,128)(2,1)S(1)}, u32[]{:S(2)}, u32[]{:S(2)}) collective-permute-start(bf16[64,7168]{1,0:T(8,128)(2,1)S(1)} %get-tuple-element.58), channel_id=1, source_target_pairs={{0,96},{1,25},{2,98},{3,27},{4,100},{5,29},{6,102},{7,31},{8,104},... | collective-permute-start | bytes 2752520 | tf_op jit(solution)/shard_map/ppermute | solution.py:47
  35.3 26.8 %collective-permute-start.8 = (bf16[64,7168]{1,0:T(8,128)(2,1)S(1)}, bf16[64,7168]{1,0:T(8,128)(2,1)S(1)}, u32[]{:S(2)}, u32[]{:S(2)}) collective-permute-start(bf16[64,7168]{1,0:T(8,128)(2,1)S(1)} %get-tuple-element.59), channel_id=1, source_target_pairs={{0,32},{1,17},{2,34},{3,19},{4,36},{5,21},{6,38},{7,23},{8,40},{9,... | collective-permute-start | bytes 2752520 | tf_op jit(solution)/shard_map/ppermute | solution.py:47
  69.3 14.8 %collective-permute-start.13 = (bf16[64,7168]{1,0:T(8,128)(2,1)}, bf16[64,7168]{1,0:T(8,128)(2,1)S(1)}, u32[]{:S(2)}, u32[]{:S(2)}) collective-permute-start(bf16[64,7168]{1,0:T(8,128)(2,1)} %get-tuple-element.92), channel_id=1, source_target_pairs={{0,64},{1,9},{2,66},{3,11},{4,68},{5,13},{6,70},{7,15},{8,72},{9,1... | collective-permute-start | bytes 2752520 | tf_op jit(solution)/shard_map/ppermute | solution.py:47
  70.5 24.8 %collective-permute-start.14 = (bf16[64,7168]{1,0:T(8,128)(2,1)}, bf16[64,7168]{1,0:T(8,128)(2,1)S(1)}, u32[]{:S(2)}, u32[]{:S(2)}) collective-permute-start(bf16[64,7168]{1,0:T(8,128)(2,1)} %get-tuple-element.93), channel_id=1, source_target_pairs={{0,32},{1,17},{2,34},{3,19},{4,36},{5,21},{6,38},{7,23},{8,40},{9,... | collective-permute-start | bytes 2752520 | tf_op jit(solution)/shard_map/ppermute | solution.py:47
  73.8 21.4 %collective-permute-start.12 = (bf16[64,7168]{1,0:T(8,128)(2,1)}, bf16[64,7168]{1,0:T(8,128)(2,1)}, u32[]{:S(2)}, u32[]{:S(2)}) collective-permute-start(bf16[64,7168]{1,0:T(8,128)(2,1)} %get-tuple-element.83), channel_id=1, source_target_pairs={{0,96},{1,25},{2,98},{3,27},{4,100},{5,29},{6,102},{7,31},{8,104},... | collective-permute-start | bytes 2752520 | tf_op jit(solution)/shard_map/ppermute | solution.py:47
  95.2 0.9 copy-start.5
  96.1 21.9 %copy-start.7 = (bf16[1,1536,576]{1,2,0:T(8,128)(2,1)S(1)}, bf16[1,1536,576]{1,2,0:T(8,128)(2,1)}, u32[]{:S(2)}) copy-start(bf16[1,1536,576]{1,2,0:T(8,128)(2,1)} %param.18) | copy-start | bytes 5308420
  98.6 8.8 %collective-permute-start.15 = (bf16[32,7168]{1,0:T(8,128)(2,1)S(1)}, bf16[32,7168]{1,0:T(8,128)(2,1)S(1)}, u32[]{:S(2)}, u32[]{:S(2)}) collective-permute-start(bf16[32,7168]{1,0:T(8,128)(2,1)S(1)} %get-tuple-element.95), channel_id=1, source_target_pairs={{0,24},{1,97},{2,26},{3,99},{4,28},{5,101},{6,30},{7,103},{8,0},{9... | collective-permute-start | bytes 1376264 | tf_op jit(solution)/shard_map/ppermute | solution.py:47
  100.6 8.5 %collective-permute-start.16 = (bf16[32,7168]{1,0:T(8,128)(2,1)S(1)}, bf16[32,7168]{1,0:T(8,128)(2,1)S(1)}, u32[]{:S(2)}, u32[]{:S(2)}) collective-permute-start(bf16[32,7168]{1,0:T(8,128)(2,1)S(1)} %get-tuple-element.96), channel_id=1, source_target_pairs={{0,8},{1,65},{2,10},{3,67},{4,12},{5,69},{6,14},{7,71},{8,16},{9,7... | collective-permute-start | bytes 1376264 | tf_op jit(solution)/shard_map/ppermute | solution.py:47
  101.0 13.4 %collective-permute-start.17 = (bf16[32,7168]{1,0:T(8,128)(2,1)S(1)}, bf16[32,7168]{1,0:T(8,128)(2,1)S(1)}, u32[]{:S(2)}, u32[]{:S(2)}) collective-permute-start(bf16[32,7168]{1,0:T(8,128)(2,1)S(1)} %get-tuple-element.97), channel_id=1, source_target_pairs={{0,16},{1,33},{2,18},{3,35},{4,20},{5,37},{6,22},{7,39},{8,24},{9,... | collective-permute-start | bytes 1376264 | tf_op jit(solution)/shard_map/ppermute | solution.py:47
  114.6 4.9 %collective-permute-start.18 = (bf16[8,7168]{1,0:T(8,128)(2,1)S(1)}, bf16[8,7168]{1,0:T(8,128)(2,1)S(1)}, u32[]{:S(2)}, u32[]{:S(2)}) collective-permute-start(bf16[8,7168]{1,0:T(8,128)(2,1)S(1)} %get-tuple-element.99), channel_id=1, source_target_pairs={{0,6},{1,7},{2,0},{3,1},{4,2},{5,3},{6,4},{7,5},{8,14},{9,15},{10,... | collective-permute-start | bytes 344072 | tf_op jit(solution)/shard_map/ppermute | solution.py:47
  116.5 8.0 %collective-permute-start.19 = (bf16[8,7168]{1,0:T(8,128)(2,1)S(1)}, bf16[8,7168]{1,0:T(8,128)(2,1)S(1)}, u32[]{:S(2)}, u32[]{:S(2)}) collective-permute-start(bf16[8,7168]{1,0:T(8,128)(2,1)S(1)} %get-tuple-element.100), channel_id=1, source_target_pairs={{0,2},{1,3},{2,4},{3,5},{4,6},{5,7},{6,0},{7,1},{8,10},{9,11},{10,... | collective-permute-start | bytes 344072 | tf_op jit(solution)/shard_map/ppermute | solution.py:47
  116.7 7.8 %collective-permute-start.20 = (bf16[8,7168]{1,0:T(8,128)(2,1)S(1)}, bf16[8,7168]{1,0:T(8,128)(2,1)S(1)}, u32[]{:S(2)}, u32[]{:S(2)}) collective-permute-start(bf16[8,7168]{1,0:T(8,128)(2,1)S(1)} %get-tuple-element.101), channel_id=1, source_target_pairs={{0,4},{1,5},{2,6},{3,7},{4,0},{5,1},{6,2},{7,3},{8,12},{9,13},{10,... | collective-permute-start | bytes 344072 | tf_op jit(solution)/shard_map/ppermute | solution.py:47

commit v4 on v3

--- a/solution.py
+++ b/solution.py
@@ -13,7 +13,8 @@
 AXES = ("zl", "zh", "x", "y", "core")
 SIZES = (2, 2, 4, 4, 2)
 LINE = 4
-STEPS = (0, 1, -1, 2)
+STEPS = (0, 2, 1, -1)
+EARLY = 2
 META = 128
 CHUNK = 512
 LIMIT = 5
@@ -78,6 +79,7 @@
         in_specs=in_vmem(4),
         out_specs=in_vmem(1)[0],
         out_shape=jax.ShapeDtypeStruct((tok_rows, width + META), jnp.bfloat16),
+        compiler_params=pltpu.CompilerParams(vmem_limit_bytes=LIMIT * 2**20),
         name="normalize",
     )(hidden, norm_gain.reshape(1, -1), routes, gate_values)
 
@@ -142,7 +144,7 @@
         in_specs=[pl.BlockSpec(memory_space=pltpu.SMEM)] + in_vmem(LINE),
         out_specs=in_vmem(LINE),
         out_shape=[jax.ShapeDtypeStruct((slots, width), jnp.bfloat16)] * LINE,
-        compiler_params=pltpu.CompilerParams(vmem_limit_bytes=8 * 2**20),
+        compiler_params=pltpu.CompilerParams(vmem_limit_bytes=LIMIT * 2**20),
         cost_estimate=pl.CostEstimate(
             flops=2 * LINE * slots * LINE * piece_rows * width,
             bytes_accessed=2 * LINE * width * (slots + piece_rows),
@@ -168,12 +170,13 @@
         in_specs=[pl.BlockSpec(memory_space=pltpu.SMEM)] + in_vmem(LINE),
         out_specs=in_vmem(1)[0],
         out_shape=jax.ShapeDtypeStruct((2 * rows, LINE * slots), jnp.bfloat16),
+        compiler_params=pltpu.CompilerParams(vmem_limit_bytes=LIMIT * 2**20),
         name="slot_weights",
     )(experts, *pieces)
 
 
 def load_kernel(count, *refs):
-    stored, loaded, arrived = refs[:count], refs[count : 2 * count], refs[2 * count]
+    stored, loaded, arrived = refs[:count], refs[count : 2 * count], refs[-1]
     fetches = [
         pltpu.make_async_copy(source, target, arrived.at[n])
         for n, (source, target) in enumerate(zip(stored, loaded))
@@ -184,25 +187,24 @@
         fetch.wait()
 
 
-def load(weights):
+def load(weights, room):
     count = len(weights)
+    shapes = [w.shape for w in weights] + [room]
     return pl.pallas_call(
         lambda *refs: load_kernel(count, *refs),
         in_specs=[pl.BlockSpec(memory_space=pltpu.HBM)] * count,
-        out_specs=in_vmem(count),
-        out_shape=[jax.ShapeDtypeStruct(w.shape, jnp.bfloat16) for w in weights],
+        out_specs=in_vmem(count + 1),
+        out_shape=[jax.ShapeDtypeStruct(shape, jnp.bfloat16) for shape in shapes],
         scratch_shapes=[pltpu.SemaphoreType.DMA((count,))],
         compiler_params=pltpu.CompilerParams(vmem_limit_bytes=LIMIT * 2**20),
         cost_estimate=pl.CostEstimate(
-            flops=0, bytes_accessed=2 * sum(w.size for w in weights), transcendentals=0
+            flops=600 * sum(w.size for w in weights), bytes_accessed=0, transcendentals=0
         ),
         name="load_weights",
     )(*weights)
 
 
-def experts_kernel(count, *refs):
-    pieces, refs = refs[:count], refs[count:]
-    near, far, outs = refs[:3], refs[3:6], refs[6:]
+def apply_experts(pieces, near, far, down_ready, outs):
     rows = jnp.concatenate([piece[...] for piece in pieces], axis=0)
     piece_rows, width = pieces[0].shape
 
@@ -213,6 +215,7 @@
 
     near_act = activate(near[0], near[1])
     far_act = activate(far[0], far[1])
+    down_ready()
     for start in range(0, width, CHUNK):
         columns = slice(start, start + CHUNK)
         total = (
@@ -223,52 +226,90 @@
             out[:, columns] = total[n * piece_rows : (n + 1) * piece_rows]
 
 
-def run_experts(pieces, near, far):
+def first_kernel(count, *refs):
+    pieces, weights, stored = refs[:count], refs[count : count + 5], refs[count + 6]
+    outs, loaded, arrived = refs[count + 7 : -2], refs[-2], refs[-1]
+    fetch = pltpu.make_async_copy(stored, loaded, arrived)
+    fetch.start()
+    apply_experts(pieces, weights[:3], list(weights[3:]) + [loaded], fetch.wait, outs)
+
+
+def later_kernel(count, *refs):
+    pieces, weights, outs = refs[:count], refs[count : count + 6], refs[count + 6 :]
+    apply_experts(pieces, weights[:3], weights[3:], lambda: None, outs)
+
+
+def run_experts(pieces, weights, stored=None):
     count = len(pieces)
     piece_rows, width = pieces[0].shape
-    size = sum(w.size for w in near) + sum(w.size for w in far)
-    return pl.pallas_call(
-        lambda *refs: experts_kernel(count, *refs),
-        in_specs=in_vmem(count + 6),
-        out_specs=in_vmem(count),
-        out_shape=[jax.ShapeDtypeStruct((piece_rows, width), jnp.bfloat16)] * count,
+    results = [jax.ShapeDtypeStruct((piece_rows, width), jnp.bfloat16)] * count
+    in_specs = in_vmem(count + len(weights))
+    operands = [*pieces, *weights]
+    scratch = []
+    aliases = {}
+    kernel = later_kernel
+    if stored is not None:
+        kernel = first_kernel
+        in_specs.append(pl.BlockSpec(memory_space=pltpu.HBM))
+        operands.append(stored)
+        aliases = {len(operands) - 2: len(results)}
+        results.append(jax.ShapeDtypeStruct(stored.shape, stored.dtype))
+        scratch.append(pltpu.SemaphoreType.DMA)
+    size = sum(w.size for w in weights)
+    return pl.pallas_call(
+        lambda *refs: kernel(count, *refs),
+        in_specs=in_specs,
+        out_specs=in_vmem(len(results)),
+        out_shape=results,
+        scratch_shapes=scratch,
+        input_output_aliases=aliases,
         compiler_params=pltpu.CompilerParams(vmem_limit_bytes=LIMIT * 2**20),
         cost_estimate=pl.CostEstimate(
             flops=2 * count * piece_rows * size, bytes_accessed=2 * size, transcendentals=0
         ),
         name="experts",
-    )(*pieces, *near, *far)
-
-
-def spread_kernel(weigh_ref, *refs):
-    pieces, outs = refs[:LINE], refs[LINE:]
-    count, width = outs[0].shape
+    )(*operands)
+
+
+def spread_kernel(first_slot, count, *refs):
+    weigh_ref, pieces, refs = refs[0], refs[1 : 1 + count], refs[1 + count :]
     half = weigh_ref.shape[0] // 2
+    piece_rows, width = pieces[0].shape
+    slots = slice(first_slot, first_slot + count * piece_rows)
+    outs = refs if first_slot == 0 else refs[1:]
     for start in range(0, width, CHUNK):
         columns = slice(start, start + CHUNK)
         rows = jnp.concatenate([p[:, columns] for p in pieces], axis=0)
-        both = jnp.dot(weigh_ref[...], rows, preferred_element_type=jnp.float32)
-        total = (both[:half] + both[half:]).astype(jnp.bfloat16)
-        for n in range(LINE):
-            outs[n][:, columns] = total[n * count : (n + 1) * count]
-
-
-def spread(weights, pieces):
+        both = jnp.dot(weigh_ref[:, slots], rows, preferred_element_type=jnp.float32)
+        total = both[:half] + both[half:]
+        if first_slot > 0:
+            total = (total + refs[0][:, columns]).astype(jnp.bfloat16)
+        for n, out in enumerate(outs):
+            out[:, columns] = total[n * out.shape[0] : (n + 1) * out.shape[0]]
+
+
+def spread(weights, pieces, begun=None):
     slots, width = pieces[0].shape
     rows = weights.shape[0] // 2
-    return pl.pallas_call(
-        spread_kernel,
-        in_specs=in_vmem(1 + LINE),
-        out_specs=in_vmem(LINE),
-        out_shape=[jax.ShapeDtypeStruct((rows // LINE, width), jnp.bfloat16)] * LINE,
-        compiler_params=pltpu.CompilerParams(vmem_limit_bytes=8 * 2**20),
+    first_slot = 0 if begun is None else EARLY * slots
+    results = [jax.ShapeDtypeStruct((rows, width), jnp.float32)]
+    operands = [weights, *pieces]
+    if begun is not None:
+        results = [jax.ShapeDtypeStruct((rows // LINE, width), jnp.bfloat16)] * LINE
+        operands.append(begun)
+    return pl.pallas_call(
+        lambda *refs: spread_kernel(first_slot, len(pieces), *refs),
+        in_specs=in_vmem(len(operands)),
+        out_specs=in_vmem(len(results)),
+        out_shape=results,
+        compiler_params=pltpu.CompilerParams(vmem_limit_bytes=LIMIT * 2**20),
         cost_estimate=pl.CostEstimate(
-            flops=2 * 2 * rows * LINE * slots * width,
-            bytes_accessed=2 * width * (LINE * slots + rows),
+            flops=2 * 2 * rows * len(pieces) * slots * width,
+            bytes_accessed=2 * width * (len(pieces) * slots + 2 * rows),
             transcendentals=0,
         ),
         name="spread_slots",
-    )(weights, *pieces)
+    )(*operands)
 
 
 def add_kernel(parts, *refs):
@@ -288,7 +329,7 @@
         in_specs=in_vmem(LINE),
         out_specs=in_vmem(parts),
         out_shape=[jax.ShapeDtypeStruct((rows // parts, width), jnp.bfloat16)] * parts,
-        compiler_params=pltpu.CompilerParams(vmem_limit_bytes=8 * 2**20),
+        compiler_params=pltpu.CompilerParams(vmem_limit_bytes=LIMIT * 2**20),
         cost_estimate=pl.CostEstimate(
             flops=LINE * rows * width,
             bytes_accessed=2 * (LINE + 1) * rows * width,
@@ -361,15 +402,17 @@
     weights = weigh(plane, experts, tok_rows, topk)
     attn_out = attend(queries, latent_cache, lengths)
 
-    loaded = load((w_gate, w_up, w_down, far_gate, far_up, far_down))
-    results = []
-    for group in (slots[:2], slots[2:]):
-        group, loaded, results = lax.optimization_barrier((group, loaded, results))
-        results = results + list(run_experts(group, loaded[:3], loaded[3:]))
+    loaded = load((w_gate, w_up, w_down, far_gate, far_up), w_down.shape)
+    group, loaded = lax.optimization_barrier((slots[:EARLY], loaded))
+    *results, last = run_experts(group, loaded, far_down)
+    group, loaded, last = lax.optimization_barrier((slots[EARLY:], loaded[:5], last))
+    results = results + list(run_experts(group, [*loaded, last]))
     back = [results[0]] + [
         hand_back(piece, THIRD, step) for piece, step in zip(results[1:], STEPS[1:])
     ]
-    dense = spread(weights, back)
+    (begun,) = spread(weights, back[:EARLY])
+    begun, late = lax.optimization_barrier((begun, back[EARLY:]))
+    dense = spread(weights, late, begun)
     dense = [dense[0]] + [
         hand_back(piece, SECOND, step) for piece, step in zip(dense[1:], STEPS[1:])
     ]

time: 127 us -> 108 us (0.85)
  Pallas kernels: 37.5 us -> 29.9 us
  waiting for transfers between devices: 50.9 us -> 45.4 us
  starting transfers between devices: 29.8 us -> 25.2 us
  local copies, waits for them, and re-layouts: 0.94 us -> 3.03 us
  matrix products: 3.38 us -> 1.91 us
    ppermute x3, waiting for transfers between devices: 5.29 us -> 0.01 us  [to_other_core(): return lax.ppermute(rows, 'core', [(0, 1), (1, 0)])]
    ppermute x18, starting transfers between devices: 26.6 us -> 23.5 us  [shift(): return lax.ppermute(rows, AXES, pairs)]
    pallas_call x3 -> x4, Pallas kernels: 16.6 us -> 14.3 us  [the longest x2 12.1 us: run_experts(): pl.pallas_call(lambda *refs: kernel(count, *refs), in_specs=in_specs, out...]
    pallas_call x1, Pallas kernels: 13.6 us -> 11.5 us  [load(): pl.pallas_call(lambda *refs: load_kernel(count, *refs), in_specs=[pl.Bloc...]
    unnamed x16 -> x12, local copies, waits for them, and re-layouts: 0.94 us -> 3.03 us
    pallas_call x1, Pallas kernels: 1.74 us -> 0.17 us  [normalize(): pl.pallas_call(normalize_kernel, in_specs=in_vmem(4), out_specs=in_vmem(1...]
    pallas_call x1, Pallas kernels: 2.63 us -> 1.06 us  [weigh(): pl.pallas_call(lambda *refs: weigh_kernel(tok_rows, topk, *refs), in_spec...]
    dot_general x1, matrix products: 2.06 us -> 0.58 us  [attend(): jnp.einsum('rhk,rck->rhc', queries, latent_cache, preferred_element_type=...]
  transfers between devices with their start and end apart: 21 -> 21, of which waited for: 14 -> 13; matrix products, arithmetic and copies ran while one was open for 4% -> 2% of each run, Pallas kernels for 22% -> 26%
where the time goes in v4:
time: 108 us; the launch traced here: 107 us
  waiting for transfers between devices  45.4 us (42%)
  Pallas kernels  29.9 us (28%)
  starting transfers between devices  25.2 us (23%)
  local copies, waits for them, and re-layouts  3.03 us (3%)
  matrix products  1.91 us (2%)
  between operations  1.44 us (1%)
    ppermute x18, waiting for transfers between devices, shift(): return lax.ppermute(rows, AXES, pairs)  45.4 us
    ppermute x18, starting transfers between devices, shift(): return lax.ppermute(rows, AXES, pairs)  23.5 us
    pallas_call x2, Pallas kernels, run_experts(): pl.pallas_call(lambda *refs: kernel(count, *refs), in_specs=in_specs, out...  12.1 us
    pallas_call x1, Pallas kernels, load(): pl.pallas_call(lambda *refs: load_kernel(count, *refs), in_specs=[pl.Bloc...  11.5 us
    unnamed x12, local copies, waits for them, and re-layouts  3.03 us
    pallas_call x2, Pallas kernels, spread(): pl.pallas_call(lambda *refs: spread_kernel(first_slot, len(pieces), *refs...  2.19 us
  transfers between devices with their start and end apart: 21, of which 13 were waited for; matrix products, arithmetic and copies ran while one was open for 2% of the time, Pallas kernels for 26%

profile of v4, /device:TPU:4, one launch (start us, length us, event | category | flops | bytes accessed | tf_op | source)
XLA Modules:
  0.0 107.3 jit_solution(18422100997755120398)
XLA Ops:
  0.6 0.1 collective-permute-start.6
  0.8 0.9 copy-done.1
  1.6 0.7 copy-done.2
  2.4 0.7 copy-done.3
  3.1 0.7 copy-done.4
  3.8 0.2 normalize.1
  3.9 3.1 %collective-permute-start.2 = (bf16[8,7296]{1,0:T(8,128)(2,1)S(1)}, bf16[8,7296]{1,0:T(8,128)(2,1)S(1)}, u32[]{:S(2)}, u32[]{:S(2)}) collective-permute-start(bf16[8,7296]{1,0:T(8,128)(2,1)S(1)} %normalize.1), channel_id=1, source_target_pairs={{0,6},{1,7},{2,0},{3,1},{4,2},{5,3},{6,4},{7,5},{8,14},{9,15},{10,... | collective-permute-start | bytes 350216 | tf_op jit(solution)/shard_map/ppermute | solution.py:48
  7.0 2.2 %collective-permute-start = (bf16[8,7296]{1,0:T(8,128)(2,1)S(1)}, bf16[8,7296]{1,0:T(8,128)(2,1)S(1)}, u32[]{:S(2)}, u32[]{:S(2)}) collective-permute-start(bf16[8,7296]{1,0:T(8,128)(2,1)S(1)} %normalize.1), channel_id=1, source_target_pairs={{0,4},{1,5},{2,6},{3,7},{4,0},{5,1},{6,2},{7,3},{8,12},{9,13},{10,... | collective-permute-start | bytes 350216 | tf_op jit(solution)/shard_map/ppermute | solution.py:48
  9.2 0.9 collective-permute-done.2
  10.1 5.9 %collective-permute-done.1 = bf16[8,7296]{1,0:T(8,128)(2,1)S(1)} collective-permute-done((bf16[8,7296]{1,0:T(8,128)(2,1)S(1)}, bf16[8,7296]{1,0:T(8,128)(2,1)S(1)}, u32[]{:S(2)}, u32[]{:S(2)}) %collective-permute-start.1) | collective-permute-done | bytes 116768 | tf_op jit(solution)/shard_map/ppermute | solution.py:48
  16.1 0.1 collective-permute-start.8
  16.2 0.6 collective-permute-start.3
  16.8 2.1 %collective-permute-start.4 = (bf16[32,7296]{1,0:T(8,128)(2,1)S(1)}, bf16[32,7296]{1,0:T(8,128)(2,1)S(1)}, u32[]{:S(2)}, u32[]{:S(2)}) collective-permute-start(bf16[32,7296]{1,0:T(8,128)(2,1)S(1)} %pad_maximum_fusion.refs_1_), channel_id=1, source_target_pairs={{0,8},{1,65},{2,10},{3,67},{4,12},{5,69},{6,14},{7,71},{8,16},{9,7... | collective-permute-start | bytes 1400840 | tf_op jit(solution)/shard_map/ppermute | solution.py:48
  18.9 7.5 %collective-permute-done.3.refs_2_ = bf16[32,7296]{1,0:T(8,128)(2,1)S(1)} collective-permute-done((bf16[32,7296]{1,0:T(8,128)(2,1)S(1)}, bf16[32,7296]{1,0:T(8,128)(2,1)S(1)}, u32[]{:S(2)}, u32[]{:S(2)}) %collective-permute-start.3) | collective-permute-done | bytes 466976 | tf_op jit(solution)/shard_map/ppermute | solution.py:48
  26.4 4.0 %collective-permute-done.4.refs_3_ = bf16[32,7296]{1,0:T(8,128)(2,1)S(1)} collective-permute-done((bf16[32,7296]{1,0:T(8,128)(2,1)S(1)}, bf16[32,7296]{1,0:T(8,128)(2,1)S(1)}, u32[]{:S(2)}, u32[]{:S(2)}) %collective-permute-start.4) | collective-permute-done | bytes 466976 | tf_op jit(solution)/shard_map/ppermute | solution.py:48
  30.5 1.5 %collective-permute-start.9 = (bf16[512,7168]{1,0:T(8,128)(2,1)}, bf16[512,7168]{1,0:T(8,128)(2,1)}, u32[]{:S(2)}, u32[]{:S(2)}) collective-permute-start(bf16[512,7168]{1,0:T(8,128)(2,1)} %refs_2_), channel_id=1, source_target_pairs={{0,1},{1,0},{2,3},{3,2},{4,5},{5,4},{6,7},{7,6},{8,9},{9,8},{10,11... | collective-permute-start | bytes 22020104 | tf_op jit(solution)/shard_map/ppermute | solution.py:52
  32.1 2.0 %select_slots.1 = (bf16[64,7168]{1,0:T(8,128)(2,1)S(1)}, bf16[64,7168]{1,0:T(8,128)(2,1)S(1)}, bf16[64,7168]{1,0:T(8,128)(2,1)S(1)}, bf16[64,7168]{1,0:T(8,128)(2,1)S(1)}) custom-call(s32[4]{0:T(128)S(1)} %pad_add_fusion.refs_0_, bf16[32,7296]{1,0:T(8,128)(2,1)S(1)} %pad_maximum_fusion.refs_1_, bf16[32,7296]{1,0:T(8,128)(2,1)S(1)} %collective-permute-done.3.refs_2_, ...), custom_call_target="tpu_custom_call" | custom-call | flops 469762048 | bytes 5505024 | tf_op jit(solution)/shard_map/select_slots/pallas_call | solution.py:142
  34.1 2.7 %collective-permute-start.7 = (bf16[64,7168]{1,0:T(8,128)(2,1)S(1)}, bf16[64,7168]{1,0:T(8,128)(2,1)S(1)}, u32[]{:S(2)}, u32[]{:S(2)}) collective-permute-start(bf16[64,7168]{1,0:T(8,128)(2,1)S(1)} %get-tuple-element.61), channel_id=1, source_target_pairs={{0,32},{1,17},{2,34},{3,19},{4,36},{5,21},{6,38},{7,23},{8,40},{9,... | collective-permute-start | bytes 2752520 | tf_op jit(solution)/shard_map/ppermute | solution.py:48
  36.8 1.0 collective-permute-start.11
  37.8 2.2 %collective-permute-start.12 = (bf16[64,7168]{1,0:T(8,128)(2,1)S(1)}, bf16[64,7168]{1,0:T(8,128)(2,1)S(1)}, u32[]{:S(2)}, u32[]{:S(2)}) collective-permute-start(bf16[64,7168]{1,0:T(8,128)(2,1)S(1)} %get-tuple-element.83), channel_id=1, source_target_pairs={{0,96},{1,25},{2,98},{3,27},{4,100},{5,29},{6,102},{7,31},{8,104},... | collective-permute-start | bytes 2752520 | tf_op jit(solution)/shard_map/ppermute | solution.py:48
  40.1 11.5 %load_weights.1 = (bf16[7168,512]{1,0:T(8,128)(2,1)S(1)}, bf16[7168,512]{1,0:T(8,128)(2,1)S(1)}, bf16[512,7168]{1,0:T(8,128)(2,1)S(1)}, bf16[7168,512]{1,0:T(8,1...) custom-call(bf16[7168,512]{1,0:T(8,128)(2,1)} %refs_0_, bf16[7168,512]{1,0:T(8,128)(2,1)} %refs_1_, ...), custom_call_target="tpu_custom_call" | custom-call | flops 11010048000 | tf_op jit(solution)/shard_map/load_weights/pallas_call | solution.py:193
  51.6 6.1 %experts.2 = (bf16[64,7168]{1,0:T(8,128)(2,1)S(1)}, bf16[64,7168]{1,0:T(8,128)(2,1)S(1)}, bf16[512,7168]{1,0:T(8,128)(2,1)S(1)}) custom-call(bf16[64,7168]{1,0:T(8,128)(2,1)S(1)} %get-tuple-element.72.refs_0_, bf16[64,7168]{1,0:T(8,128)(2,1)S(1)} %collective-permute-done.7.refs_1_, ...), custom_call_target="tpu_custom_call", output_to_operand_aliasing={{2}: (7, {})} | custom-call | flops 5637144576 | bytes 44040192 | tf_op jit(solution)/shard_map/experts/pallas_call | solution.py:259
  57.7 0.5 collective-permute-start.10
  58.2 0.8 collective-permute-done.11.refs_0_
  58.9 0.2 collective-permute-done.12.refs_1_
  59.1 6.0 %experts.3 = (bf16[64,7168]{1,0:T(8,128)(2,1)S(1)}, bf16[64,7168]{1,0:T(8,128)(2,1)S(1)}) custom-call(bf16[64,7168]{1,0:T(8,128)(2,1)S(1)} %collective-permute-done.11.refs_0_, bf16[64,7168]{1,0:T(8,128)(2,1)S(1)} %collective-permute-done.12.refs_1_, bf16[7168,512]{1,0:T(8,128)(2,1)S(1)} %get-tuple-element.87.refs_2_, ...), custom_call_target="tpu_custom_call" | custom-call | flops 5637144576 | bytes 44040192 | tf_op jit(solution)/shard_map/experts/pallas_call | solution.py:259
  65.1 2.7 %collective-permute-start.13 = (bf16[64,7168]{1,0:T(8,128)(2,1)S(1)}, bf16[64,7168]{1,0:T(8,128)(2,1)S(1)}, u32[]{:S(2)}, u32[]{:S(2)}) collective-permute-start(bf16[64,7168]{1,0:T(8,128)(2,1)S(1)} %get-tuple-element.93), channel_id=1, source_target_pairs={{0,96},{1,25},{2,98},{3,27},{4,100},{5,29},{6,102},{7,31},{8,104},... | collective-permute-start | bytes 2752520 | tf_op jit(solution)/shard_map/ppermute | solution.py:48
  68.5 1.1 slot_weights.1.refs_0_
  69.5 3.3 %collective-permute-done.10.refs_2_ = bf16[64,7168]{1,0:T(8,128)(2,1)S(1)} collective-permute-done((bf16[64,7168]{1,0:T(8,128)(2,1)S(1)}, bf16[64,7168]{1,0:T(8,128)(2,1)S(1)}, u32[]{:S(2)}, u32[]{:S(2)}) %collective-permute-start.10) | collective-permute-done | bytes 917536 | tf_op jit(solution)/shard_map/ppermute | solution.py:48
  72.8 1.1 %spread_slots.2.refs_3_ = f32[128,7168]{1,0:T(8,128)S(1)} custom-call(bf16[256,256]{1,0:T(8,128)(2,1)S(1)} %slot_weights.1.refs_0_, bf16[64,7168]{1,0:T(8,128)(2,1)S(1)} %get-tuple-element.80.refs_1_, bf16[64,7168]{1,0:T(8,128)(2,1)S(1)} %collective-permute-done.10.refs_2_), custom_call_target="tpu_custom_call" | custom-call | flops 469762048 | bytes 5505024 | tf_op jit(solution)/shard_map/spread_slots/pallas_call | solution.py:300
  73.9 6.5 %collective-permute-done.13.refs_1_ = bf16[64,7168]{1,0:T(8,128)(2,1)S(1)} collective-permute-done((bf16[64,7168]{1,0:T(8,128)(2,1)S(1)}, bf16[64,7168]{1,0:T(8,128)(2,1)S(1)}, u32[]{:S(2)}, u32[]{:S(2)}) %collective-permute-start.13) | collective-permute-done | bytes 917536 | tf_op jit(solution)/shard_map/ppermute | solution.py:48
  80.4 2.3 %collective-permute-done.14.refs_2_ = bf16[64,7168]{1,0:T(8,128)(2,1)S(1)} collective-permute-done((bf16[64,7168]{1,0:T(8,128)(2,1)S(1)}, bf16[64,7168]{1,0:T(8,128)(2,1)S(1)}, u32[]{:S(2)}, u32[]{:S(2)}) %collective-permute-start.14) | collective-permute-done | bytes 917536 | tf_op jit(solution)/shard_map/ppermute | solution.py:48
  82.6 1.1 %spread_slots.3 = (bf16[32,7168]{1,0:T(8,128)(2,1)S(1)}, bf16[32,7168]{1,0:T(8,128)(2,1)S(1)}, bf16[32,7168]{1,0:T(8,128)(2,1)S(1)}, bf16[32,7168]{1,0:T(8,128)(2,1)S(1)}) custom-call(bf16[256,256]{1,0:T(8,128)(2,1)S(1)} %slot_weights.1.refs_0_, bf16[64,7168]{1,0:T(8,128)(2,1)S(1)} %collective-permute-done.13.refs_1_, ...), custom_call_target="tpu_custom_call" | custom-call | flops 469762048 | bytes 5505024 | tf_op jit(solution)/shard_map/spread_slots/pallas_call | solution.py:300
  83.8 1.5 %collective-permute-start.15 = (bf16[32,7168]{1,0:T(8,128)(2,1)S(1)}, bf16[32,7168]{1,0:T(8,128)(2,1)S(1)}, u32[]{:S(2)}, u32[]{:S(2)}) collective-permute-start(bf16[32,7168]{1,0:T(8,128)(2,1)S(1)} %get-tuple-element.99), channel_id=1, source_target_pairs={{0,16},{1,33},{2,18},{3,35},{4,20},{5,37},{6,22},{7,39},{8,24},{9,... | collective-permute-start | bytes 1376264 | tf_op jit(solution)/shard_map/ppermute | solution.py:48
  85.2 1.9 %collective-permute-start.16 = (bf16[32,7168]{1,0:T(8,128)(2,1)S(1)}, bf16[32,7168]{1,0:T(8,128)(2,1)S(1)}, u32[]{:S(2)}, u32[]{:S(2)}) collective-permute-start(bf16[32,7168]{1,0:T(8,128)(2,1)S(1)} %get-tuple-element.100), channel_id=1, source_target_pairs={{0,24},{1,97},{2,26},{3,99},{4,28},{5,101},{6,30},{7,103},{8,0},{9... | collective-permute-start | bytes 1376264 | tf_op jit(solution)/shard_map/ppermute | solution.py:48
  87.1 0.3 collective-permute-start.17
  87.4 0.6 fusion.15
  88.0 0.3 fusion.11
  88.3 5.7 %collective-permute-done.15.refs_1_ = bf16[32,7168]{1,0:T(8,128)(2,1)S(1)} collective-permute-done((bf16[32,7168]{1,0:T(8,128)(2,1)S(1)}, bf16[32,7168]{1,0:T(8,128)(2,1)S(1)}, u32[]{:S(2)}, u32[]{:S(2)}) %collective-permute-start.15) | collective-permute-done | bytes 458784 | tf_op jit(solution)/shard_map/ppermute | solution.py:48
  93.9 4.9 %collective-permute-done.16.refs_2_ = bf16[32,7168]{1,0:T(8,128)(2,1)S(1)} collective-permute-done((bf16[32,7168]{1,0:T(8,128)(2,1)S(1)}, bf16[32,7168]{1,0:T(8,128)(2,1)S(1)}, u32[]{:S(2)}, u32[]{:S(2)}) %collective-permute-start.16) | collective-permute-done | bytes 458784 | tf_op jit(solution)/shard_map/ppermute | solution.py:48
  98.8 0.2 add_pieces.2
  99.0 0.6 collective-permute-start.18
  99.7 0.7 collective-permute-start.19
  100.4 1.3 %collective-permute-start.20 = (bf16[8,7168]{1,0:T(8,128)(2,1)S(1)}, bf16[8,7168]{1,0:T(8,128)(2,1)S(1)}, u32[]{:S(2)}, u32[]{:S(2)}) collective-permute-start(bf16[8,7168]{1,0:T(8,128)(2,1)S(1)} %get-tuple-element.105), channel_id=1, source_target_pairs={{0,2},{1,3},{2,4},{3,5},{4,6},{5,7},{6,0},{7,1},{8,10},{9,11},{10,... | collective-permute-start | bytes 344072 | tf_op jit(solution)/shard_map/ppermute | solution.py:48
  101.7 1.3 %fusion.8 = bf16[1,128,512]{2,1,0:T(8,128)(2,1)} fusion(bf16[1,1536,576]{1,2,0:T(8,128)(2,1)S(1)} %copy-done.5, f32[128,1536]{1,0:T(8,128)S(1)} %get-tuple-element.107, f32[128]{0:T(128)S(1)} %fusion.11, f32[128]{0:T(128)S(1)} %get-tuple-element.106), kind=kOutput, calls=%fused_computation.7 | convolution fusion | flops 201981952 | bytes 2491392 | tf_op jit(solution)/shard_map/rhc,rcl->rhl/dot_general | solution.py:352
  103.0 2.4 %collective-permute-done.18.refs_1_ = bf16[8,7168]{1,0:T(8,128)(2,1)S(1)} collective-permute-done((bf16[8,7168]{1,0:T(8,128)(2,1)S(1)}, bf16[8,7168]{1,0:T(8,128)(2,1)S(1)}, u32[]{:S(2)}, u32[]{:S(2)}) %collective-permute-start.18) | collective-permute-done | bytes 114720 | tf_op jit(solution)/shard_map/ppermute | solution.py:48
  105.4 1.2 %collective-permute-done.20.refs_3_ = bf16[8,7168]{1,0:T(8,128)(2,1)S(1)} collective-permute-done((bf16[8,7168]{1,0:T(8,128)(2,1)S(1)}, bf16[8,7168]{1,0:T(8,128)(2,1)S(1)}, u32[]{:S(2)}, u32[]{:S(2)}) %collective-permute-start.20) | collective-permute-done | bytes 114720 | tf_op jit(solution)/shard_map/ppermute | solution.py:48
  106.6 0.7 add_pieces.3
  (22 shorter events, 0.2 us)
Async XLA Ops:
  0.6 86.8 %copy-start = (bf16[1,128,576]{1,2,0:T(8,128)(2,1)S(1)}, bf16[1,128,576]{1,2,0:T(8,128)(2,1)}, u32[]{:S(2)}) copy-start(bf16[1,128,576]{1,2,0:T(8,128)(2,1)} %param.17) | copy-start | bytes 442372
  0.6 29.8 %collective-permute-start.6 = (bf16[7168,512]{1,0:T(8,128)(2,1)}, bf16[7168,512]{1,0:T(8,128)(2,1)}, u32[]{:S(2)}, u32[]{:S(2)}) collective-permute-start(bf16[7168,512]{1,0:T(8,128)(2,1)} %refs_0_), channel_id=1, source_target_pairs={{0,1},{1,0},{2,3},{3,2},{4,5},{5,4},{6,7},{7,6},{8,9},{9,8},{10,11... | collective-permute-start | bytes 22020104 | tf_op jit(solution)/shard_map/ppermute | solution.py:52
  0.7 0.9 copy-start.1
  1.6 0.7 copy-start.2
  2.4 0.7 copy-start.3
  3.1 0.7 copy-start.4
  3.9 6.2 %collective-permute-start.2 = (bf16[8,7296]{1,0:T(8,128)(2,1)S(1)}, bf16[8,7296]{1,0:T(8,128)(2,1)S(1)}, u32[]{:S(2)}, u32[]{:S(2)}) collective-permute-start(bf16[8,7296]{1,0:T(8,128)(2,1)S(1)} %normalize.1), channel_id=1, source_target_pairs={{0,6},{1,7},{2,0},{3,1},{4,2},{5,3},{6,4},{7,5},{8,14},{9,15},{10,... | collective-permute-start | bytes 350216 | tf_op jit(solution)/shard_map/ppermute | solution.py:48
  7.0 9.0 %collective-permute-start.1 = (bf16[8,7296]{1,0:T(8,128)(2,1)S(1)}, bf16[8,7296]{1,0:T(8,128)(2,1)S(1)}, u32[]{:S(2)}, u32[]{:S(2)}) collective-permute-start(bf16[8,7296]{1,0:T(8,128)(2,1)S(1)} %normalize.1), channel_id=1, source_target_pairs={{0,2},{1,3},{2,4},{3,5},{4,6},{5,7},{6,0},{7,1},{8,10},{9,11},{10,... | collective-permute-start | bytes 350216 | tf_op jit(solution)/shard_map/ppermute | solution.py:48
  7.0 9.0 %collective-permute-start = (bf16[8,7296]{1,0:T(8,128)(2,1)S(1)}, bf16[8,7296]{1,0:T(8,128)(2,1)S(1)}, u32[]{:S(2)}, u32[]{:S(2)}) collective-permute-start(bf16[8,7296]{1,0:T(8,128)(2,1)S(1)} %normalize.1), channel_id=1, source_target_pairs={{0,4},{1,5},{2,6},{3,7},{4,0},{5,1},{6,2},{7,3},{8,12},{9,13},{10,... | collective-permute-start | bytes 350216 | tf_op jit(solution)/shard_map/ppermute | solution.py:48
  16.1 24.0 %collective-permute-start.8 = (bf16[7168,512]{1,0:T(8,128)(2,1)}, bf16[7168,512]{1,0:T(8,128)(2,1)}, u32[]{:S(2)}, u32[]{:S(2)}) collective-permute-start(bf16[7168,512]{1,0:T(8,128)(2,1)} %refs_1_), channel_id=1, source_target_pairs={{0,1},{1,0},{2,3},{3,2},{4,5},{5,4},{6,7},{7,6},{8,9},{9,8},{10,11... | collective-permute-start | bytes 22020104 | tf_op jit(solution)/shard_map/ppermute | solution.py:52
  16.2 10.3 %collective-permute-start.3 = (bf16[32,7296]{1,0:T(8,128)(2,1)S(1)}, bf16[32,7296]{1,0:T(8,128)(2,1)S(1)}, u32[]{:S(2)}, u32[]{:S(2)}) collective-permute-start(bf16[32,7296]{1,0:T(8,128)(2,1)S(1)} %pad_maximum_fusion.refs_1_), channel_id=1, source_target_pairs={{0,16},{1,33},{2,18},{3,35},{4,20},{5,37},{6,22},{7,39},{8,24},{9,... | collective-permute-start | bytes 1400840 | tf_op jit(solution)/shard_map/ppermute | solution.py:48
  16.8 13.7 %collective-permute-start.4 = (bf16[32,7296]{1,0:T(8,128)(2,1)S(1)}, bf16[32,7296]{1,0:T(8,128)(2,1)S(1)}, u32[]{:S(2)}, u32[]{:S(2)}) collective-permute-start(bf16[32,7296]{1,0:T(8,128)(2,1)S(1)} %pad_maximum_fusion.refs_1_), channel_id=1, source_target_pairs={{0,8},{1,65},{2,10},{3,67},{4,12},{5,69},{6,14},{7,71},{8,16},{9,7... | collective-permute-start | bytes 1400840 | tf_op jit(solution)/shard_map/ppermute | solution.py:48
  18.9 11.6 %collective-permute-start.5 = (bf16[32,7296]{1,0:T(8,128)(2,1)S(1)}, bf16[32,7296]{1,0:T(8,128)(2,1)S(1)}, u32[]{:S(2)}, u32[]{:S(2)}) collective-permute-start(bf16[32,7296]{1,0:T(8,128)(2,1)S(1)} %pad_maximum_fusion.refs_1_), channel_id=1, source_target_pairs={{0,24},{1,97},{2,26},{3,99},{4,28},{5,101},{6,30},{7,103},{8,0},{9... | collective-permute-start | bytes 1400840 | tf_op jit(solution)/shard_map/ppermute | solution.py:48
  30.5 21.1 %collective-permute-start.9 = (bf16[512,7168]{1,0:T(8,128)(2,1)}, bf16[512,7168]{1,0:T(8,128)(2,1)}, u32[]{:S(2)}, u32[]{:S(2)}) collective-permute-start(bf16[512,7168]{1,0:T(8,128)(2,1)} %refs_2_), channel_id=1, source_target_pairs={{0,1},{1,0},{2,3},{3,2},{4,5},{5,4},{6,7},{7,6},{8,9},{9,8},{10,11... | collective-permute-start | bytes 22020104 | tf_op jit(solution)/shard_map/ppermute | solution.py:52
  34.1 17.4 %collective-permute-start.7 = (bf16[64,7168]{1,0:T(8,128)(2,1)S(1)}, bf16[64,7168]{1,0:T(8,128)(2,1)S(1)}, u32[]{:S(2)}, u32[]{:S(2)}) collective-permute-start(bf16[64,7168]{1,0:T(8,128)(2,1)S(1)} %get-tuple-element.61), channel_id=1, source_target_pairs={{0,32},{1,17},{2,34},{3,19},{4,36},{5,21},{6,38},{7,23},{8,40},{9,... | collective-permute-start | bytes 2752520 | tf_op jit(solution)/shard_map/ppermute | solution.py:48
  36.8 22.1 %collective-permute-start.11 = (bf16[64,7168]{1,0:T(8,128)(2,1)S(1)}, bf16[64,7168]{1,0:T(8,128)(2,1)S(1)}, u32[]{:S(2)}, u32[]{:S(2)}) collective-permute-start(bf16[64,7168]{1,0:T(8,128)(2,1)S(1)} %get-tuple-element.82), channel_id=1, source_target_pairs={{0,64},{1,9},{2,66},{3,11},{4,68},{5,13},{6,70},{7,15},{8,72},{9,1... | collective-permute-start | bytes 2752520 | tf_op jit(solution)/shard_map/ppermute | solution.py:48
  37.8 21.2 %collective-permute-start.12 = (bf16[64,7168]{1,0:T(8,128)(2,1)S(1)}, bf16[64,7168]{1,0:T(8,128)(2,1)S(1)}, u32[]{:S(2)}, u32[]{:S(2)}) collective-permute-start(bf16[64,7168]{1,0:T(8,128)(2,1)S(1)} %get-tuple-element.83), channel_id=1, source_target_pairs={{0,96},{1,25},{2,98},{3,27},{4,100},{5,29},{6,102},{7,31},{8,104},... | collective-permute-start | bytes 2752520 | tf_op jit(solution)/shard_map/ppermute | solution.py:48
  57.7 15.2 %collective-permute-start.10 = (bf16[64,7168]{1,0:T(8,128)(2,1)S(1)}, bf16[64,7168]{1,0:T(8,128)(2,1)S(1)}, u32[]{:S(2)}, u32[]{:S(2)}) collective-permute-start(bf16[64,7168]{1,0:T(8,128)(2,1)S(1)} %get-tuple-element.81), channel_id=1, source_target_pairs={{0,32},{1,17},{2,34},{3,19},{4,36},{5,21},{6,38},{7,23},{8,40},{9,... | collective-permute-start | bytes 2752520 | tf_op jit(solution)/shard_map/ppermute | solution.py:48
  65.1 22.3 %copy-start.5 = (bf16[1,1536,576]{1,2,0:T(8,128)(2,1)S(1)}, bf16[1,1536,576]{1,2,0:T(8,128)(2,1)}, u32[]{:S(2)}) copy-start(bf16[1,1536,576]{1,2,0:T(8,128)(2,1)} %param.18) | copy-start | bytes 5308420
  65.1 15.3 %collective-permute-start.13 = (bf16[64,7168]{1,0:T(8,128)(2,1)S(1)}, bf16[64,7168]{1,0:T(8,128)(2,1)S(1)}, u32[]{:S(2)}, u32[]{:S(2)}) collective-permute-start(bf16[64,7168]{1,0:T(8,128)(2,1)S(1)} %get-tuple-element.93), channel_id=1, source_target_pairs={{0,96},{1,25},{2,98},{3,27},{4,100},{5,29},{6,102},{7,31},{8,104},... | collective-permute-start | bytes 2752520 | tf_op jit(solution)/shard_map/ppermute | solution.py:48
  67.8 14.8 %collective-permute-start.14 = (bf16[64,7168]{1,0:T(8,128)(2,1)S(1)}, bf16[64,7168]{1,0:T(8,128)(2,1)S(1)}, u32[]{:S(2)}, u32[]{:S(2)}) collective-permute-start(bf16[64,7168]{1,0:T(8,128)(2,1)S(1)} %get-tuple-element.94), channel_id=1, source_target_pairs={{0,64},{1,9},{2,66},{3,11},{4,68},{5,13},{6,70},{7,15},{8,72},{9,1... | collective-permute-start | bytes 2752520 | tf_op jit(solution)/shard_map/ppermute | solution.py:48
  83.8 10.2 %collective-permute-start.15 = (bf16[32,7168]{1,0:T(8,128)(2,1)S(1)}, bf16[32,7168]{1,0:T(8,128)(2,1)S(1)}, u32[]{:S(2)}, u32[]{:S(2)}) collective-permute-start(bf16[32,7168]{1,0:T(8,128)(2,1)S(1)} %get-tuple-element.99), channel_id=1, source_target_pairs={{0,16},{1,33},{2,18},{3,35},{4,20},{5,37},{6,22},{7,39},{8,24},{9,... | collective-permute-start | bytes 1376264 | tf_op jit(solution)/shard_map/ppermute | solution.py:48
  85.2 13.6 %collective-permute-start.16 = (bf16[32,7168]{1,0:T(8,128)(2,1)S(1)}, bf16[32,7168]{1,0:T(8,128)(2,1)S(1)}, u32[]{:S(2)}, u32[]{:S(2)}) collective-permute-start(bf16[32,7168]{1,0:T(8,128)(2,1)S(1)} %get-tuple-element.100), channel_id=1, source_target_pairs={{0,24},{1,97},{2,26},{3,99},{4,28},{5,101},{6,30},{7,103},{8,0},{9... | collective-permute-start | bytes 1376264 | tf_op jit(solution)/shard_map/ppermute | solution.py:48
  87.1 11.7 %collective-permute-start.17 = (bf16[32,7168]{1,0:T(8,128)(2,1)S(1)}, bf16[32,7168]{1,0:T(8,128)(2,1)S(1)}, u32[]{:S(2)}, u32[]{:S(2)}) collective-permute-start(bf16[32,7168]{1,0:T(8,128)(2,1)S(1)} %get-tuple-element.101), channel_id=1, source_target_pairs={{0,8},{1,65},{2,10},{3,67},{4,12},{5,69},{6,14},{7,71},{8,16},{9,7... | collective-permute-start | bytes 1376264 | tf_op jit(solution)/shard_map/ppermute | solution.py:48
  99.0 6.4 %collective-permute-start.18 = (bf16[8,7168]{1,0:T(8,128)(2,1)S(1)}, bf16[8,7168]{1,0:T(8,128)(2,1)S(1)}, u32[]{:S(2)}, u32[]{:S(2)}) collective-permute-start(bf16[8,7168]{1,0:T(8,128)(2,1)S(1)} %get-tuple-element.103), channel_id=1, source_target_pairs={{0,4},{1,5},{2,6},{3,7},{4,0},{5,1},{6,2},{7,3},{8,12},{9,13},{10,... | collective-permute-start | bytes 344072 | tf_op jit(solution)/shard_map/ppermute | solution.py:48
  99.7 5.8 %collective-permute-start.19 = (bf16[8,7168]{1,0:T(8,128)(2,1)S(1)}, bf16[8,7168]{1,0:T(8,128)(2,1)S(1)}, u32[]{:S(2)}, u32[]{:S(2)}) collective-permute-start(bf16[8,7168]{1,0:T(8,128)(2,1)S(1)} %get-tuple-element.104), channel_id=1, source_target_pairs={{0,6},{1,7},{2,0},{3,1},{4,2},{5,3},{6,4},{7,5},{8,14},{9,15},{10,... | collective-permute-start | bytes 344072 | tf_op jit(solution)/shard_map/ppermute | solution.py:48
  100.4 6.2 %collective-permute-start.20 = (bf16[8,7168]{1,0:T(8,128)(2,1)S(1)}, bf16[8,7168]{1,0:T(8,128)(2,1)S(1)}, u32[]{:S(2)}, u32[]{:S(2)}) collective-permute-start(bf16[8,7168]{1,0:T(8,128)(2,1)S(1)} %get-tuple-element.105), channel_id=1, source_target_pairs={{0,2},{1,3},{2,4},{3,5},{4,6},{5,7},{6,0},{7,1},{8,10},{9,11},{10,... | collective-permute-start | bytes 344072 | tf_op jit(solution)/shard_map/ppermute | solution.py:48

commit v5 on v4

--- a/solution.py
+++ b/solution.py
@@ -56,7 +56,17 @@
     return [pl.BlockSpec(memory_space=pltpu.VMEM)] * count
 
 
-def normalize_kernel(hidden_ref, gain_ref, routes_ref, gates_ref, out_ref):
+def normalize_kernel(*refs):
+    stored, out_ref, held, arrived = refs[:4], refs[4], refs[5:9], refs[9]
+    fetches = [
+        pltpu.make_async_copy(source, target, arrived.at[n])
+        for n, (source, target) in enumerate(zip(stored, held))
+    ]
+    for fetch in fetches:
+        fetch.start()
+    for fetch in fetches:
+        fetch.wait()
+    hidden_ref, gain_ref, routes_ref, gates_ref = held
     features = hidden_ref[...].astype(jnp.float32)
     squares = jnp.mean(features * features, axis=-1, keepdims=True)
     normed = features * lax.rsqrt(squares + norm_eps) * gain_ref[...]
@@ -74,14 +84,16 @@
 
 def normalize(hidden, norm_gain, routes, gate_values):
     tok_rows, width = hidden.shape
+    operands = (hidden, norm_gain.reshape(1, -1), routes, gate_values)
     return pl.pallas_call(
         normalize_kernel,
-        in_specs=in_vmem(4),
+        in_specs=[pl.BlockSpec(memory_space=pltpu.HBM)] * 4,
         out_specs=in_vmem(1)[0],
         out_shape=jax.ShapeDtypeStruct((tok_rows, width + META), jnp.bfloat16),
-        compiler_params=pltpu.CompilerParams(vmem_limit_bytes=LIMIT * 2**20),
+        scratch_shapes=[pltpu.VMEM(operand.shape, operand.dtype) for operand in operands]
+        + [pltpu.SemaphoreType.DMA((4,))],
         name="normalize",
-    )(hidden, norm_gain.reshape(1, -1), routes, gate_values)
+    )(*operands)
 
 
 def slot_table(meta, experts_ref, tok_rows, topk):
@@ -355,9 +367,9 @@
     return attended.astype(jnp.bfloat16)
 
 
-FIRST = ("y", "y")
+FIRST = ("y", "x")
 SECOND = ("x", "z")
-THIRD = ("z", "x")
+THIRD = ("z", "y")
 
 
 def target_experts():
@@ -366,8 +378,8 @@
     found = []
     for step in STEPS:
         to_z = jnp.where(core == 0, (z + step) % LINE, z)
-        to_x = jnp.where(core == 0, x, (x + step) % LINE)
-        found.append((((to_z % 2) * 2 + to_z // 2) * 4 + to_x) * 2 + y // 2)
+        to_y = jnp.where(core == 0, y, (y + step) % LINE)
+        found.append((((to_z % 2) * 2 + to_z // 2) * 4 + x) * 2 + to_y // 2)
     return jnp.stack(found).astype(jnp.int32)
 
 
@@ -388,17 +400,16 @@
 ):
     tok_rows, topk = routes.shape
     experts = target_experts()
-    far_gate = to_other_core(w_gate)
     own = normalize(hidden, norm_gain, routes, gate_values)
+    own, w_gate, w_up = lax.optimization_barrier((own, w_gate, w_up))
+    far_gate, far_up = to_other_core(w_gate), to_other_core(w_up)
     line = jnp.concatenate(gather_line(own, FIRST), axis=0)
-    line, w_up = lax.optimization_barrier((line, w_up))
-    far_up = to_other_core(w_up)
     plane = gather_line(line, SECOND)
-    plane, w_gate, w_up, w_down, far_gate = lax.optimization_barrier(
-        (plane, w_gate, w_up, w_down, far_gate)
-    )
+    plane, w_gate, w_up, far_gate = lax.optimization_barrier((plane, w_gate, w_up, far_gate))
+    chosen = select(plane, experts, tok_rows, topk)
+    chosen, w_down = lax.optimization_barrier((chosen, w_down))
+    slots = hand_out(chosen, THIRD)
     far_down = to_other_core(w_down)
-    slots = hand_out(select(plane, experts, tok_rows, topk), THIRD)
     weights = weigh(plane, experts, tok_rows, topk)
     attn_out = attend(queries, latent_cache, lengths)
 

time: 108 us -> 106 us (0.981)
  waiting for transfers between devices: 45.4 us -> 40.9 us
  starting transfers between devices: 25.2 us -> 27.6 us
  local copies, waits for them, and re-layouts: 3.03 us -> 1 us
  Pallas kernels: 29.9 us -> 31.6 us
    ppermute x18, waiting for transfers between devices: 45.4 us -> 40.9 us  [shift(): return lax.ppermute(rows, AXES, pairs)]
    ppermute x18, starting transfers between devices: 23.5 us -> 27.4 us  [shift(): return lax.ppermute(rows, AXES, pairs)]
    unnamed x12 -> x7, local copies, waits for them, and re-layouts: 3.03 us -> 0.98 us
    pallas_call x1, Pallas kernels: 0.17 us -> 1.79 us  [normalize(): pl.pallas_call(normalize_kernel, in_specs=[pl.BlockSpec(memory_space=pltp...]
    ppermute x3, starting transfers between devices: 1.71 us -> 0.18 us  [to_other_core(): return lax.ppermute(rows, 'core', [(0, 1), (1, 0)])]
  transfers between devices with their start and end apart: 21 -> 21, of which waited for: 13 -> 12; matrix products, arithmetic and copies ran while one was open for 2% -> 3% of each run, Pallas kernels for 26% -> 26%
where the time goes in v5:
time: 106 us; the launch traced here: 105 us
  waiting for transfers between devices  40.9 us (39%)
  Pallas kernels  31.6 us (30%)
  starting transfers between devices  27.6 us (26%)
  matrix products  1.91 us (2%)
  between operations  1.45 us (1%)
    ppermute x18, waiting for transfers between devices, shift(): return lax.ppermute(rows, AXES, pairs)  40.9 us
    ppermute x18, starting transfers between devices, shift(): return lax.ppermute(rows, AXES, pairs)  27.4 us
    pallas_call x2, Pallas kernels, run_experts(): pl.pallas_call(lambda *refs: kernel(count, *refs), in_specs=in_specs, out...  12.1 us
    pallas_call x1, Pallas kernels, load(): pl.pallas_call(lambda *refs: load_kernel(count, *refs), in_specs=[pl.Bloc...  11.5 us
    pallas_call x2, Pallas kernels, spread(): pl.pallas_call(lambda *refs: spread_kernel(first_slot, len(pieces), *refs...  2.21 us
  transfers between devices with their start and end apart: 21, of which 12 were waited for; matrix products, arithmetic and copies ran while one was open for 3% of the time, Pallas kernels for 26%

profile of v5, /device:TPU:4, one launch (start us, length us, event | category | flops | bytes accessed | tf_op | source)
XLA Modules:
  0.0 104.8 jit_solution(15105989523480339845)
XLA Ops:
  0.6 0.0 copy-start
  0.6 1.8 %normalize.1 = bf16[8,7296]{1,0:T(8,128)(2,1)} custom-call(bf16[8,7168]{1,0:T(8,128)(2,1)} %refs_0_.1, f32[1,7168]{1,0:T(1,128)} %bitcast.26, s32[8,8]{1,0:T(8,128)} %refs_2_.1, f32[8,8]{1,0:T(8,128)} %refs_3_.1), custom_call_target="tpu_custom_call" | custom-call | tf_op jit(solution)/shard_map/normalize/pallas_call | solution.py:88
  2.4 0.1 collective-permute-start.6
  2.5 3.3 %collective-permute-start = (bf16[8,7296]{1,0:T(8,128)(2,1)}, bf16[8,7296]{1,0:T(8,128)(2,1)S(1)}, u32[]{:S(2)}, u32[]{:S(2)}) collective-permute-start(bf16[8,7296]{1,0:T(8,128)(2,1)} %normalize.1), channel_id=1, source_target_pairs={{0,4},{1,17},{2,6},{3,19},{4,0},{5,21},{6,2},{7,23},{8,12},{9,25},... | collective-permute-start | bytes 350216 | tf_op jit(solution)/shard_map/ppermute | solution.py:48
  5.8 0.7 collective-permute-start.1
  6.5 2.6 %collective-permute-start.2 = (bf16[8,7296]{1,0:T(8,128)(2,1)}, bf16[8,7296]{1,0:T(8,128)(2,1)S(1)}, u32[]{:S(2)}, u32[]{:S(2)}) collective-permute-start(bf16[8,7296]{1,0:T(8,128)(2,1)} %normalize.1), channel_id=1, source_target_pairs={{0,6},{1,25},{2,0},{3,27},{4,2},{5,29},{6,4},{7,31},{8,14},{9,1},{... | collective-permute-start | bytes 350216 | tf_op jit(solution)/shard_map/ppermute | solution.py:48
  9.1 0.9 constant_dynamic-update-slice_fusion.3
  10.0 2.0 %collective-permute-done.1 = bf16[8,7296]{1,0:T(8,128)(2,1)S(1)} collective-permute-done((bf16[8,7296]{1,0:T(8,128)(2,1)}, bf16[8,7296]{1,0:T(8,128)(2,1)S(1)}, u32[]{:S(2)}, u32[]{:S(2)}) %collective-permute-start.1) | collective-permute-done | bytes 116768 | tf_op jit(solution)/shard_map/ppermute | solution.py:48
  12.1 0.6 collective-permute-start.3
  12.7 2.1 %collective-permute-start.4 = (bf16[32,7296]{1,0:T(8,128)(2,1)S(1)}, bf16[32,7296]{1,0:T(8,128)(2,1)S(1)}, u32[]{:S(2)}, u32[]{:S(2)}) collective-permute-start(bf16[32,7296]{1,0:T(8,128)(2,1)S(1)} %constant_dynamic-update-slice_fusion.refs_1_), channel_id=1, source_target_pairs={{0,8},{1,65},{2,10},{3,67},{4,12},{5,69},{6,14},{7,71},{8,16},{9,7... | collective-permute-start | bytes 1400840 | tf_op jit(solution)/shard_map/ppermute | solution.py:48
  14.8 0.1 collective-permute-start.5
  14.8 0.1 pad_add_fusion.refs_0_
  14.9 7.4 %collective-permute-done.3.refs_2_ = bf16[32,7296]{1,0:T(8,128)(2,1)S(1)} collective-permute-done((bf16[32,7296]{1,0:T(8,128)(2,1)S(1)}, bf16[32,7296]{1,0:T(8,128)(2,1)S(1)}, u32[]{:S(2)}, u32[]{:S(2)}) %collective-permute-start.3) | collective-permute-done | bytes 466976 | tf_op jit(solution)/shard_map/ppermute | solution.py:48
  22.4 4.0 %collective-permute-done.4.refs_3_ = bf16[32,7296]{1,0:T(8,128)(2,1)S(1)} collective-permute-done((bf16[32,7296]{1,0:T(8,128)(2,1)S(1)}, bf16[32,7296]{1,0:T(8,128)(2,1)S(1)}, u32[]{:S(2)}, u32[]{:S(2)}) %collective-permute-start.4) | collective-permute-done | bytes 466976 | tf_op jit(solution)/shard_map/ppermute | solution.py:48
  26.4 2.0 %select_slots.1 = (bf16[64,7168]{1,0:T(8,128)(2,1)S(1)}, bf16[64,7168]{1,0:T(8,128)(2,1)S(1)}, bf16[64,7168]{1,0:T(8,128)(2,1)S(1)}, bf16[64,7168]{1,0:T(8,128)(2,1)S(1)}) custom-call(s32[4]{0:T(128)S(1)} %pad_add_fusion.refs_0_, bf16[32,7296]{1,0:T(8,128)(2,1)S(1)} %constant_dynamic-update-slice_fusion.refs_1_, ...), custom_call_target="tpu_custom_call" | custom-call | flops 469762048 | bytes 5505024 | tf_op jit(solution)/shard_map/select_slots/pallas_call | solution.py:154
  28.4 0.1 collective-permute-start.9
  28.5 4.0 %collective-permute-start.7 = (bf16[64,7168]{1,0:T(8,128)(2,1)S(1)}, bf16[64,7168]{1,0:T(8,128)(2,1)S(1)}, u32[]{:S(2)}, u32[]{:S(2)}) collective-permute-start(bf16[64,7168]{1,0:T(8,128)(2,1)S(1)} %get-tuple-element.71), channel_id=1, source_target_pairs={{0,32},{1,5},{2,34},{3,7},{4,36},{5,1},{6,38},{7,3},{8,40},{9,13},... | collective-permute-start | bytes 2752520 | tf_op jit(solution)/shard_map/ppermute | solution.py:48
  32.5 1.0 collective-permute-start.11
  33.5 2.2 %collective-permute-start.12 = (bf16[64,7168]{1,0:T(8,128)(2,1)S(1)}, bf16[64,7168]{1,0:T(8,128)(2,1)S(1)}, u32[]{:S(2)}, u32[]{:S(2)}) collective-permute-start(bf16[64,7168]{1,0:T(8,128)(2,1)S(1)} %get-tuple-element.93), channel_id=1, source_target_pairs={{0,96},{1,7},{2,98},{3,1},{4,100},{5,3},{6,102},{7,5},{8,104},{9,1... | collective-permute-start | bytes 2752520 | tf_op jit(solution)/shard_map/ppermute | solution.py:48
  35.7 11.5 %load_weights.1 = (bf16[7168,512]{1,0:T(8,128)(2,1)S(1)}, bf16[7168,512]{1,0:T(8,128)(2,1)S(1)}, bf16[512,7168]{1,0:T(8,128)(2,1)S(1)}, bf16[7168,512]{1,0:T(8,1...) custom-call(bf16[7168,512]{1,0:T(8,128)(2,1)} %refs_0_.2, bf16[7168,512]{1,0:T(8,128)(2,1)} %refs_1_, ...), custom_call_target="tpu_custom_call" | custom-call | flops 11010048000 | tf_op jit(solution)/shard_map/load_weights/pallas_call | solution.py:205
  47.2 6.1 %experts.2 = (bf16[64,7168]{1,0:T(8,128)(2,1)S(1)}, bf16[64,7168]{1,0:T(8,128)(2,1)S(1)}, bf16[512,7168]{1,0:T(8,128)(2,1)S(1)}) custom-call(bf16[64,7168]{1,0:T(8,128)(2,1)S(1)} %get-tuple-element.82.refs_0_, bf16[64,7168]{1,0:T(8,128)(2,1)S(1)} %collective-permute-done.7.refs_1_, ...), custom_call_target="tpu_custom_call", output_to_operand_aliasing={{2}: (7, {})} | custom-call | flops 5637144576 | bytes 44040192 | tf_op jit(solution)/shard_map/experts/pallas_call | solution.py:271
  53.3 0.5 collective-permute-start.10
  53.8 0.9 collective-permute-done.12.refs_1_
  54.7 6.0 %experts.3 = (bf16[64,7168]{1,0:T(8,128)(2,1)S(1)}, bf16[64,7168]{1,0:T(8,128)(2,1)S(1)}) custom-call(bf16[64,7168]{1,0:T(8,128)(2,1)S(1)} %collective-permute-done.11.refs_0_, bf16[64,7168]{1,0:T(8,128)(2,1)S(1)} %collective-permute-done.12.refs_1_, bf16[7168,512]{1,0:T(8,128)(2,1)S(1)} %get-tuple-element.97.refs_2_, ...), custom_call_target="tpu_custom_call" | custom-call | flops 5637144576 | bytes 44040192 | tf_op jit(solution)/shard_map/experts/pallas_call | solution.py:271
  60.8 0.0 copy-start.1
  60.8 2.7 %collective-permute-start.13 = (bf16[64,7168]{1,0:T(8,128)(2,1)S(1)}, bf16[64,7168]{1,0:T(8,128)(2,1)S(1)}, u32[]{:S(2)}, u32[]{:S(2)}) collective-permute-start(bf16[64,7168]{1,0:T(8,128)(2,1)S(1)} %get-tuple-element.103), channel_id=1, source_target_pairs={{0,96},{1,7},{2,98},{3,1},{4,100},{5,3},{6,102},{7,5},{8,104},{9,1... | collective-permute-start | bytes 2752520 | tf_op jit(solution)/shard_map/ppermute | solution.py:48
  64.1 1.1 %slot_weights.1.refs_0_ = bf16[256,256]{1,0:T(8,128)(2,1)S(1)} custom-call(s32[4]{0:T(128)S(1)} %pad_add_fusion.refs_0_, bf16[32,7296]{1,0:T(8,128)(2,1)S(1)} %constant_dynamic-update-slice_fusion.refs_1_, bf16[32,7296]{1,0:T(8,128)(2,1)S(1)} %collective-permute-done.3.refs_2_, bf16[32,7296]{1,0:T(8,128)(2,1)S(1)} %collective-permute-done.4.refs_3_, ...), custom_call_target="tpu_custom_call" | custom-call | tf_op jit(solution)/shard_map/slot_weights/pallas_call | solution.py:180
  65.2 3.3 %collective-permute-done.10.refs_2_ = bf16[64,7168]{1,0:T(8,128)(2,1)S(1)} collective-permute-done((bf16[64,7168]{1,0:T(8,128)(2,1)S(1)}, bf16[64,7168]{1,0:T(8,128)(2,1)S(1)}, u32[]{:S(2)}, u32[]{:S(2)}) %collective-permute-start.10) | collective-permute-done | bytes 917536 | tf_op jit(solution)/shard_map/ppermute | solution.py:48
  68.5 1.1 %spread_slots.2.refs_3_ = f32[128,7168]{1,0:T(8,128)S(1)} custom-call(bf16[256,256]{1,0:T(8,128)(2,1)S(1)} %slot_weights.1.refs_0_, bf16[64,7168]{1,0:T(8,128)(2,1)S(1)} %get-tuple-element.90.refs_1_, bf16[64,7168]{1,0:T(8,128)(2,1)S(1)} %collective-permute-done.10.refs_2_), custom_call_target="tpu_custom_call" | custom-call | flops 469762048 | bytes 5505024 | tf_op jit(solution)/shard_map/spread_slots/pallas_call | solution.py:312
  69.6 6.4 %collective-permute-done.13.refs_1_ = bf16[64,7168]{1,0:T(8,128)(2,1)S(1)} collective-permute-done((bf16[64,7168]{1,0:T(8,128)(2,1)S(1)}, bf16[64,7168]{1,0:T(8,128)(2,1)S(1)}, u32[]{:S(2)}, u32[]{:S(2)}) %collective-permute-start.13) | collective-permute-done | bytes 917536 | tf_op jit(solution)/shard_map/ppermute | solution.py:48
  76.0 2.3 %collective-permute-done.14.refs_2_ = bf16[64,7168]{1,0:T(8,128)(2,1)S(1)} collective-permute-done((bf16[64,7168]{1,0:T(8,128)(2,1)S(1)}, bf16[64,7168]{1,0:T(8,128)(2,1)S(1)}, u32[]{:S(2)}, u32[]{:S(2)}) %collective-permute-start.14) | collective-permute-done | bytes 917536 | tf_op jit(solution)/shard_map/ppermute | solution.py:48
  78.3 1.1 %spread_slots.3 = (bf16[32,7168]{1,0:T(8,128)(2,1)S(1)}, bf16[32,7168]{1,0:T(8,128)(2,1)S(1)}, bf16[32,7168]{1,0:T(8,128)(2,1)S(1)}, bf16[32,7168]{1,0:T(8,128)(2,1)S(1)}) custom-call(bf16[256,256]{1,0:T(8,128)(2,1)S(1)} %slot_weights.1.refs_0_, bf16[64,7168]{1,0:T(8,128)(2,1)S(1)} %collective-permute-done.13.refs_1_, ...), custom_call_target="tpu_custom_call" | custom-call | flops 469762048 | bytes 5505024 | tf_op jit(solution)/shard_map/spread_slots/pallas_call | solution.py:312
  79.4 1.6 %collective-permute-start.15 = (bf16[32,7168]{1,0:T(8,128)(2,1)S(1)}, bf16[32,7168]{1,0:T(8,128)(2,1)S(1)}, u32[]{:S(2)}, u32[]{:S(2)}) collective-permute-start(bf16[32,7168]{1,0:T(8,128)(2,1)S(1)} %get-tuple-element.109), channel_id=1, source_target_pairs={{0,16},{1,33},{2,18},{3,35},{4,20},{5,37},{6,22},{7,39},{8,24},{9,... | collective-permute-start | bytes 1376264 | tf_op jit(solution)/shard_map/ppermute | solution.py:48
  81.0 2.0 %collective-permute-start.16 = (bf16[32,7168]{1,0:T(8,128)(2,1)S(1)}, bf16[32,7168]{1,0:T(8,128)(2,1)S(1)}, u32[]{:S(2)}, u32[]{:S(2)}) collective-permute-start(bf16[32,7168]{1,0:T(8,128)(2,1)S(1)} %get-tuple-element.110), channel_id=1, source_target_pairs={{0,24},{1,97},{2,26},{3,99},{4,28},{5,101},{6,30},{7,103},{8,0},{9... | collective-permute-start | bytes 1376264 | tf_op jit(solution)/shard_map/ppermute | solution.py:48
  83.0 0.0 collective-permute-start.17
  83.1 0.6 fusion.15
  83.7 0.3 fusion.11
  83.9 5.7 %collective-permute-done.15.refs_1_ = bf16[32,7168]{1,0:T(8,128)(2,1)S(1)} collective-permute-done((bf16[32,7168]{1,0:T(8,128)(2,1)S(1)}, bf16[32,7168]{1,0:T(8,128)(2,1)S(1)}, u32[]{:S(2)}, u32[]{:S(2)}) %collective-permute-start.15) | collective-permute-done | bytes 458784 | tf_op jit(solution)/shard_map/ppermute | solution.py:48
  89.6 4.9 %collective-permute-done.16.refs_2_ = bf16[32,7168]{1,0:T(8,128)(2,1)S(1)} collective-permute-done((bf16[32,7168]{1,0:T(8,128)(2,1)S(1)}, bf16[32,7168]{1,0:T(8,128)(2,1)S(1)}, u32[]{:S(2)}, u32[]{:S(2)}) %collective-permute-start.16) | collective-permute-done | bytes 458784 | tf_op jit(solution)/shard_map/ppermute | solution.py:48
  94.5 0.2 add_pieces.2
  94.7 1.6 %collective-permute-start.18 = (bf16[8,7168]{1,0:T(8,128)(2,1)S(1)}, bf16[8,7168]{1,0:T(8,128)(2,1)S(1)}, u32[]{:S(2)}, u32[]{:S(2)}) collective-permute-start(bf16[8,7168]{1,0:T(8,128)(2,1)S(1)} %get-tuple-element.113), channel_id=1, source_target_pairs={{0,4},{1,17},{2,6},{3,19},{4,0},{5,21},{6,2},{7,23},{8,12},{9,25},... | collective-permute-start | bytes 344072 | tf_op jit(solution)/shard_map/ppermute | solution.py:48
  96.3 1.8 %collective-permute-start.19 = (bf16[8,7168]{1,0:T(8,128)(2,1)S(1)}, bf16[8,7168]{1,0:T(8,128)(2,1)S(1)}, u32[]{:S(2)}, u32[]{:S(2)}) collective-permute-start(bf16[8,7168]{1,0:T(8,128)(2,1)S(1)} %get-tuple-element.114), channel_id=1, source_target_pairs={{0,6},{1,25},{2,0},{3,27},{4,2},{5,29},{6,4},{7,31},{8,14},{9,1},{... | collective-permute-start | bytes 344072 | tf_op jit(solution)/shard_map/ppermute | solution.py:48
  98.1 0.8 collective-permute-start.20
  98.9 1.3 %fusion.8 = bf16[1,128,512]{2,1,0:T(8,128)(2,1)} fusion(bf16[1,1536,576]{1,2,0:T(8,128)(2,1)S(1)} %copy-done.1, f32[128,1536]{1,0:T(8,128)S(1)} %get-tuple-element.117, f32[128]{0:T(128)S(1)} %fusion.11, f32[128]{0:T(128)S(1)} %get-tuple-element.116), kind=kOutput, calls=%fused_computation.7 | convolution fusion | flops 201981952 | bytes 2491392 | tf_op jit(solution)/shard_map/rhc,rcl->rhl/dot_general | solution.py:364
  100.2 0.9 collective-permute-done.18.refs_1_
  101.1 1.8 %collective-permute-done.19.refs_2_ = bf16[8,7168]{1,0:T(8,128)(2,1)S(1)} collective-permute-done((bf16[8,7168]{1,0:T(8,128)(2,1)S(1)}, bf16[8,7168]{1,0:T(8,128)(2,1)S(1)}, u32[]{:S(2)}, u32[]{:S(2)}) %collective-permute-start.19) | collective-permute-done | bytes 114720 | tf_op jit(solution)/shard_map/ppermute | solution.py:48
  102.9 1.2 %collective-permute-done.20.refs_3_ = bf16[8,7168]{1,0:T(8,128)(2,1)S(1)} collective-permute-done((bf16[8,7168]{1,0:T(8,128)(2,1)S(1)}, bf16[8,7168]{1,0:T(8,128)(2,1)S(1)}, u32[]{:S(2)}, u32[]{:S(2)}) %collective-permute-start.20) | collective-permute-done | bytes 114720 | tf_op jit(solution)/shard_map/ppermute | solution.py:48
  104.1 0.7 add_pieces.3
  (17 shorter events, 0.1 us)
Async XLA Ops:
  0.6 82.4 %copy-start = (bf16[1,128,576]{1,2,0:T(8,128)(2,1)S(1)}, bf16[1,128,576]{1,2,0:T(8,128)(2,1)}, u32[]{:S(2)}) copy-start(bf16[1,128,576]{1,2,0:T(8,128)(2,1)} %param.17) | copy-start | bytes 442372
  2.4 23.9 %collective-permute-start.6 = (bf16[7168,512]{1,0:T(8,128)(2,1)}, bf16[7168,512]{1,0:T(8,128)(2,1)}, u32[]{:S(2)}, u32[]{:S(2)}) collective-permute-start(bf16[7168,512]{1,0:T(8,128)(2,1)} %refs_0_.2), channel_id=1, source_target_pairs={{0,1},{1,0},{2,3},{3,2},{4,5},{5,4},{6,7},{7,6},{8,9},{9,8},{10,11... | collective-permute-start | bytes 22020104 | tf_op jit(solution)/shard_map/ppermute | solution.py:52
  2.5 7.5 %collective-permute-start = (bf16[8,7296]{1,0:T(8,128)(2,1)}, bf16[8,7296]{1,0:T(8,128)(2,1)S(1)}, u32[]{:S(2)}, u32[]{:S(2)}) collective-permute-start(bf16[8,7296]{1,0:T(8,128)(2,1)} %normalize.1), channel_id=1, source_target_pairs={{0,4},{1,17},{2,6},{3,19},{4,0},{5,21},{6,2},{7,23},{8,12},{9,25},... | collective-permute-start | bytes 350216 | tf_op jit(solution)/shard_map/ppermute | solution.py:48
  5.8 6.2 %collective-permute-start.1 = (bf16[8,7296]{1,0:T(8,128)(2,1)}, bf16[8,7296]{1,0:T(8,128)(2,1)S(1)}, u32[]{:S(2)}, u32[]{:S(2)}) collective-permute-start(bf16[8,7296]{1,0:T(8,128)(2,1)} %normalize.1), channel_id=1, source_target_pairs={{0,2},{1,9},{2,4},{3,11},{4,6},{5,13},{6,0},{7,15},{8,10},{9,17},{... | collective-permute-start | bytes 350216 | tf_op jit(solution)/shard_map/ppermute | solution.py:48
  6.5 5.6 %collective-permute-start.2 = (bf16[8,7296]{1,0:T(8,128)(2,1)}, bf16[8,7296]{1,0:T(8,128)(2,1)S(1)}, u32[]{:S(2)}, u32[]{:S(2)}) collective-permute-start(bf16[8,7296]{1,0:T(8,128)(2,1)} %normalize.1), channel_id=1, source_target_pairs={{0,6},{1,25},{2,0},{3,27},{4,2},{5,29},{6,4},{7,31},{8,14},{9,1},{... | collective-permute-start | bytes 350216 | tf_op jit(solution)/shard_map/ppermute | solution.py:48
  9.1 26.7 %collective-permute-start.8 = (bf16[7168,512]{1,0:T(8,128)(2,1)}, bf16[7168,512]{1,0:T(8,128)(2,1)}, u32[]{:S(2)}, u32[]{:S(2)}) collective-permute-start(bf16[7168,512]{1,0:T(8,128)(2,1)} %refs_1_), channel_id=1, source_target_pairs={{0,1},{1,0},{2,3},{3,2},{4,5},{5,4},{6,7},{7,6},{8,9},{9,8},{10,11... | collective-permute-start | bytes 22020104 | tf_op jit(solution)/shard_map/ppermute | solution.py:52
  12.1 10.3 %collective-permute-start.3 = (bf16[32,7296]{1,0:T(8,128)(2,1)S(1)}, bf16[32,7296]{1,0:T(8,128)(2,1)S(1)}, u32[]{:S(2)}, u32[]{:S(2)}) collective-permute-start(bf16[32,7296]{1,0:T(8,128)(2,1)S(1)} %constant_dynamic-update-slice_fusion.refs_1_), channel_id=1, source_target_pairs={{0,16},{1,33},{2,18},{3,35},{4,20},{5,37},{6,22},{7,39},{8,24},{9,... | collective-permute-start | bytes 1400840 | tf_op jit(solution)/shard_map/ppermute | solution.py:48
  12.7 13.7 %collective-permute-start.4 = (bf16[32,7296]{1,0:T(8,128)(2,1)S(1)}, bf16[32,7296]{1,0:T(8,128)(2,1)S(1)}, u32[]{:S(2)}, u32[]{:S(2)}) collective-permute-start(bf16[32,7296]{1,0:T(8,128)(2,1)S(1)} %constant_dynamic-update-slice_fusion.refs_1_), channel_id=1, source_target_pairs={{0,8},{1,65},{2,10},{3,67},{4,12},{5,69},{6,14},{7,71},{8,16},{9,7... | collective-permute-start | bytes 1400840 | tf_op jit(solution)/shard_map/ppermute | solution.py:48
  14.8 11.6 %collective-permute-start.5 = (bf16[32,7296]{1,0:T(8,128)(2,1)S(1)}, bf16[32,7296]{1,0:T(8,128)(2,1)S(1)}, u32[]{:S(2)}, u32[]{:S(2)}) collective-permute-start(bf16[32,7296]{1,0:T(8,128)(2,1)S(1)} %constant_dynamic-update-slice_fusion.refs_1_), channel_id=1, source_target_pairs={{0,24},{1,97},{2,26},{3,99},{4,28},{5,101},{6,30},{7,103},{8,0},{9... | collective-permute-start | bytes 1400840 | tf_op jit(solution)/shard_map/ppermute | solution.py:48
  28.4 18.8 %collective-permute-start.9 = (bf16[512,7168]{1,0:T(8,128)(2,1)}, bf16[512,7168]{1,0:T(8,128)(2,1)}, u32[]{:S(2)}, u32[]{:S(2)}) collective-permute-start(bf16[512,7168]{1,0:T(8,128)(2,1)} %refs_2_.2), channel_id=1, source_target_pairs={{0,1},{1,0},{2,3},{3,2},{4,5},{5,4},{6,7},{7,6},{8,9},{9,8},{10,11... | collective-permute-start | bytes 22020104 | tf_op jit(solution)/shard_map/ppermute | solution.py:52
  28.5 18.7 %collective-permute-start.7 = (bf16[64,7168]{1,0:T(8,128)(2,1)S(1)}, bf16[64,7168]{1,0:T(8,128)(2,1)S(1)}, u32[]{:S(2)}, u32[]{:S(2)}) collective-permute-start(bf16[64,7168]{1,0:T(8,128)(2,1)S(1)} %get-tuple-element.71), channel_id=1, source_target_pairs={{0,32},{1,5},{2,34},{3,7},{4,36},{5,1},{6,38},{7,3},{8,40},{9,13},... | collective-permute-start | bytes 2752520 | tf_op jit(solution)/shard_map/ppermute | solution.py:48
  32.5 21.4 %collective-permute-start.11 = (bf16[64,7168]{1,0:T(8,128)(2,1)S(1)}, bf16[64,7168]{1,0:T(8,128)(2,1)S(1)}, u32[]{:S(2)}, u32[]{:S(2)}) collective-permute-start(bf16[64,7168]{1,0:T(8,128)(2,1)S(1)} %get-tuple-element.92), channel_id=1, source_target_pairs={{0,64},{1,3},{2,66},{3,5},{4,68},{5,7},{6,70},{7,1},{8,72},{9,11},... | collective-permute-start | bytes 2752520 | tf_op jit(solution)/shard_map/ppermute | solution.py:48
  33.5 21.2 %collective-permute-start.12 = (bf16[64,7168]{1,0:T(8,128)(2,1)S(1)}, bf16[64,7168]{1,0:T(8,128)(2,1)S(1)}, u32[]{:S(2)}, u32[]{:S(2)}) collective-permute-start(bf16[64,7168]{1,0:T(8,128)(2,1)S(1)} %get-tuple-element.93), channel_id=1, source_target_pairs={{0,96},{1,7},{2,98},{3,1},{4,100},{5,3},{6,102},{7,5},{8,104},{9,1... | collective-permute-start | bytes 2752520 | tf_op jit(solution)/shard_map/ppermute | solution.py:48
  53.3 15.2 %collective-permute-start.10 = (bf16[64,7168]{1,0:T(8,128)(2,1)S(1)}, bf16[64,7168]{1,0:T(8,128)(2,1)S(1)}, u32[]{:S(2)}, u32[]{:S(2)}) collective-permute-start(bf16[64,7168]{1,0:T(8,128)(2,1)S(1)} %get-tuple-element.91), channel_id=1, source_target_pairs={{0,32},{1,5},{2,34},{3,7},{4,36},{5,1},{6,38},{7,3},{8,40},{9,13},... | collective-permute-start | bytes 2752520 | tf_op jit(solution)/shard_map/ppermute | solution.py:48
  60.8 22.3 %copy-start.1 = (bf16[1,1536,576]{1,2,0:T(8,128)(2,1)S(1)}, bf16[1,1536,576]{1,2,0:T(8,128)(2,1)}, u32[]{:S(2)}) copy-start(bf16[1,1536,576]{1,2,0:T(8,128)(2,1)} %param.18) | copy-start | bytes 5308420
  60.8 15.3 %collective-permute-start.13 = (bf16[64,7168]{1,0:T(8,128)(2,1)S(1)}, bf16[64,7168]{1,0:T(8,128)(2,1)S(1)}, u32[]{:S(2)}, u32[]{:S(2)}) collective-permute-start(bf16[64,7168]{1,0:T(8,128)(2,1)S(1)} %get-tuple-element.103), channel_id=1, source_target_pairs={{0,96},{1,7},{2,98},{3,1},{4,100},{5,3},{6,102},{7,5},{8,104},{9,1... | collective-permute-start | bytes 2752520 | tf_op jit(solution)/shard_map/ppermute | solution.py:48
  63.5 14.8 %collective-permute-start.14 = (bf16[64,7168]{1,0:T(8,128)(2,1)S(1)}, bf16[64,7168]{1,0:T(8,128)(2,1)S(1)}, u32[]{:S(2)}, u32[]{:S(2)}) collective-permute-start(bf16[64,7168]{1,0:T(8,128)(2,1)S(1)} %get-tuple-element.104), channel_id=1, source_target_pairs={{0,64},{1,3},{2,66},{3,5},{4,68},{5,7},{6,70},{7,1},{8,72},{9,11},... | collective-permute-start | bytes 2752520 | tf_op jit(solution)/shard_map/ppermute | solution.py:48
  79.4 10.2 %collective-permute-start.15 = (bf16[32,7168]{1,0:T(8,128)(2,1)S(1)}, bf16[32,7168]{1,0:T(8,128)(2,1)S(1)}, u32[]{:S(2)}, u32[]{:S(2)}) collective-permute-start(bf16[32,7168]{1,0:T(8,128)(2,1)S(1)} %get-tuple-element.109), channel_id=1, source_target_pairs={{0,16},{1,33},{2,18},{3,35},{4,20},{5,37},{6,22},{7,39},{8,24},{9,... | collective-permute-start | bytes 1376264 | tf_op jit(solution)/shard_map/ppermute | solution.py:48
  81.0 13.5 %collective-permute-start.16 = (bf16[32,7168]{1,0:T(8,128)(2,1)S(1)}, bf16[32,7168]{1,0:T(8,128)(2,1)S(1)}, u32[]{:S(2)}, u32[]{:S(2)}) collective-permute-start(bf16[32,7168]{1,0:T(8,128)(2,1)S(1)} %get-tuple-element.110), channel_id=1, source_target_pairs={{0,24},{1,97},{2,26},{3,99},{4,28},{5,101},{6,30},{7,103},{8,0},{9... | collective-permute-start | bytes 1376264 | tf_op jit(solution)/shard_map/ppermute | solution.py:48
  83.0 11.4 %collective-permute-start.17 = (bf16[32,7168]{1,0:T(8,128)(2,1)S(1)}, bf16[32,7168]{1,0:T(8,128)(2,1)S(1)}, u32[]{:S(2)}, u32[]{:S(2)}) collective-permute-start(bf16[32,7168]{1,0:T(8,128)(2,1)S(1)} %get-tuple-element.111), channel_id=1, source_target_pairs={{0,8},{1,65},{2,10},{3,67},{4,12},{5,69},{6,14},{7,71},{8,16},{9,7... | collective-permute-start | bytes 1376264 | tf_op jit(solution)/shard_map/ppermute | solution.py:48
  94.7 6.4 %collective-permute-start.18 = (bf16[8,7168]{1,0:T(8,128)(2,1)S(1)}, bf16[8,7168]{1,0:T(8,128)(2,1)S(1)}, u32[]{:S(2)}, u32[]{:S(2)}) collective-permute-start(bf16[8,7168]{1,0:T(8,128)(2,1)S(1)} %get-tuple-element.113), channel_id=1, source_target_pairs={{0,4},{1,17},{2,6},{3,19},{4,0},{5,21},{6,2},{7,23},{8,12},{9,25},... | collective-permute-start | bytes 344072 | tf_op jit(solution)/shard_map/ppermute | solution.py:48
  96.3 6.6 %collective-permute-start.19 = (bf16[8,7168]{1,0:T(8,128)(2,1)S(1)}, bf16[8,7168]{1,0:T(8,128)(2,1)S(1)}, u32[]{:S(2)}, u32[]{:S(2)}) collective-permute-start(bf16[8,7168]{1,0:T(8,128)(2,1)S(1)} %get-tuple-element.114), channel_id=1, source_target_pairs={{0,6},{1,25},{2,0},{3,27},{4,2},{5,29},{6,4},{7,31},{8,14},{9,1},{... | collective-permute-start | bytes 344072 | tf_op jit(solution)/shard_map/ppermute | solution.py:48
  98.1 6.0 %collective-permute-start.20 = (bf16[8,7168]{1,0:T(8,128)(2,1)S(1)}, bf16[8,7168]{1,0:T(8,128)(2,1)S(1)}, u32[]{:S(2)}, u32[]{:S(2)}) collective-permute-start(bf16[8,7168]{1,0:T(8,128)(2,1)S(1)} %get-tuple-element.115), channel_id=1, source_target_pairs={{0,2},{1,9},{2,4},{3,11},{4,6},{5,13},{6,0},{7,15},{8,10},{9,17},{... | collective-permute-start | bytes 344072 | tf_op jit(solution)/shard_map/ppermute | solution.py:48

commit v6 on v5

--- a/solution.py
+++ b/solution.py
@@ -16,7 +16,7 @@
 STEPS = (0, 2, 1, -1)
 EARLY = 2
 META = 128
-CHUNK = 512
+CHUNK = 1024
 LIMIT = 5
 
 norm_eps = 1e-06

time: 106 us -> 106 us (level)
  no operation moved by 1% of the time
where the time goes in v6:
time: 106 us; the launch traced here: 105 us
  waiting for transfers between devices  40.9 us (39%)
  Pallas kernels  31.6 us (30%)
  starting transfers between devices  27.6 us (26%)
  matrix products  1.91 us (2%)
  between operations  1.45 us (1%)
    ppermute x18, waiting for transfers between devices, shift(): return lax.ppermute(rows, AXES, pairs)  40.9 us
    ppermute x18, starting transfers between devices, shift(): return lax.ppermute(rows, AXES, pairs)  27.4 us
    pallas_call x2, Pallas kernels, run_experts(): pl.pallas_call(lambda *refs: kernel(count, *refs), in_specs=in_specs, out...  12.1 us
    pallas_call x1, Pallas kernels, load(): pl.pallas_call(lambda *refs: load_kernel(count, *refs), in_specs=[pl.Bloc...  11.5 us
    pallas_call x2, Pallas kernels, spread(): pl.pallas_call(lambda *refs: spread_kernel(first_slot, len(pieces), *refs...  2.21 us
  transfers between devices with their start and end apart: 21, of which 12 were waited for; matrix products, arithmetic and copies ran while one was open for 3% of the time, Pallas kernels for 26%

profile of v6, /device:TPU:4, one launch (start us, length us, event | category | flops | bytes accessed | tf_op | source)
XLA Modules:
  0.0 104.8 jit_solution(10685474372380588026)
XLA Ops:
  0.6 0.0 copy-start
  0.6 1.8 %normalize.1 = bf16[8,7296]{1,0:T(8,128)(2,1)} custom-call(bf16[8,7168]{1,0:T(8,128)(2,1)} %refs_0_.1, f32[1,7168]{1,0:T(1,128)} %bitcast.26, s32[8,8]{1,0:T(8,128)} %refs_2_.1, f32[8,8]{1,0:T(8,128)} %refs_3_.1), custom_call_target="tpu_custom_call" | custom-call | tf_op jit(solution)/shard_map/normalize/pallas_call | solution.py:88
  2.4 0.1 collective-permute-start.6
  2.5 3.3 %collective-permute-start = (bf16[8,7296]{1,0:T(8,128)(2,1)}, bf16[8,7296]{1,0:T(8,128)(2,1)S(1)}, u32[]{:S(2)}, u32[]{:S(2)}) collective-permute-start(bf16[8,7296]{1,0:T(8,128)(2,1)} %normalize.1), channel_id=1, source_target_pairs={{0,4},{1,17},{2,6},{3,19},{4,0},{5,21},{6,2},{7,23},{8,12},{9,25},... | collective-permute-start | bytes 350216 | tf_op jit(solution)/shard_map/ppermute | solution.py:48
  5.8 0.7 collective-permute-start.1
  6.5 2.6 %collective-permute-start.2 = (bf16[8,7296]{1,0:T(8,128)(2,1)}, bf16[8,7296]{1,0:T(8,128)(2,1)S(1)}, u32[]{:S(2)}, u32[]{:S(2)}) collective-permute-start(bf16[8,7296]{1,0:T(8,128)(2,1)} %normalize.1), channel_id=1, source_target_pairs={{0,6},{1,25},{2,0},{3,27},{4,2},{5,29},{6,4},{7,31},{8,14},{9,1},{... | collective-permute-start | bytes 350216 | tf_op jit(solution)/shard_map/ppermute | solution.py:48
  9.1 0.9 constant_dynamic-update-slice_fusion.3
  10.0 2.0 %collective-permute-done.1 = bf16[8,7296]{1,0:T(8,128)(2,1)S(1)} collective-permute-done((bf16[8,7296]{1,0:T(8,128)(2,1)}, bf16[8,7296]{1,0:T(8,128)(2,1)S(1)}, u32[]{:S(2)}, u32[]{:S(2)}) %collective-permute-start.1) | collective-permute-done | bytes 116768 | tf_op jit(solution)/shard_map/ppermute | solution.py:48
  12.1 0.6 collective-permute-start.3
  12.7 2.1 %collective-permute-start.4 = (bf16[32,7296]{1,0:T(8,128)(2,1)S(1)}, bf16[32,7296]{1,0:T(8,128)(2,1)S(1)}, u32[]{:S(2)}, u32[]{:S(2)}) collective-permute-start(bf16[32,7296]{1,0:T(8,128)(2,1)S(1)} %constant_dynamic-update-slice_fusion.refs_1_), channel_id=1, source_target_pairs={{0,8},{1,65},{2,10},{3,67},{4,12},{5,69},{6,14},{7,71},{8,16},{9,7... | collective-permute-start | bytes 1400840 | tf_op jit(solution)/shard_map/ppermute | solution.py:48
  14.8 0.1 collective-permute-start.5
  14.8 0.1 pad_add_fusion.refs_0_
  14.9 7.4 %collective-permute-done.3.refs_2_ = bf16[32,7296]{1,0:T(8,128)(2,1)S(1)} collective-permute-done((bf16[32,7296]{1,0:T(8,128)(2,1)S(1)}, bf16[32,7296]{1,0:T(8,128)(2,1)S(1)}, u32[]{:S(2)}, u32[]{:S(2)}) %collective-permute-start.3) | collective-permute-done | bytes 466976 | tf_op jit(solution)/shard_map/ppermute | solution.py:48
  22.4 4.0 %collective-permute-done.4.refs_3_ = bf16[32,7296]{1,0:T(8,128)(2,1)S(1)} collective-permute-done((bf16[32,7296]{1,0:T(8,128)(2,1)S(1)}, bf16[32,7296]{1,0:T(8,128)(2,1)S(1)}, u32[]{:S(2)}, u32[]{:S(2)}) %collective-permute-start.4) | collective-permute-done | bytes 466976 | tf_op jit(solution)/shard_map/ppermute | solution.py:48
  26.4 2.0 %select_slots.1 = (bf16[64,7168]{1,0:T(8,128)(2,1)S(1)}, bf16[64,7168]{1,0:T(8,128)(2,1)S(1)}, bf16[64,7168]{1,0:T(8,128)(2,1)S(1)}, bf16[64,7168]{1,0:T(8,128)(2,1)S(1)}) custom-call(s32[4]{0:T(128)S(1)} %pad_add_fusion.refs_0_, bf16[32,7296]{1,0:T(8,128)(2,1)S(1)} %constant_dynamic-update-slice_fusion.refs_1_, ...), custom_call_target="tpu_custom_call" | custom-call | flops 469762048 | bytes 5505024 | tf_op jit(solution)/shard_map/select_slots/pallas_call | solution.py:154
  28.4 0.1 collective-permute-start.9
  28.5 4.0 %collective-permute-start.7 = (bf16[64,7168]{1,0:T(8,128)(2,1)S(1)}, bf16[64,7168]{1,0:T(8,128)(2,1)S(1)}, u32[]{:S(2)}, u32[]{:S(2)}) collective-permute-start(bf16[64,7168]{1,0:T(8,128)(2,1)S(1)} %get-tuple-element.71), channel_id=1, source_target_pairs={{0,32},{1,5},{2,34},{3,7},{4,36},{5,1},{6,38},{7,3},{8,40},{9,13},... | collective-permute-start | bytes 2752520 | tf_op jit(solution)/shard_map/ppermute | solution.py:48
  32.5 1.0 collective-permute-start.11
  33.5 2.2 %collective-permute-start.12 = (bf16[64,7168]{1,0:T(8,128)(2,1)S(1)}, bf16[64,7168]{1,0:T(8,128)(2,1)S(1)}, u32[]{:S(2)}, u32[]{:S(2)}) collective-permute-start(bf16[64,7168]{1,0:T(8,128)(2,1)S(1)} %get-tuple-element.93), channel_id=1, source_target_pairs={{0,96},{1,7},{2,98},{3,1},{4,100},{5,3},{6,102},{7,5},{8,104},{9,1... | collective-permute-start | bytes 2752520 | tf_op jit(solution)/shard_map/ppermute | solution.py:48
  35.7 11.5 %load_weights.1 = (bf16[7168,512]{1,0:T(8,128)(2,1)S(1)}, bf16[7168,512]{1,0:T(8,128)(2,1)S(1)}, bf16[512,7168]{1,0:T(8,128)(2,1)S(1)}, bf16[7168,512]{1,0:T(8,1...) custom-call(bf16[7168,512]{1,0:T(8,128)(2,1)} %refs_0_.2, bf16[7168,512]{1,0:T(8,128)(2,1)} %refs_1_, ...), custom_call_target="tpu_custom_call" | custom-call | flops 11010048000 | tf_op jit(solution)/shard_map/load_weights/pallas_call | solution.py:205
  47.2 6.1 %experts.2 = (bf16[64,7168]{1,0:T(8,128)(2,1)S(1)}, bf16[64,7168]{1,0:T(8,128)(2,1)S(1)}, bf16[512,7168]{1,0:T(8,128)(2,1)S(1)}) custom-call(bf16[64,7168]{1,0:T(8,128)(2,1)S(1)} %get-tuple-element.82.refs_0_, bf16[64,7168]{1,0:T(8,128)(2,1)S(1)} %collective-permute-done.7.refs_1_, ...), custom_call_target="tpu_custom_call", output_to_operand_aliasing={{2}: (7, {})} | custom-call | flops 5637144576 | bytes 44040192 | tf_op jit(solution)/shard_map/experts/pallas_call | solution.py:271
  53.3 0.5 collective-permute-start.10
  53.8 0.9 collective-permute-done.12.refs_1_
  54.7 6.0 %experts.3 = (bf16[64,7168]{1,0:T(8,128)(2,1)S(1)}, bf16[64,7168]{1,0:T(8,128)(2,1)S(1)}) custom-call(bf16[64,7168]{1,0:T(8,128)(2,1)S(1)} %collective-permute-done.11.refs_0_, bf16[64,7168]{1,0:T(8,128)(2,1)S(1)} %collective-permute-done.12.refs_1_, bf16[7168,512]{1,0:T(8,128)(2,1)S(1)} %get-tuple-element.97.refs_2_, ...), custom_call_target="tpu_custom_call" | custom-call | flops 5637144576 | bytes 44040192 | tf_op jit(solution)/shard_map/experts/pallas_call | solution.py:271
  60.8 0.0 copy-start.1
  60.8 2.7 %collective-permute-start.13 = (bf16[64,7168]{1,0:T(8,128)(2,1)S(1)}, bf16[64,7168]{1,0:T(8,128)(2,1)S(1)}, u32[]{:S(2)}, u32[]{:S(2)}) collective-permute-start(bf16[64,7168]{1,0:T(8,128)(2,1)S(1)} %get-tuple-element.103), channel_id=1, source_target_pairs={{0,96},{1,7},{2,98},{3,1},{4,100},{5,3},{6,102},{7,5},{8,104},{9,1... | collective-permute-start | bytes 2752520 | tf_op jit(solution)/shard_map/ppermute | solution.py:48
  64.1 1.1 %slot_weights.1.refs_0_ = bf16[256,256]{1,0:T(8,128)(2,1)S(1)} custom-call(s32[4]{0:T(128)S(1)} %pad_add_fusion.refs_0_, bf16[32,7296]{1,0:T(8,128)(2,1)S(1)} %constant_dynamic-update-slice_fusion.refs_1_, bf16[32,7296]{1,0:T(8,128)(2,1)S(1)} %collective-permute-done.3.refs_2_, bf16[32,7296]{1,0:T(8,128)(2,1)S(1)} %collective-permute-done.4.refs_3_, ...), custom_call_target="tpu_custom_call" | custom-call | tf_op jit(solution)/shard_map/slot_weights/pallas_call | solution.py:180
  65.2 3.3 %collective-permute-done.10.refs_2_ = bf16[64,7168]{1,0:T(8,128)(2,1)S(1)} collective-permute-done((bf16[64,7168]{1,0:T(8,128)(2,1)S(1)}, bf16[64,7168]{1,0:T(8,128)(2,1)S(1)}, u32[]{:S(2)}, u32[]{:S(2)}) %collective-permute-start.10) | collective-permute-done | bytes 917536 | tf_op jit(solution)/shard_map/ppermute | solution.py:48
  68.5 1.1 %spread_slots.2.refs_3_ = f32[128,7168]{1,0:T(8,128)S(1)} custom-call(bf16[256,256]{1,0:T(8,128)(2,1)S(1)} %slot_weights.1.refs_0_, bf16[64,7168]{1,0:T(8,128)(2,1)S(1)} %get-tuple-element.90.refs_1_, bf16[64,7168]{1,0:T(8,128)(2,1)S(1)} %collective-permute-done.10.refs_2_), custom_call_target="tpu_custom_call" | custom-call | flops 469762048 | bytes 5505024 | tf_op jit(solution)/shard_map/spread_slots/pallas_call | solution.py:312
  69.6 6.4 %collective-permute-done.13.refs_1_ = bf16[64,7168]{1,0:T(8,128)(2,1)S(1)} collective-permute-done((bf16[64,7168]{1,0:T(8,128)(2,1)S(1)}, bf16[64,7168]{1,0:T(8,128)(2,1)S(1)}, u32[]{:S(2)}, u32[]{:S(2)}) %collective-permute-start.13) | collective-permute-done | bytes 917536 | tf_op jit(solution)/shard_map/ppermute | solution.py:48
  76.0 2.3 %collective-permute-done.14.refs_2_ = bf16[64,7168]{1,0:T(8,128)(2,1)S(1)} collective-permute-done((bf16[64,7168]{1,0:T(8,128)(2,1)S(1)}, bf16[64,7168]{1,0:T(8,128)(2,1)S(1)}, u32[]{:S(2)}, u32[]{:S(2)}) %collective-permute-start.14) | collective-permute-done | bytes 917536 | tf_op jit(solution)/shard_map/ppermute | solution.py:48
  78.3 1.1 %spread_slots.3 = (bf16[32,7168]{1,0:T(8,128)(2,1)S(1)}, bf16[32,7168]{1,0:T(8,128)(2,1)S(1)}, bf16[32,7168]{1,0:T(8,128)(2,1)S(1)}, bf16[32,7168]{1,0:T(8,128)(2,1)S(1)}) custom-call(bf16[256,256]{1,0:T(8,128)(2,1)S(1)} %slot_weights.1.refs_0_, bf16[64,7168]{1,0:T(8,128)(2,1)S(1)} %collective-permute-done.13.refs_1_, ...), custom_call_target="tpu_custom_call" | custom-call | flops 469762048 | bytes 5505024 | tf_op jit(solution)/shard_map/spread_slots/pallas_call | solution.py:312
  79.4 1.6 %collective-permute-start.15 = (bf16[32,7168]{1,0:T(8,128)(2,1)S(1)}, bf16[32,7168]{1,0:T(8,128)(2,1)S(1)}, u32[]{:S(2)}, u32[]{:S(2)}) collective-permute-start(bf16[32,7168]{1,0:T(8,128)(2,1)S(1)} %get-tuple-element.109), channel_id=1, source_target_pairs={{0,16},{1,33},{2,18},{3,35},{4,20},{5,37},{6,22},{7,39},{8,24},{9,... | collective-permute-start | bytes 1376264 | tf_op jit(solution)/shard_map/ppermute | solution.py:48
  81.0 2.0 %collective-permute-start.16 = (bf16[32,7168]{1,0:T(8,128)(2,1)S(1)}, bf16[32,7168]{1,0:T(8,128)(2,1)S(1)}, u32[]{:S(2)}, u32[]{:S(2)}) collective-permute-start(bf16[32,7168]{1,0:T(8,128)(2,1)S(1)} %get-tuple-element.110), channel_id=1, source_target_pairs={{0,24},{1,97},{2,26},{3,99},{4,28},{5,101},{6,30},{7,103},{8,0},{9... | collective-permute-start | bytes 1376264 | tf_op jit(solution)/shard_map/ppermute | solution.py:48
  83.0 0.0 collective-permute-start.17
  83.1 0.6 fusion.15
  83.7 0.3 fusion.11
  83.9 5.7 %collective-permute-done.15.refs_1_ = bf16[32,7168]{1,0:T(8,128)(2,1)S(1)} collective-permute-done((bf16[32,7168]{1,0:T(8,128)(2,1)S(1)}, bf16[32,7168]{1,0:T(8,128)(2,1)S(1)}, u32[]{:S(2)}, u32[]{:S(2)}) %collective-permute-start.15) | collective-permute-done | bytes 458784 | tf_op jit(solution)/shard_map/ppermute | solution.py:48
  89.6 4.9 %collective-permute-done.16.refs_2_ = bf16[32,7168]{1,0:T(8,128)(2,1)S(1)} collective-permute-done((bf16[32,7168]{1,0:T(8,128)(2,1)S(1)}, bf16[32,7168]{1,0:T(8,128)(2,1)S(1)}, u32[]{:S(2)}, u32[]{:S(2)}) %collective-permute-start.16) | collective-permute-done | bytes 458784 | tf_op jit(solution)/shard_map/ppermute | solution.py:48
  94.5 0.2 add_pieces.2
  94.7 1.6 %collective-permute-start.18 = (bf16[8,7168]{1,0:T(8,128)(2,1)S(1)}, bf16[8,7168]{1,0:T(8,128)(2,1)S(1)}, u32[]{:S(2)}, u32[]{:S(2)}) collective-permute-start(bf16[8,7168]{1,0:T(8,128)(2,1)S(1)} %get-tuple-element.113), channel_id=1, source_target_pairs={{0,4},{1,17},{2,6},{3,19},{4,0},{5,21},{6,2},{7,23},{8,12},{9,25},... | collective-permute-start | bytes 344072 | tf_op jit(solution)/shard_map/ppermute | solution.py:48
  96.3 1.8 %collective-permute-start.19 = (bf16[8,7168]{1,0:T(8,128)(2,1)S(1)}, bf16[8,7168]{1,0:T(8,128)(2,1)S(1)}, u32[]{:S(2)}, u32[]{:S(2)}) collective-permute-start(bf16[8,7168]{1,0:T(8,128)(2,1)S(1)} %get-tuple-element.114), channel_id=1, source_target_pairs={{0,6},{1,25},{2,0},{3,27},{4,2},{5,29},{6,4},{7,31},{8,14},{9,1},{... | collective-permute-start | bytes 344072 | tf_op jit(solution)/shard_map/ppermute | solution.py:48
  98.1 0.8 collective-permute-start.20
  98.9 1.3 %fusion.8 = bf16[1,128,512]{2,1,0:T(8,128)(2,1)} fusion(bf16[1,1536,576]{1,2,0:T(8,128)(2,1)S(1)} %copy-done.1, f32[128,1536]{1,0:T(8,128)S(1)} %get-tuple-element.117, f32[128]{0:T(128)S(1)} %fusion.11, f32[128]{0:T(128)S(1)} %get-tuple-element.116), kind=kOutput, calls=%fused_computation.7 | convolution fusion | flops 201981952 | bytes 2491392 | tf_op jit(solution)/shard_map/rhc,rcl->rhl/dot_general | solution.py:364
  100.2 0.9 collective-permute-done.18.refs_1_
  101.1 1.8 %collective-permute-done.19.refs_2_ = bf16[8,7168]{1,0:T(8,128)(2,1)S(1)} collective-permute-done((bf16[8,7168]{1,0:T(8,128)(2,1)S(1)}, bf16[8,7168]{1,0:T(8,128)(2,1)S(1)}, u32[]{:S(2)}, u32[]{:S(2)}) %collective-permute-start.19) | collective-permute-done | bytes 114720 | tf_op jit(solution)/shard_map/ppermute | solution.py:48
  102.9 1.2 %collective-permute-done.20.refs_3_ = bf16[8,7168]{1,0:T(8,128)(2,1)S(1)} collective-permute-done((bf16[8,7168]{1,0:T(8,128)(2,1)S(1)}, bf16[8,7168]{1,0:T(8,128)(2,1)S(1)}, u32[]{:S(2)}, u32[]{:S(2)}) %collective-permute-start.20) | collective-permute-done | bytes 114720 | tf_op jit(solution)/shard_map/ppermute | solution.py:48
  104.1 0.7 add_pieces.3
  (17 shorter events, 0.1 us)
Async XLA Ops:
  0.6 82.4 %copy-start = (bf16[1,128,576]{1,2,0:T(8,128)(2,1)S(1)}, bf16[1,128,576]{1,2,0:T(8,128)(2,1)}, u32[]{:S(2)}) copy-start(bf16[1,128,576]{1,2,0:T(8,128)(2,1)} %param.17) | copy-start | bytes 442372
  2.4 23.9 %collective-permute-start.6 = (bf16[7168,512]{1,0:T(8,128)(2,1)}, bf16[7168,512]{1,0:T(8,128)(2,1)}, u32[]{:S(2)}, u32[]{:S(2)}) collective-permute-start(bf16[7168,512]{1,0:T(8,128)(2,1)} %refs_0_.2), channel_id=1, source_target_pairs={{0,1},{1,0},{2,3},{3,2},{4,5},{5,4},{6,7},{7,6},{8,9},{9,8},{10,11... | collective-permute-start | bytes 22020104 | tf_op jit(solution)/shard_map/ppermute | solution.py:52
  2.5 7.5 %collective-permute-start = (bf16[8,7296]{1,0:T(8,128)(2,1)}, bf16[8,7296]{1,0:T(8,128)(2,1)S(1)}, u32[]{:S(2)}, u32[]{:S(2)}) collective-permute-start(bf16[8,7296]{1,0:T(8,128)(2,1)} %normalize.1), channel_id=1, source_target_pairs={{0,4},{1,17},{2,6},{3,19},{4,0},{5,21},{6,2},{7,23},{8,12},{9,25},... | collective-permute-start | bytes 350216 | tf_op jit(solution)/shard_map/ppermute | solution.py:48
  5.8 6.2 %collective-permute-start.1 = (bf16[8,7296]{1,0:T(8,128)(2,1)}, bf16[8,7296]{1,0:T(8,128)(2,1)S(1)}, u32[]{:S(2)}, u32[]{:S(2)}) collective-permute-start(bf16[8,7296]{1,0:T(8,128)(2,1)} %normalize.1), channel_id=1, source_target_pairs={{0,2},{1,9},{2,4},{3,11},{4,6},{5,13},{6,0},{7,15},{8,10},{9,17},{... | collective-permute-start | bytes 350216 | tf_op jit(solution)/shard_map/ppermute | solution.py:48
  6.5 5.6 %collective-permute-start.2 = (bf16[8,7296]{1,0:T(8,128)(2,1)}, bf16[8,7296]{1,0:T(8,128)(2,1)S(1)}, u32[]{:S(2)}, u32[]{:S(2)}) collective-permute-start(bf16[8,7296]{1,0:T(8,128)(2,1)} %normalize.1), channel_id=1, source_target_pairs={{0,6},{1,25},{2,0},{3,27},{4,2},{5,29},{6,4},{7,31},{8,14},{9,1},{... | collective-permute-start | bytes 350216 | tf_op jit(solution)/shard_map/ppermute | solution.py:48
  9.1 26.7 %collective-permute-start.8 = (bf16[7168,512]{1,0:T(8,128)(2,1)}, bf16[7168,512]{1,0:T(8,128)(2,1)}, u32[]{:S(2)}, u32[]{:S(2)}) collective-permute-start(bf16[7168,512]{1,0:T(8,128)(2,1)} %refs_1_), channel_id=1, source_target_pairs={{0,1},{1,0},{2,3},{3,2},{4,5},{5,4},{6,7},{7,6},{8,9},{9,8},{10,11... | collective-permute-start | bytes 22020104 | tf_op jit(solution)/shard_map/ppermute | solution.py:52
  12.1 10.3 %collective-permute-start.3 = (bf16[32,7296]{1,0:T(8,128)(2,1)S(1)}, bf16[32,7296]{1,0:T(8,128)(2,1)S(1)}, u32[]{:S(2)}, u32[]{:S(2)}) collective-permute-start(bf16[32,7296]{1,0:T(8,128)(2,1)S(1)} %constant_dynamic-update-slice_fusion.refs_1_), channel_id=1, source_target_pairs={{0,16},{1,33},{2,18},{3,35},{4,20},{5,37},{6,22},{7,39},{8,24},{9,... | collective-permute-start | bytes 1400840 | tf_op jit(solution)/shard_map/ppermute | solution.py:48
  12.7 13.7 %collective-permute-start.4 = (bf16[32,7296]{1,0:T(8,128)(2,1)S(1)}, bf16[32,7296]{1,0:T(8,128)(2,1)S(1)}, u32[]{:S(2)}, u32[]{:S(2)}) collective-permute-start(bf16[32,7296]{1,0:T(8,128)(2,1)S(1)} %constant_dynamic-update-slice_fusion.refs_1_), channel_id=1, source_target_pairs={{0,8},{1,65},{2,10},{3,67},{4,12},{5,69},{6,14},{7,71},{8,16},{9,7... | collective-permute-start | bytes 1400840 | tf_op jit(solution)/shard_map/ppermute | solution.py:48
  14.8 11.6 %collective-permute-start.5 = (bf16[32,7296]{1,0:T(8,128)(2,1)S(1)}, bf16[32,7296]{1,0:T(8,128)(2,1)S(1)}, u32[]{:S(2)}, u32[]{:S(2)}) collective-permute-start(bf16[32,7296]{1,0:T(8,128)(2,1)S(1)} %constant_dynamic-update-slice_fusion.refs_1_), channel_id=1, source_target_pairs={{0,24},{1,97},{2,26},{3,99},{4,28},{5,101},{6,30},{7,103},{8,0},{9... | collective-permute-start | bytes 1400840 | tf_op jit(solution)/shard_map/ppermute | solution.py:48
  28.4 18.8 %collective-permute-start.9 = (bf16[512,7168]{1,0:T(8,128)(2,1)}, bf16[512,7168]{1,0:T(8,128)(2,1)}, u32[]{:S(2)}, u32[]{:S(2)}) collective-permute-start(bf16[512,7168]{1,0:T(8,128)(2,1)} %refs_2_.2), channel_id=1, source_target_pairs={{0,1},{1,0},{2,3},{3,2},{4,5},{5,4},{6,7},{7,6},{8,9},{9,8},{10,11... | collective-permute-start | bytes 22020104 | tf_op jit(solution)/shard_map/ppermute | solution.py:52
  28.5 18.7 %collective-permute-start.7 = (bf16[64,7168]{1,0:T(8,128)(2,1)S(1)}, bf16[64,7168]{1,0:T(8,128)(2,1)S(1)}, u32[]{:S(2)}, u32[]{:S(2)}) collective-permute-start(bf16[64,7168]{1,0:T(8,128)(2,1)S(1)} %get-tuple-element.71), channel_id=1, source_target_pairs={{0,32},{1,5},{2,34},{3,7},{4,36},{5,1},{6,38},{7,3},{8,40},{9,13},... | collective-permute-start | bytes 2752520 | tf_op jit(solution)/shard_map/ppermute | solution.py:48
  32.5 21.3 %collective-permute-start.11 = (bf16[64,7168]{1,0:T(8,128)(2,1)S(1)}, bf16[64,7168]{1,0:T(8,128)(2,1)S(1)}, u32[]{:S(2)}, u32[]{:S(2)}) collective-permute-start(bf16[64,7168]{1,0:T(8,128)(2,1)S(1)} %get-tuple-element.92), channel_id=1, source_target_pairs={{0,64},{1,3},{2,66},{3,5},{4,68},{5,7},{6,70},{7,1},{8,72},{9,11},... | collective-permute-start | bytes 2752520 | tf_op jit(solution)/shard_map/ppermute | solution.py:48
  33.5 21.2 %collective-permute-start.12 = (bf16[64,7168]{1,0:T(8,128)(2,1)S(1)}, bf16[64,7168]{1,0:T(8,128)(2,1)S(1)}, u32[]{:S(2)}, u32[]{:S(2)}) collective-permute-start(bf16[64,7168]{1,0:T(8,128)(2,1)S(1)} %get-tuple-element.93), channel_id=1, source_target_pairs={{0,96},{1,7},{2,98},{3,1},{4,100},{5,3},{6,102},{7,5},{8,104},{9,1... | collective-permute-start | bytes 2752520 | tf_op jit(solution)/shard_map/ppermute | solution.py:48
  53.3 15.2 %collective-permute-start.10 = (bf16[64,7168]{1,0:T(8,128)(2,1)S(1)}, bf16[64,7168]{1,0:T(8,128)(2,1)S(1)}, u32[]{:S(2)}, u32[]{:S(2)}) collective-permute-start(bf16[64,7168]{1,0:T(8,128)(2,1)S(1)} %get-tuple-element.91), channel_id=1, source_target_pairs={{0,32},{1,5},{2,34},{3,7},{4,36},{5,1},{6,38},{7,3},{8,40},{9,13},... | collective-permute-start | bytes 2752520 | tf_op jit(solution)/shard_map/ppermute | solution.py:48
  60.8 22.3 %copy-start.1 = (bf16[1,1536,576]{1,2,0:T(8,128)(2,1)S(1)}, bf16[1,1536,576]{1,2,0:T(8,128)(2,1)}, u32[]{:S(2)}) copy-start(bf16[1,1536,576]{1,2,0:T(8,128)(2,1)} %param.18) | copy-start | bytes 5308420
  60.8 15.3 %collective-permute-start.13 = (bf16[64,7168]{1,0:T(8,128)(2,1)S(1)}, bf16[64,7168]{1,0:T(8,128)(2,1)S(1)}, u32[]{:S(2)}, u32[]{:S(2)}) collective-permute-start(bf16[64,7168]{1,0:T(8,128)(2,1)S(1)} %get-tuple-element.103), channel_id=1, source_target_pairs={{0,96},{1,7},{2,98},{3,1},{4,100},{5,3},{6,102},{7,5},{8,104},{9,1... | collective-permute-start | bytes 2752520 | tf_op jit(solution)/shard_map/ppermute | solution.py:48
  63.5 14.8 %collective-permute-start.14 = (bf16[64,7168]{1,0:T(8,128)(2,1)S(1)}, bf16[64,7168]{1,0:T(8,128)(2,1)S(1)}, u32[]{:S(2)}, u32[]{:S(2)}) collective-permute-start(bf16[64,7168]{1,0:T(8,128)(2,1)S(1)} %get-tuple-element.104), channel_id=1, source_target_pairs={{0,64},{1,3},{2,66},{3,5},{4,68},{5,7},{6,70},{7,1},{8,72},{9,11},... | collective-permute-start | bytes 2752520 | tf_op jit(solution)/shard_map/ppermute | solution.py:48
  79.4 10.2 %collective-permute-start.15 = (bf16[32,7168]{1,0:T(8,128)(2,1)S(1)}, bf16[32,7168]{1,0:T(8,128)(2,1)S(1)}, u32[]{:S(2)}, u32[]{:S(2)}) collective-permute-start(bf16[32,7168]{1,0:T(8,128)(2,1)S(1)} %get-tuple-element.109), channel_id=1, source_target_pairs={{0,16},{1,33},{2,18},{3,35},{4,20},{5,37},{6,22},{7,39},{8,24},{9,... | collective-permute-start | bytes 1376264 | tf_op jit(solution)/shard_map/ppermute | solution.py:48
  81.0 13.5 %collective-permute-start.16 = (bf16[32,7168]{1,0:T(8,128)(2,1)S(1)}, bf16[32,7168]{1,0:T(8,128)(2,1)S(1)}, u32[]{:S(2)}, u32[]{:S(2)}) collective-permute-start(bf16[32,7168]{1,0:T(8,128)(2,1)S(1)} %get-tuple-element.110), channel_id=1, source_target_pairs={{0,24},{1,97},{2,26},{3,99},{4,28},{5,101},{6,30},{7,103},{8,0},{9... | collective-permute-start | bytes 1376264 | tf_op jit(solution)/shard_map/ppermute | solution.py:48
  83.0 11.4 %collective-permute-start.17 = (bf16[32,7168]{1,0:T(8,128)(2,1)S(1)}, bf16[32,7168]{1,0:T(8,128)(2,1)S(1)}, u32[]{:S(2)}, u32[]{:S(2)}) collective-permute-start(bf16[32,7168]{1,0:T(8,128)(2,1)S(1)} %get-tuple-element.111), channel_id=1, source_target_pairs={{0,8},{1,65},{2,10},{3,67},{4,12},{5,69},{6,14},{7,71},{8,16},{9,7... | collective-permute-start | bytes 1376264 | tf_op jit(solution)/shard_map/ppermute | solution.py:48
  94.7 6.4 %collective-permute-start.18 = (bf16[8,7168]{1,0:T(8,128)(2,1)S(1)}, bf16[8,7168]{1,0:T(8,128)(2,1)S(1)}, u32[]{:S(2)}, u32[]{:S(2)}) collective-permute-start(bf16[8,7168]{1,0:T(8,128)(2,1)S(1)} %get-tuple-element.113), channel_id=1, source_target_pairs={{0,4},{1,17},{2,6},{3,19},{4,0},{5,21},{6,2},{7,23},{8,12},{9,25},... | collective-permute-start | bytes 344072 | tf_op jit(solution)/shard_map/ppermute | solution.py:48
  96.3 6.6 %collective-permute-start.19 = (bf16[8,7168]{1,0:T(8,128)(2,1)S(1)}, bf16[8,7168]{1,0:T(8,128)(2,1)S(1)}, u32[]{:S(2)}, u32[]{:S(2)}) collective-permute-start(bf16[8,7168]{1,0:T(8,128)(2,1)S(1)} %get-tuple-element.114), channel_id=1, source_target_pairs={{0,6},{1,25},{2,0},{3,27},{4,2},{5,29},{6,4},{7,31},{8,14},{9,1},{... | collective-permute-start | bytes 344072 | tf_op jit(solution)/shard_map/ppermute | solution.py:48
  98.1 6.0 %collective-permute-start.20 = (bf16[8,7168]{1,0:T(8,128)(2,1)S(1)}, bf16[8,7168]{1,0:T(8,128)(2,1)S(1)}, u32[]{:S(2)}, u32[]{:S(2)}) collective-permute-start(bf16[8,7168]{1,0:T(8,128)(2,1)S(1)} %get-tuple-element.115), channel_id=1, source_target_pairs={{0,2},{1,9},{2,4},{3,11},{4,6},{5,13},{6,0},{7,15},{8,10},{9,17},{... | collective-permute-start | bytes 344072 | tf_op jit(solution)/shard_map/ppermute | solution.py:48
